TPU v7x, 512 devices: a whole 4x8x8 slice. The times are simulated.
512 devices in a mesh: fsdp: 64 (over y, x, core), tensor: 8 (over z).
Axes of the slice: x: 4, y: 8, z: 8, core: 2. Of those that a mesh axis runs over, the one named last changes fastest.
Arguments:
- gradient: bfloat16 [8192, 28672], P('fsdp', 'tensor')
- momentum: bfloat16 [8192, 28672], P('fsdp', 'tensor')
- q_basis: bfloat16 [256, 28672], P('fsdp', 'tensor'), may hold values from -0.03125 to 0.03125
Outputs:
- momentum_next: bfloat16 [8192, 28672], P('fsdp', 'tensor')
- update: bfloat16 [8192, 28672], P('fsdp', 'tensor')
- q_next: bfloat16 [256, 28672], P('fsdp', 'tensor')
All inputs are finite; a program needn't handle non-finite values.
Results may differ from a plain program's by a relative error of at most 0.038.
Values may be sent and summed in bfloat16 or wider, within the bound.
No kernel may reach another device: no remote copies, remote signals or barrier semaphores. Data moves between devices by JAX's collectives and lax.ppermute only.
A program may use at most 64 MiB of HBM per device.

v0:
```python
import math

import jax
import jax.numpy as jnp
from jax import lax
from jax.sharding import PartitionSpec as P

D = 8192
FF = 28672
RANK = 256


MU_KEEP = 0.9


def gram_of(power_rows):
    return lax.dot_general(
        power_rows,
        power_rows,
        (((0,), (0,)), ((), ())),
        precision=lax.Precision.HIGHEST,
        preferred_element_type=jnp.float32,
    )


def orthonormal(power_rows, gram_total):
    factor = jnp.linalg.cholesky(gram_total)
    basis = lax.linalg.triangular_solve(
        factor, power_rows, left_side=False, lower=True, transpose_a=True
    )
    return basis.astype(jnp.bfloat16)


def body(gradient, momentum, q_basis):
    blended = (momentum.astype(jnp.float32) + gradient.astype(jnp.float32)).astype(jnp.bfloat16)
    rank_dev = q_basis.shape[0]
    partial_power = lax.dot_general(
        blended,
        lax.all_gather(q_basis, "fsdp", axis=0, tiled=True),
        (((1,), (1,)), ((), ())),
        preferred_element_type=jnp.float32,
    )
    power_full = lax.psum(partial_power.astype(jnp.bfloat16), "tensor").astype(jnp.float32)
    gram_total = lax.psum(gram_of(power_full), "fsdp")
    basis_low = orthonormal(power_full, gram_total)
    local_terms = lax.dot_general(
        basis_low, blended, (((0,), (0,)), ((), ())), preferred_element_type=jnp.float32
    )
    project = lax.psum(local_terms, "fsdp").astype(jnp.bfloat16)
    project_wide = project.astype(jnp.float32)
    squares = lax.psum(jnp.sum(project_wide * project_wide, axis=1, keepdims=True), "tensor")
    q_full = (project_wide / jnp.sqrt(squares + 1e-06)).astype(jnp.bfloat16)
    carried = jnp.dot(basis_low, project, preferred_element_type=jnp.float32)
    momentum_next = (blended.astype(jnp.float32) - (1.0 - MU_KEEP) * carried).astype(jnp.bfloat16)
    scale_factor = math.sqrt(D * FF / RANK)
    update = (scale_factor * jnp.dot(basis_low, q_full, preferred_element_type=jnp.float32)).astype(
        jnp.bfloat16
    )
    q_next = lax.dynamic_slice_in_dim(q_full, lax.axis_index("fsdp") * rank_dev, rank_dev, 0)
    return (momentum_next, update, q_next)


def solution(mesh):
    placed = (P("fsdp", "tensor"), P("fsdp", "tensor"), P("fsdp", "tensor"))
    return jax.shard_map(
        body,
        mesh=mesh,
        in_specs=placed,
        out_specs=(P("fsdp", "tensor"), P("fsdp", "tensor"), P("fsdp", "tensor")),
        check_vma=False,
    )
```

profile of v0, /device:TPU:1, one launch (start us, length us, event | category | flops | bytes accessed | tf_op | source)
XLA Modules:
  0.0 742.0 jit_solution(6740431460330392108)
XLA Ops:
  7.2 0.0 all-gather.3.cloned.1.call-start
  7.2 0.7 all-gather.3.cloned.1.call-update
  7.9 0.0 copy-start
  7.9 0.0 copy-start.1
  7.9 0.0 all-reduce.5.cloned.1.call-start
  8.0 91.6 %all-gather.3.cloned.1.call-done = bf16[64,4,3584]{2,1,0:T(4,128)(2,1)} async-done(((bf16[1,4,3584]{2,1,0:T(4,128)(2,1)}), bf16[64,4,3584]{2,1,0:T(4,128)(2,1)}) %all-gather.3.cloned.1.call-update) | async-done | bytes 1835024 | tf_op jit(solution)/shard_map/all_gather | solution.py:39
  99.5 3.9 reshape.43
  103.5 0.0 copy-done
  103.5 0.0 copy-done.1
  103.5 2.9 convolution_convert_fusion
  106.3 0.0 all-reduce.5.cloned.1.call-update
  106.3 0.0 all-reduce.7.cloned.1.call-start
  106.4 70.6 %all-reduce.5.cloned.1.call-done = bf16[128,256]{1,0:T(8,128)(2,1)} async-done(((bf16[128,256]{1,0:T(8,128)(2,1)}), bf16[128,256]{1,0:T(8,128)(2,1)}) %all-reduce.5.cloned.1.call-update) | async-done | bytes 65552 | tf_op jit(solution)/shard_map/psum | solution.py:43
  177.0 1.8 fusion.19
  178.8 0.0 all-reduce.7.cloned.1.call-update
  178.9 191.9 %all-reduce.7.cloned.1.call-done = f32[256,256]{0,1:T(8,128)} async-done(((f32[256,256]{0,1:T(8,128)}), f32[256,256]{0,1:T(8,128)}) %all-reduce.7.cloned.1.call-update) | async-done | bytes 262160 | tf_op jit(solution)/shard_map/psum | solution.py:44
  370.8 1.1 copy.11
  371.9 0.0 copy-start.3
  371.9 1.0 fusion.5
  372.9 11.7 %cholesky.50 = f32[128,128]{1,0:T(8,128)S(1)} custom-call(f32[128,128]{1,0:T(8,128)S(1)} %cholesky.118), custom_call_target="Cholesky" | custom-call | tf_op jit(solution)/shard_map/jit(cholesky)/cholesky | solution.py:27
  384.7 9.8 %custom-call.14 = f32[1,128,128]{1,2,0:T(8,128)S(1)} custom-call(f32[1,128,128]{2,1,0:T(8,128)S(1)} %get-tuple-element.24), custom_call_target="InvertDiagBlocksLowerTriangular" | custom-call | tf_op jit(solution)/shard_map/jit(cholesky)/cholesky | solution.py:27
  394.5 0.2 constant_dynamic-update-slice_fusion
  394.7 0.3 convolution_subtract_fusion.1
  395.0 11.7 %cholesky.105 = f32[128,128]{1,0:T(8,128)S(1)} custom-call(f32[128,128]{1,0:T(8,128)S(1)} %convolution_subtract_fusion.1), custom_call_target="Cholesky" | custom-call | tf_op jit(solution)/shard_map/jit(cholesky)/cholesky | solution.py:27
  406.7 0.6 compare_reduce_fusion
  408.7 0.1 triangular_solve.60
  408.8 4.1 while.1
  408.9 0.6 fusion.30
  409.5 1.4 bitcast_dynamic-update-slice_fusion.2
  410.9 0.6 fusion.30
  411.5 1.4 bitcast_dynamic-update-slice_fusion.2
  412.9 19.7 %custom-call.15 = f32[2,128,128]{1,2,0:T(8,128)S(1)} custom-call(f32[2,128,128]{2,1,0:T(8,128)S(1)} %get-tuple-element.10), custom_call_target="InvertDiagBlocksLowerTriangular" | custom-call | tf_op jit(solution)/shard_map/triangular_solve | solution.py:28
  432.6 0.0 copy-done.3
  432.6 0.2 fusion.18
  432.9 0.3 convolution_subtract_fusion
  433.2 0.3 convolution_convert_fusion.1
  433.5 2.4 fusion.12
  435.9 280.0 %all-reduce.8 = bf16[256,3584]{1,0:T(8,128)(2,1)S(1)} all-reduce(f32[256,3584]{1,0:T(8,128)} %fusion.12), channel_id=1, replica_groups=mesh['fsdp'=64,'tensor'=8] {'fsdp'}, use_global_device_ids=true, to_apply=%region_6.7 | all-reduce | flops 917504 | bytes 5505024 | tf_op jit(solution)/shard_map/psum | solution.py:49
  715.9 0.0 copy-start.2
  715.9 0.4 fusion.3
  716.4 0.7 copy-done.2
  717.1 1.5 fusion.1
  718.6 14.3 %psum.31 = f32[256,1]{0,1:T(1,128)S(1)} all-reduce(f32[256,1]{0,1:T(1,128)S(1)} %bitcast.42), channel_id=1, replica_groups=mesh['fsdp'=64,'tensor'=8] {'tensor'}, use_global_device_ids=true, to_apply=%region_8.9 | all-reduce | flops 256 | bytes 2048 | tf_op jit(solution)/shard_map/psum | solution.py:51
  732.9 0.5 fusion.4
  733.4 1.4 fusion.2
  734.8 0.6 constant_dynamic-slice_fusion.1
  (10 shorter events, 0.2 us)
Async XLA Ops:
  7.2 92.4 %all-gather.3.cloned.1.call-start = ((), (), s32[]{:S(2)}) async-start(), calls=%async_computation.2 | async-start | bytes 1863680 | tf_op jit(solution)/shard_map/all_gather | solution.py:39
  7.9 95.6 %copy-start = (bf16[128,3584]{1,0:T(8,128)(2,1)S(1)}, bf16[128,3584]{1,0:T(8,128)(2,1)}, u32[]{:S(2)}) copy-start(bf16[128,3584]{1,0:T(8,128)(2,1)} %param.3) | copy-start | bytes 2752516
  7.9 95.6 %copy-start.1 = (bf16[128,3584]{1,0:T(8,128)(2,1)S(1)}, bf16[128,3584]{1,0:T(8,128)(2,1)}, u32[]{:S(2)}) copy-start(bf16[128,3584]{1,0:T(8,128)(2,1)} %param.4) | copy-start | bytes 2752516
  7.9 169.1 %all-reduce.5.cloned.1.call-start = ((), (), s32[]{:S(2)}) async-start(), calls=%async_computation | async-start | bytes 131072 | tf_op jit(solution)/shard_map/psum | solution.py:43
  106.3 264.4 %all-reduce.7.cloned.1.call-start = ((), (), s32[]{:S(2)}) async-start(), calls=%async_computation.1 | async-start | bytes 524288 | tf_op jit(solution)/shard_map/psum | solution.py:44
  371.9 60.7 %copy-start.3 = (bf16[128,256]{1,0:T(8,128)(2,1)S(1)}, bf16[128,256]{1,0:T(8,128)(2,1)}, u32[]{:S(2)}) copy-start(bf16[128,256]{1,0:T(8,128)(2,1)} %all-reduce.5.cloned.1.call-done) | copy-start | bytes 196612
  715.9 1.2 copy-start.2
Sparse Core Ops, SparseCore 0:
  11.3 88.2 all-gather.2
  106.5 70.4 all-reduce.4
  181.4 189.3 all-reduce.6
where the time goes:
time: 749 us; the launch traced here: 742 us
  waiting for transfers between devices  355 us (47%)
  blocking collectives  294 us (39%)
  other arithmetic  55.6 us (7%)
  between operations  15.2 us (2%)
  matrix products  11.3 us (2%)
  local copies, waits for them, and re-layouts  10.4 us (1%)
    psum x1, blocking collectives, body(): project = lax.psum(local_terms, 'fsdp').astype(jnp.bfloat16)  280 us
    psum x1, waiting for transfers between devices, body(): gram_total = lax.psum(gram_of(power_full), 'fsdp')  192 us
    all_gather x1, waiting for transfers between devices, body(): lax.all_gather(q_basis, 'fsdp', axis=0, tiled=True)  91.6 us
    psum x1, waiting for transfers between devices, body(): lax.psum(partial_power.astype(jnp.bfloat16), 'tensor').astype(jnp.float32)  70.6 us
    another operation x6, other arithmetic, orthonormal(): factor = jnp.linalg.cholesky(gram_total)  34 us
    another operation x3, other arithmetic, orthonormal(): lax.linalg.triangular_solve(factor, power_rows, left_side=False, lower=Tr...  19.7 us
  transfers between devices with their start and end apart: 3, of which 3 were waited for; matrix products, arithmetic and copies ran while one was open for 0% of the time, Pallas kernels for 0%

commit v1 on v0

v1 whole, which is shorter than its diff:
```python
import math

import jax
import jax.numpy as jnp
from jax import lax
from jax.sharding import Mesh
from jax.sharding import PartitionSpec as P

D = 8192
FF = 28672
RANK = 256


MU_KEEP = 0.9

NY, NX, NC, NZ = 8, 4, 2, 8


def swap_cores(value):
    return lax.ppermute(value, "c", [(0, 1), (1, 0)])


def gather(value, axis, size):
    spread = jnp.broadcast_to(value[None], (size, *value.shape))
    return lax.all_to_all(spread, axis, 0, 0, tiled=True)


def scatter_sum(value, axis):
    return jnp.sum(lax.all_to_all(value, axis, 0, 0, tiled=True).astype(jnp.float32), axis=0)


def gram_sum(gram):
    part = scatter_sum(gram.reshape(NX * NC, RANK // (NX * NC), RANK), ("x", "c"))
    part = jnp.sum(gather(part, "y", NY), axis=0)
    return gather(part, ("x", "c"), NX * NC).reshape(RANK, RANK)


def halves(value, core):
    half = value.shape[-1] // 2
    first, second = value[..., :half], value[..., half:]
    return jnp.where(core == 0, first, second), jnp.where(core == 0, second, first)


def body(gradient, momentum, q_basis):
    core = lax.axis_index("c")
    rank_dev = q_basis.shape[0]
    blended = (momentum.astype(jnp.float32) + gradient.astype(jnp.float32)).astype(jnp.bfloat16)

    q_half = lax.all_to_all(q_basis, "c", 1, 0, tiled=True)
    q_half = gather(q_half, "y", NY).reshape(-1, q_half.shape[-1])
    q_half = lax.all_gather(q_half, "x", axis=0, tiled=True)
    q_other = swap_cores(q_half)
    b_half, b_other = halves(blended, core)
    contract_last = (((1,), (1,)), ((), ()))
    power_t = lax.dot_general(
        q_half, b_half, contract_last, preferred_element_type=jnp.float32
    ) + lax.dot_general(q_other, b_other, contract_last, preferred_element_type=jnp.float32)
    rows = power_t.shape[1]
    power_t = power_t.reshape(NX, NY, NC * rank_dev, rows).transpose(1, 0, 2, 3)
    power_t = power_t.reshape(RANK, rows).astype(jnp.bfloat16)
    power_t = jnp.sum(gather(power_t, "z", NZ).astype(jnp.float32), axis=0)

    gram = lax.dot_general(
        power_t,
        power_t,
        contract_last,
        precision=lax.Precision.HIGHEST,
        preferred_element_type=jnp.float32,
    )
    factor = jnp.linalg.cholesky(gram_sum(gram))
    basis_t = lax.linalg.triangular_solve(factor, power_t, left_side=True, lower=True)
    basis_t = basis_t.astype(jnp.bfloat16)

    basis_t = basis_t.reshape(NY, NX, NC, rank_dev, rows).transpose(2, 1, 0, 3, 4)
    basis_t = basis_t.reshape(NC, RANK // NC, rows)
    own_t = jnp.where(core == 0, basis_t[0], basis_t[1])
    other_t = jnp.where(core == 0, basis_t[1], basis_t[0])

    contract_rows = (((1,), (0,)), ((), ()))
    other_terms = lax.dot_general(other_t, blended, contract_rows, preferred_element_type=jnp.float32)
    arrived = swap_cores(other_terms.astype(jnp.bfloat16))
    own_terms = lax.dot_general(own_t, blended, contract_rows, preferred_element_type=jnp.float32)
    chip_terms = (own_terms + arrived.astype(jnp.float32)).astype(jnp.bfloat16)
    cols = chip_terms.shape[1]
    project = scatter_sum(chip_terms.reshape(NX * NY, rank_dev, cols), ("x", "y"))
    project = project.astype(jnp.bfloat16)

    own_project = gather(project, "y", NY).reshape(NY * rank_dev, cols)
    own_project = lax.all_gather(own_project, "x", axis=0, tiled=True)
    project_full = jnp.concatenate([own_project, swap_cores(own_project)], axis=0)
    project_wide = project_full.astype(jnp.float32)
    squares = jnp.sum(project_wide * project_wide, axis=1, keepdims=True)
    squares = jnp.sum(gather(squares, "z", NZ), axis=0)
    q_full = (project_wide / jnp.sqrt(squares + 1e-06)).astype(jnp.bfloat16)

    basis_own_first = jnp.concatenate([own_t, other_t], axis=0)
    contract_rank = (((0,), (0,)), ((), ()))
    carried = lax.dot_general(
        basis_own_first, project_full, contract_rank, preferred_element_type=jnp.float32
    )
    momentum_next = (blended.astype(jnp.float32) - (1.0 - MU_KEEP) * carried).astype(jnp.bfloat16)
    scale_factor = math.sqrt(D * FF / RANK)
    scaled = lax.dot_general(
        basis_own_first, q_full, contract_rank, preferred_element_type=jnp.float32
    )
    update = (scale_factor * scaled).astype(jnp.bfloat16)
    place = lax.axis_index("x") * NY + lax.axis_index("y")
    q_next = lax.dynamic_slice_in_dim(q_full, place * rank_dev, rank_dev, 0)
    return (momentum_next, update, q_next)


def solution(mesh):
    split = Mesh(mesh.devices.reshape(NY, NX, NC, NZ), ("y", "x", "c", "z"))
    spec = P(("y", "x", "c"), "z")
    return jax.shard_map(
        body,
        mesh=split,
        in_specs=(spec, spec, spec),
        out_specs=(spec, spec, spec),
        check_vma=False,
    )
```

time: 749 us -> 256 us (0.34)
  waiting for transfers between devices: 355 us -> 27.8 us
  blocking collectives: 294 us -> 123 us
  starting transfers between devices: 0.12 us -> 30.5 us
  between operations: 15.2 us -> 2.26 us
    psum x2 -> x0, blocking collectives: 294 us -> none  [the longest x1 280 us: body(): project = lax.psum(local_terms, 'fsdp').astype(jnp.bfloat16)]
    psum x2 -> x0, waiting for transfers between devices: 263 us -> none  [the longest x1 192 us: body(): gram_total = lax.psum(gram_of(power_full), 'fsdp')]
    all_to_all x0 -> x6, blocking collectives: none -> 100 us  [the longest x3 50.9 us: gather(): return lax.all_to_all(spread, axis, 0, 0, tiled=True)]
    all_gather x1 -> x0, waiting for transfers between devices: 91.6 us -> none  [body(): lax.all_gather(q_basis, 'fsdp', axis=0, tiled=True)]
    all_gather x0 -> x2, blocking collectives: none -> 23.3 us  [the longest x1 12 us: body(): own_project = lax.all_gather(own_project, 'x', axis=0, tiled=True)]
    all_to_all x0 -> x3, waiting for transfers between devices: none -> 23.2 us  [gather(): return lax.all_to_all(spread, axis, 0, 0, tiled=True)]
    ppermute x0 -> x3, starting transfers between devices: none -> 17.8 us  [swap_cores(): return lax.ppermute(value, 'c', [(0, 1), (1, 0)])]
    all_to_all x0 -> x3, starting transfers between devices: none -> 12.7 us  [gather(): return lax.all_to_all(spread, axis, 0, 0, tiled=True)]
  transfers between devices with their start and end apart: 3 -> 6, of which waited for: 3 -> 6; matrix products, arithmetic and copies ran while one was open for 0% -> 1% of each run, Pallas kernels for 0% -> 0%
where the time goes in v1:
time: 256 us; the launch traced here: 255 us
  blocking collectives  123 us (48%)
  other arithmetic  55.6 us (22%)
  starting transfers between devices  30.5 us (12%)
  waiting for transfers between devices  27.8 us (11%)
  local copies, waits for them, and re-layouts  9.91 us (4%)
  matrix products  6.06 us (2%)
    all_to_all x3, blocking collectives, gather(): return lax.all_to_all(spread, axis, 0, 0, tiled=True)  50.9 us
    all_to_all x2, blocking collectives, scatter_sum(): lax.all_to_all(value, axis, 0, 0, tiled=True).astype(jnp.float32)  37.8 us
    another operation x6, other arithmetic, body(): factor = jnp.linalg.cholesky(gram_sum(gram))  33.9 us
    all_to_all x3, waiting for transfers between devices, gather(): return lax.all_to_all(spread, axis, 0, 0, tiled=True)  23.2 us
    another operation x4, other arithmetic, body(): lax.linalg.triangular_solve(factor, power_t, left_side=True, lower=True)  19.9 us
    ppermute x3, starting transfers between devices, swap_cores(): return lax.ppermute(value, 'c', [(0, 1), (1, 0)])  17.8 us
    all_to_all x3, starting transfers between devices, gather(): return lax.all_to_all(spread, axis, 0, 0, tiled=True)  12.7 us
    all_gather x1, blocking collectives, body(): own_project = lax.all_gather(own_project, 'x', axis=0, tiled=True)  12 us
  transfers between devices with their start and end apart: 6, of which 6 were waited for; matrix products, arithmetic and copies ran while one was open for 1% of the time, Pallas kernels for 0%

profile of v1, /device:TPU:1, one launch (start us, length us, event | category | flops | bytes accessed | tf_op | source)
XLA Modules:
  0.0 255.4 jit_solution(8674728804784867174)
XLA Ops:
  0.7 11.3 %all_to_all.56 = bf16[4,2,1792]{2,0,1:T(4,128)(2,1)S(1)} all-to-all(bf16[4,2,1792]{2,0,1:T(4,128)(2,1)} %bitcast.77), channel_id=1, replica_groups=mesh['y'=8,'x'=4,'c'=2,'z'=8] {'c'}, dimensions={1} | all-to-all | bytes 57344 | tf_op jit(solution)/shard_map/all_to_all | solution.py:49
  12.0 0.7 broadcast_in_dim.16
  12.7 3.4 %all-to-all-start.1 = ((bf16[8,8,1792]{2,1,0:T(8,128)(2,1)}), bf16[8,8,1792]{2,1,0:T(8,128)(2,1)S(1)}, u32[]{:S(2)}, u32[]{:S(2)}) async-start(bf16[8,8,1792]{2,1,0:T(8,128)(2,1)} %broadcast_in_dim.16), calls=%async_computation.1 | async-start | bytes 458752 | tf_op jit(solution)/shard_map/all_to_all | solution.py:25
  16.1 11.5 %all-to-all-done.1 = bf16[8,8,1792]{2,1,0:T(8,128)(2,1)S(1)} async-done(((bf16[8,8,1792]{2,1,0:T(8,128)(2,1)}), bf16[8,8,1792]{2,1,0:T(8,128)(2,1)S(1)}, u32[]{:S(2)}, u32[]{:S(2)}) %all-to-all-start.1) | async-done | bytes 229408 | tf_op jit(solution)/shard_map/all_to_all | solution.py:25
  27.6 11.2 %all_gather.6 = bf16[256,1792]{1,0:T(8,128)(2,1)S(1)} all-gather(bf16[64,1792]{1,0:T(8,128)(2,1)S(1)} %bitcast.65), channel_id=1, replica_groups=mesh['y'=8,'x'=4,'c'=2,'z'=8] {'x'}, dimensions={0}, use_global_device_ids=true | all-gather | bytes 1146880 | tf_op jit(solution)/shard_map/all_gather | solution.py:51
  38.8 6.2 %collective-permute-start = (bf16[256,1792]{1,0:T(8,128)(2,1)S(1)}, bf16[256,1792]{1,0:T(8,128)(2,1)S(1)}, u32[]{:S(2)}, u32[]{:S(2)}) collective-permute-start(bf16[256,1792]{1,0:T(8,128)(2,1)S(1)} %all_gather.6), channel_id=1, source_target_pairs={{0,8},{8,0},{1,9},{9,1},{2,10},{10,2},{3,11},{11,3},{4,12},{12,4},... | collective-permute-start | bytes 2752520 | tf_op jit(solution)/shard_map/ppermute | solution.py:20
  45.3 0.5 fusion.8
  45.7 1.4 collective-permute-done
  47.1 0.5 fusion.6
  47.8 24.2 %all_to_all.57 = bf16[8,256,128]{2,1,0:T(8,128)(2,1)S(1)} all-to-all(bf16[8,256,128]{2,1,0:T(8,128)(2,1)S(1)} %broadcast_in_dim.18), channel_id=1, replica_groups=mesh['y'=8,'x'=4,'c'=2,'z'=8] {'z'}, dimensions={0} | all-to-all | bytes 1048576 | tf_op jit(solution)/shard_map/all_to_all | solution.py:25
  72.1 0.4 fusion.17
  72.4 11.8 %all_to_all.58 = f32[8,32,256]{2,1,0:T(8,128)S(1)} all-to-all(f32[8,32,256]{2,1,0:T(8,128)S(1)} %fusion.17), channel_id=1, replica_groups=mesh['y'=8,'x'=4,'c'=2,'z'=8] {'x','c'}, dimensions={0} | all-to-all | bytes 524288 | tf_op jit(solution)/shard_map/all_to_all | solution.py:29
  84.2 12.6 %all_to_all.59 = f32[8,32,256]{2,1,0:T(8,128)S(1)} all-to-all(f32[8,32,256]{2,1,0:T(8,128)S(1)} %broadcast_in_dim.19), channel_id=1, replica_groups=mesh['y'=8,'x'=4,'c'=2,'z'=8] {'y'}, dimensions={0} | all-to-all | bytes 524288 | tf_op jit(solution)/shard_map/all_to_all | solution.py:25
  96.8 0.7 broadcast_in_dim.20
  97.6 6.0 %all-to-all-start.5 = ((f32[8,32,256]{2,1,0:T(8,128)}), f32[8,32,256]{2,1,0:T(8,128)S(1)}, u32[]{:S(2)}, u32[]{:S(2)}) async-start(f32[8,32,256]{2,1,0:T(8,128)} %broadcast_in_dim.20), calls=%async_computation.5 | async-start | bytes 524288 | tf_op jit(solution)/shard_map/all_to_all | solution.py:25
  103.5 6.5 %all-to-all-done.5 = f32[8,32,256]{2,1,0:T(8,128)S(1)} async-done(((f32[8,32,256]{2,1,0:T(8,128)}), f32[8,32,256]{2,1,0:T(8,128)S(1)}, u32[]{:S(2)}, u32[]{:S(2)}) %all-to-all-start.5) | async-done | bytes 262176 | tf_op jit(solution)/shard_map/all_to_all | solution.py:25
  110.3 11.7 %cholesky.50 = f32[128,128]{1,0:T(8,128)S(1)} custom-call(f32[128,128]{1,0:T(8,128)S(1)} %cholesky.118), custom_call_target="Cholesky" | custom-call | tf_op jit(solution)/shard_map/jit(cholesky)/cholesky | solution.py:70
  122.0 9.8 %custom-call.14 = f32[1,128,128]{1,2,0:T(8,128)S(1)} custom-call(f32[1,128,128]{2,1,0:T(8,128)S(1)} %get-tuple-element.26), custom_call_target="InvertDiagBlocksLowerTriangular" | custom-call | tf_op jit(solution)/shard_map/jit(cholesky)/cholesky | solution.py:70
  132.3 11.7 %cholesky.105 = f32[128,128]{1,0:T(8,128)S(1)} custom-call(f32[128,128]{1,0:T(8,128)S(1)} %convolution_subtract_fusion.1), custom_call_target="Cholesky" | custom-call | tf_op jit(solution)/shard_map/jit(cholesky)/cholesky | solution.py:70
  144.1 0.6 compare_reduce_fusion
  146.1 4.0 %while.1 = (s32[]{:T(128)}, f32[256,256]{1,0:T(8,128)S(1)}, s32[2,2]{1,0:T(2,128)S(1)}, f32[2,128,128]{2,1,0:T(8,128)S(1)}, s32[]{:T(128)}) while((s32[]{:T(128)}, f32[256,256]{1,0:T(8,128)S(1)}, s32[2,2]{1,0:T(2,128)S(1)}, f32[2,128,128]{2,1,0:T(8,128)S(1)}, s32[]{:T(128)}) %tuple.29), condition=%wide.while_cond, body=%wide.while_body.sunk | while | flops 2 | bytes 131189 | solution.py:71
  146.1 0.6 fusion.43
  146.7 1.4 bitcast_dynamic-update-slice_fusion.2
  148.1 0.6 fusion.43
  148.7 1.4 bitcast_dynamic-update-slice_fusion.2
  150.1 19.9 %custom-call.15 = f32[2,128,128]{1,2,0:T(8,128)S(1)} custom-call(f32[2,128,128]{2,1,0:T(8,128)S(1)} %get-tuple-element.10), custom_call_target="InvertDiagBlocksLowerTriangular" | custom-call | tf_op jit(solution)/shard_map/triangular_solve | solution.py:71
  170.0 0.3 fusion.28
  170.5 0.3 convolution_convert_fusion.1
  170.9 0.4 convolution_convert_fusion
  171.3 2.9 %collective-permute-start.1 = (bf16[128,3584]{1,0:T(8,128)(2,1)S(1)}, bf16[128,3584]{1,0:T(8,128)(2,1)S(1)}, u32[]{:S(2)}, u32[]{:S(2)}) collective-permute-start(bf16[128,3584]{1,0:T(8,128)(2,1)S(1)} %convolution_convert_fusion), channel_id=1, source_target_pairs={{0,8},{8,0},{1,9},{9,1},{2,10},{10,2},{3,11},{11,3},{4,12},{12,4},... | collective-permute-start | bytes 2752520 | tf_op jit(solution)/shard_map/ppermute | solution.py:20
  174.3 2.1 collective-permute-done.1
  176.3 0.4 add_convert_fusion
  176.9 26.1 %all_to_all.60 = bf16[32,4,3584]{2,1,0:T(4,128)(2,1)S(1)} all-to-all(bf16[32,4,3584]{2,1,0:T(4,128)(2,1)S(1)} %reshape.78), channel_id=1, replica_groups=mesh['y'=8,'x'=4,'c'=2,'z'=8] {'x','y'}, dimensions={0} | all-to-all | bytes 1835008 | tf_op jit(solution)/shard_map/all_to_all | solution.py:29
  203.0 0.4 reduce_sum.60
  203.5 14.1 %all_to_all.61 = bf16[8,4,3584]{2,1,0:T(4,128)(2,1)S(1)} all-to-all(bf16[8,4,3584]{2,1,0:T(4,128)(2,1)S(1)} %broadcast_in_dim.21), channel_id=1, replica_groups=mesh['y'=8,'x'=4,'c'=2,'z'=8] {'y'}, dimensions={0} | all-to-all | bytes 458752 | tf_op jit(solution)/shard_map/all_to_all | solution.py:25
  217.6 12.0 %all_gather.7 = bf16[128,3584]{1,0:T(8,128)(2,1)} all-gather(bf16[32,3584]{1,0:T(8,128)(2,1)S(1)} %reshape.79), channel_id=1, replica_groups=mesh['y'=8,'x'=4,'c'=2,'z'=8] {'x'}, dimensions={0}, use_global_device_ids=true | all-gather | bytes 1146880 | tf_op jit(solution)/shard_map/all_gather | solution.py:89
  229.7 8.6 %collective-permute-start.2 = (bf16[128,3584]{1,0:T(8,128)(2,1)}, bf16[128,3584]{1,0:T(8,128)(2,1)}, u32[]{:S(2)}, u32[]{:S(2)}) collective-permute-start(bf16[128,3584]{1,0:T(8,128)(2,1)} %all_gather.7), channel_id=1, source_target_pairs={{0,8},{8,0},{1,9},{9,1},{2,10},{10,2},{3,11},{11,3},{4,12},{12,4},... | collective-permute-start | bytes 2752520 | tf_op jit(solution)/shard_map/ppermute | solution.py:20
  238.3 1.2 constant_dynamic-update-slice_fusion.1
  239.6 1.2 collective-permute-done.2
  240.7 1.2 constant_dynamic-update-slice_fusion
  242.0 0.4 fusion.3
  242.4 0.6 broadcast_in_dim.22
  243.0 3.3 %all-to-all-start.8 = ((f32[8,256,1]{1,2,0:T(1,128)}), f32[8,256,1]{1,2,0:T(1,128)S(1)}, u32[]{:S(2)}, u32[]{:S(2)}) async-start(f32[8,256,1]{1,2,0:T(1,128)} %broadcast_in_dim.22), calls=%async_computation.8 | async-start | bytes 16384 | tf_op jit(solution)/shard_map/all_to_all | solution.py:25
  246.4 1.4 fusion.1
  247.7 5.1 %all-to-all-done.8 = f32[8,256,1]{1,2,0:T(1,128)S(1)} async-done(((f32[8,256,1]{1,2,0:T(1,128)}), f32[8,256,1]{1,2,0:T(1,128)S(1)}, u32[]{:S(2)}, u32[]{:S(2)}) %all-to-all-start.8) | async-done | bytes 8224 | tf_op jit(solution)/shard_map/all_to_all | solution.py:25
  252.9 0.5 fusion.4
  253.4 1.4 fusion.2
  254.8 0.6 constant_dynamic-slice_fusion.1
  (36 shorter events, 2.0 us)
Async XLA Ops:
  0.6 44.4 %copy-start.1 = (bf16[128,3584]{1,0:T(8,128)(2,1)S(1)}, bf16[128,3584]{1,0:T(8,128)(2,1)}, u32[]{:S(2)}) copy-start(bf16[128,3584]{1,0:T(8,128)(2,1)} %param.4) | copy-start | bytes 2752516
  0.6 44.4 %copy-start = (bf16[128,3584]{1,0:T(8,128)(2,1)S(1)}, bf16[128,3584]{1,0:T(8,128)(2,1)}, u32[]{:S(2)}) copy-start(bf16[128,3584]{1,0:T(8,128)(2,1)} %param.3) | copy-start | bytes 2752516
  12.7 14.9 %all-to-all-start.1 = ((bf16[8,8,1792]{2,1,0:T(8,128)(2,1)}), bf16[8,8,1792]{2,1,0:T(8,128)(2,1)S(1)}, u32[]{:S(2)}, u32[]{:S(2)}) async-start(bf16[8,8,1792]{2,1,0:T(8,128)(2,1)} %broadcast_in_dim.16), calls=%async_computation.1 | async-start | bytes 458752 | tf_op jit(solution)/shard_map/all_to_all | solution.py:25
  38.8 8.3 %collective-permute-start = (bf16[256,1792]{1,0:T(8,128)(2,1)S(1)}, bf16[256,1792]{1,0:T(8,128)(2,1)S(1)}, u32[]{:S(2)}, u32[]{:S(2)}) collective-permute-start(bf16[256,1792]{1,0:T(8,128)(2,1)S(1)} %all_gather.6), channel_id=1, source_target_pairs={{0,8},{8,0},{1,9},{9,1},{2,10},{10,2},{3,11},{11,3},{4,12},{12,4},... | collective-permute-start | bytes 2752520 | tf_op jit(solution)/shard_map/ppermute | solution.py:20
  97.6 12.5 %all-to-all-start.5 = ((f32[8,32,256]{2,1,0:T(8,128)}), f32[8,32,256]{2,1,0:T(8,128)S(1)}, u32[]{:S(2)}, u32[]{:S(2)}) async-start(f32[8,32,256]{2,1,0:T(8,128)} %broadcast_in_dim.20), calls=%async_computation.5 | async-start | bytes 524288 | tf_op jit(solution)/shard_map/all_to_all | solution.py:25
  171.3 5.0 %collective-permute-start.1 = (bf16[128,3584]{1,0:T(8,128)(2,1)S(1)}, bf16[128,3584]{1,0:T(8,128)(2,1)S(1)}, u32[]{:S(2)}, u32[]{:S(2)}) collective-permute-start(bf16[128,3584]{1,0:T(8,128)(2,1)S(1)} %convolution_convert_fusion), channel_id=1, source_target_pairs={{0,8},{8,0},{1,9},{9,1},{2,10},{10,2},{3,11},{11,3},{4,12},{12,4},... | collective-permute-start | bytes 2752520 | tf_op jit(solution)/shard_map/ppermute | solution.py:20
  229.7 11.0 %collective-permute-start.2 = (bf16[128,3584]{1,0:T(8,128)(2,1)}, bf16[128,3584]{1,0:T(8,128)(2,1)}, u32[]{:S(2)}, u32[]{:S(2)}) collective-permute-start(bf16[128,3584]{1,0:T(8,128)(2,1)} %all_gather.7), channel_id=1, source_target_pairs={{0,8},{8,0},{1,9},{9,1},{2,10},{10,2},{3,11},{11,3},{4,12},{12,4},... | collective-permute-start | bytes 2752520 | tf_op jit(solution)/shard_map/ppermute | solution.py:20
  243.0 9.9 %all-to-all-start.8 = ((f32[8,256,1]{1,2,0:T(1,128)}), f32[8,256,1]{1,2,0:T(1,128)S(1)}, u32[]{:S(2)}, u32[]{:S(2)}) async-start(f32[8,256,1]{1,2,0:T(1,128)} %broadcast_in_dim.22), calls=%async_computation.8 | async-start | bytes 16384 | tf_op jit(solution)/shard_map/all_to_all | solution.py:25

commit v2 on v1

v2 whole, which is shorter than its diff:
```python
import math

import jax
import jax.numpy as jnp
from jax import lax
from jax.experimental import pallas as pl
from jax.experimental.pallas import tpu as pltpu
from jax.sharding import Mesh
from jax.sharding import PartitionSpec as P

D = 8192
FF = 28672
RANK = 256


MU_KEEP = 0.9

NY, NX, NC, NZ = 8, 4, 2, 8


def swap_cores(value):
    return lax.ppermute(value, "c", [(0, 1), (1, 0)])


def gather(value, axis, size):
    spread = jnp.broadcast_to(value[None], (size, *value.shape))
    return lax.all_to_all(spread, axis, 0, 0, tiled=True)


def scatter_sum(value, axis):
    return jnp.sum(lax.all_to_all(value, axis, 0, 0, tiled=True).astype(jnp.float32), axis=0)


def gram_sum(power_t):
    half = RANK // 2
    upper, lower = power_t[:half], power_t[half:]

    def product(left, right):
        return lax.dot_general(
            left,
            right,
            (((1,), (1,)), ((), ())),
            precision=lax.Precision.HIGHEST,
            preferred_element_type=jnp.float32,
        )

    gram = jnp.concatenate(
        [product(upper, upper), product(upper, lower), product(lower, lower)], axis=0
    )
    part = scatter_sum(gram.reshape(NX * NC, -1, half), ("x", "c"))
    part = jnp.sum(gather(part, "y", NY), axis=0)
    return gather(part, ("x", "c"), NX * NC).reshape(3 * half, half)


SUB, LANES = 8, 128
PANEL = 64


def across(value, lane):
    return jnp.broadcast_to(value[:, lane : lane + 1], (SUB, LANES))


def down(value, row):
    return jnp.broadcast_to(value[row : row + 1, :], (SUB, LANES))


def eliminate(tiles, base, last):
    first = base // LANES
    groups = PANEL // SUB
    row_id = lax.broadcasted_iota(jnp.int32, (SUB, LANES), 0)
    for top in range(groups):
        lane = (base + top * SUB) % LANES
        cols = [[across(tiles[g, first], lane + k) for g in range(top, groups)] for k in range(SUB)]
        rows = [[down(tiles[top, t], k) for t in range(first, last)] for k in range(SUB)]
        pivots = None
        steps = []
        for k in range(SUB):
            pivot = down(cols[k][0], k)
            inverse = 1.0 / pivot
            pivots = pivot if pivots is None else jnp.where(row_id == k, pivot, pivots)
            step = [c * inverse for c in cols[k]]
            step[0] = jnp.where(row_id > k, step[0], 0.0)
            for m in range(k + 1, SUB):
                entry = down(cols[m][0], k)
                cols[m] = [c - s * entry for c, s in zip(cols[m], step)]
                factor = down(step[0], m)
                rows[m] = [x - factor * y for x, y in zip(rows[m], rows[k])]
            steps.append(step)
        for g in range(top, groups):
            for t in range(first, last):
                value = tiles[g, t]
                for k in range(SUB):
                    value = value - steps[k][g - top] * rows[k][t - first]
                tiles[g, t] = value
        scale = lax.rsqrt(pivots)
        for t in range(first, last):
            tiles[top, t] = tiles[top, t] * scale


def orthonormal_kernel(gram_ref, power_ref, basis_ref, work_ref):
    last = work_ref.shape[1] // LANES
    work_ref[:LANES, :LANES] = gram_ref[:LANES]
    work_ref[:LANES, LANES:RANK] = gram_ref[LANES:RANK]
    work_ref[LANES:, LANES:RANK] = gram_ref[RANK:]
    work_ref[:, RANK:] = power_ref[...]
    for base in range(0, RANK, PANEL):
        first = base // LANES
        tiles = {
            (g, t): work_ref[base + g * SUB : base + (g + 1) * SUB, t * LANES : (t + 1) * LANES]
            for g in range(PANEL // SUB)
            for t in range(first, last)
        }
        eliminate(tiles, base, last)
        for (g, t), tile in tiles.items():
            work_ref[base + g * SUB : base + (g + 1) * SUB, t * LANES : (t + 1) * LANES] = tile
        below = base + PANEL
        if below < RANK:
            start = below // LANES * LANES
            product = lax.dot_general(
                work_ref[base:below, start:RANK],
                work_ref[base:below, start:],
                (((0,), (0,)), ((), ())),
                precision=lax.Precision.HIGHEST,
                preferred_element_type=jnp.float32,
            )
            work_ref[below:, start:] = work_ref[below:, start:] - product[below - start :]
    basis_ref[...] = work_ref[:, RANK:].astype(basis_ref.dtype)


def orthonormal(gram, power_t):
    rows = power_t.shape[1]
    return pl.pallas_call(
        orthonormal_kernel,
        out_shape=jax.ShapeDtypeStruct((RANK, rows), jnp.bfloat16),
        scratch_shapes=[pltpu.VMEM((RANK, RANK + rows), jnp.float32)],
        compiler_params=pltpu.CompilerParams(vmem_limit_bytes=16 * 2**20),
        cost_estimate=pl.CostEstimate(flops=10**9, bytes_accessed=10**6, transcendentals=0),
        name="orthonormal",
    )(gram, power_t)


def finish_kernel(
    first_ref,
    squares_ref,
    basis_ref,
    own_ref,
    other_ref,
    project_ref,
    blended_ref,
    momentum_ref,
    update_ref,
    q_ref,
    left_ref,
):
    inverse = 1.0 / jnp.sqrt(squares_ref[...] + 1e-06)
    rows = momentum_ref.shape[0]

    @pl.when(pl.program_id(0) == 0)
    def _():
        basis = basis_ref[...].astype(jnp.float32).T
        left_ref[:rows] = basis.astype(jnp.bfloat16)
        left_ref[rows:] = (basis * inverse).astype(jnp.bfloat16)

    project = jnp.concatenate([own_ref[...], other_ref[...]], axis=0)
    both = jnp.dot(left_ref[...], project, preferred_element_type=jnp.float32)
    blended = blended_ref[...].astype(jnp.float32)
    momentum_ref[...] = (blended - (1.0 - MU_KEEP) * both[:rows]).astype(jnp.bfloat16)
    update_ref[...] = (math.sqrt(D * FF / RANK) * both[rows:]).astype(jnp.bfloat16)

    shape = (q_ref.shape[0], RANK)
    here = lax.broadcasted_iota(jnp.int32, shape, 1) == first_ref[
        0
    ] + lax.broadcasted_iota(jnp.int32, shape, 0)
    mine = jnp.sum(jnp.where(here, inverse, 0.0), axis=1, keepdims=True)
    q_ref[...] = (project_ref[...].astype(jnp.float32) * mine).astype(jnp.bfloat16)


def finish(first, squares, basis_t, own, other, project, blended):
    rows, cols = blended.shape
    rank_dev = project.shape[0]
    width = 896

    def columns(height):
        return pl.BlockSpec((height, width), lambda j: (0, j))

    def whole(array):
        return pl.BlockSpec(array.shape, lambda j: (0, 0))

    return pl.pallas_call(
        finish_kernel,
        grid=(cols // width,),
        in_specs=[
            pl.BlockSpec(memory_space=pltpu.SMEM),
            whole(squares),
            whole(basis_t),
            columns(RANK // NC),
            columns(RANK // NC),
            columns(rank_dev),
            columns(rows),
        ],
        out_specs=[columns(rows), columns(rows), columns(rank_dev)],
        out_shape=[
            jax.ShapeDtypeStruct((rows, cols), jnp.bfloat16),
            jax.ShapeDtypeStruct((rows, cols), jnp.bfloat16),
            jax.ShapeDtypeStruct((rank_dev, cols), jnp.bfloat16),
        ],
        scratch_shapes=[pltpu.VMEM((2 * rows, RANK), jnp.bfloat16)],
        compiler_params=pltpu.CompilerParams(vmem_limit_bytes=24 * 2**20),
        cost_estimate=pl.CostEstimate(
            flops=4 * rows * RANK * cols, bytes_accessed=5 * 2**20, transcendentals=0
        ),
        name="finish",
    )(first, squares, basis_t, own, other, project, blended)


def own_first(core, rank_dev):
    to = lax.broadcasted_iota(jnp.int32, (RANK, RANK), 0)
    source = lax.broadcasted_iota(jnp.int32, (RANK, RANK), 1)
    i = to % rank_dev
    y = to // rank_dev % NY
    x = to // (rank_dev * NY) % NX
    c = (to // (rank_dev * NY * NX) + core) % NC
    return (((y * NX + x) * NC + c) * rank_dev + i == source).astype(jnp.bfloat16)


def body(gradient, momentum, q_basis):
    core = lax.axis_index("c")
    rank_dev, cols = q_basis.shape
    blended = (momentum.astype(jnp.float32) + gradient.astype(jnp.float32)).astype(jnp.bfloat16)
    order = own_first(core, rank_dev)

    q_own = gather(q_basis, "y", NY).reshape(-1, cols)
    q_own = lax.all_gather(q_own, "x", axis=0, tiled=True)
    q_other = swap_cores(q_own)
    contract_last = (((1,), (1,)), ((), ()))
    power_own = lax.dot_general(q_own, blended, contract_last, preferred_element_type=jnp.float32)
    power_other = lax.dot_general(
        q_other, blended, contract_last, preferred_element_type=jnp.float32
    )
    power_t = jnp.concatenate(
        [power_own.astype(jnp.bfloat16), power_other.astype(jnp.bfloat16)], axis=0
    )
    contract_first = (((0,), (0,)), ((), ()))
    power_t = lax.dot_general(
        order, power_t, contract_first, preferred_element_type=jnp.float32
    ).astype(jnp.bfloat16)
    power_t = jnp.sum(gather(power_t, "z", NZ).astype(jnp.float32), axis=0)

    basis_t = orthonormal(gram_sum(power_t), power_t)
    matmul = (((1,), (0,)), ((), ()))
    basis_t = lax.dot_general(order, basis_t, matmul, preferred_element_type=jnp.float32).astype(
        jnp.bfloat16
    )
    own_t, other_t = basis_t[: RANK // NC], basis_t[RANK // NC :]

    other_terms = lax.dot_general(other_t, blended, matmul, preferred_element_type=jnp.float32)
    arrived = swap_cores(other_terms.astype(jnp.bfloat16))
    own_terms = lax.dot_general(own_t, blended, matmul, preferred_element_type=jnp.float32)
    chip_terms = (own_terms + arrived.astype(jnp.float32)).astype(jnp.bfloat16)
    project = scatter_sum(chip_terms.reshape(NX * NY, rank_dev, cols), ("x", "y"))
    project = project.astype(jnp.bfloat16)

    own_project = gather(project, "y", NY).reshape(NY * rank_dev, cols)
    wide = own_project.astype(jnp.float32)
    squares = gather(jnp.sum(wide * wide, axis=1)[None], ("x", "z"), NX * NZ)
    squares = jnp.sum(squares.reshape(NX, NZ, NY * rank_dev), axis=1).reshape(1, -1)
    own_project = lax.all_gather(own_project, "x", axis=0, tiled=True)
    own_project, squares = lax.optimization_barrier((own_project, squares))
    place = lax.axis_index("x") * NY + lax.axis_index("y")
    return finish(
        (place * rank_dev).reshape(1),
        jnp.concatenate([squares, swap_cores(squares)], axis=1),
        basis_t,
        own_project,
        swap_cores(own_project),
        project,
        blended,
    )


def solution(mesh):
    split = Mesh(mesh.devices.reshape(NY, NX, NC, NZ), ("y", "x", "c", "z"))
    spec = P(("y", "x", "c"), "z")
    return jax.shard_map(
        body,
        mesh=split,
        in_specs=(spec, spec, spec),
        out_specs=(spec, spec, spec),
        check_vma=False,
    )
```

time: 256 us -> 190 us (0.74)
  other arithmetic: 55.6 us -> 0.97 us
  waiting for transfers between devices: 27.8 us -> 13.5 us
  Pallas kernels: 0 us -> 11.1 us
  local copies, waits for them, and re-layouts: 9.91 us -> 2.78 us
    another operation x10 -> x0, other arithmetic: 53.9 us -> none  [the longest x6 33.9 us: body(): factor = jnp.linalg.cholesky(gram_sum(gram))]
    all_to_all x3 -> x2, waiting for transfers between devices: 23.2 us -> 8.94 us  [gather(): return lax.all_to_all(spread, axis, 0, 0, tiled=True)]
    all_to_all x3 -> x4, blocking collectives: 50.9 us -> 62.4 us  [gather(): return lax.all_to_all(spread, axis, 0, 0, tiled=True)]
    all_to_all x1 -> x0, blocking collectives: 11.3 us -> none  [body(): q_half = lax.all_to_all(q_basis, 'c', 1, 0, tiled=True)]
    pallas_call x0 -> x2, Pallas kernels: none -> 11.1 us  [the longest x1 8.29 us: orthonormal(): pl.pallas_call(orthonormal_kernel, out_shape=jax.ShapeDtypeStruct((RANK,...]
    another operation x9 -> x0, local copies, waits for them, and re-layouts: 4.05 us -> none
    ppermute x3 -> x4, starting transfers between devices: 17.8 us -> 20.9 us  [swap_cores(): return lax.ppermute(value, 'c', [(0, 1), (1, 0)])]
    all_to_all x3 -> x2, starting transfers between devices: 12.7 us -> 11.7 us  [gather(): return lax.all_to_all(spread, axis, 0, 0, tiled=True)]
  transfers between devices with their start and end apart: 6 -> 6, of which waited for: 6 -> 4; matrix products, arithmetic and copies ran while one was open for 1% -> 0% of each run, Pallas kernels for 0% -> 0%
where the time goes in v2:
time: 190 us; the launch traced here: 189 us
  blocking collectives  123 us (65%)
  starting transfers between devices  32.6 us (17%)
  waiting for transfers between devices  13.5 us (7%)
  Pallas kernels  11.1 us (6%)
  matrix products  4.06 us (2%)
  local copies, waits for them, and re-layouts  2.78 us (1%)
    all_to_all x4, blocking collectives, gather(): return lax.all_to_all(spread, axis, 0, 0, tiled=True)  62.4 us
    all_to_all x2, blocking collectives, scatter_sum(): lax.all_to_all(value, axis, 0, 0, tiled=True).astype(jnp.float32)  36.3 us
    ppermute x4, starting transfers between devices, swap_cores(): return lax.ppermute(value, 'c', [(0, 1), (1, 0)])  20.9 us
    all_gather x1, blocking collectives, body(): q_own = lax.all_gather(q_own, 'x', axis=0, tiled=True)  12.5 us
    all_gather x1, blocking collectives, body(): own_project = lax.all_gather(own_project, 'x', axis=0, tiled=True)  12.1 us
    all_to_all x2, starting transfers between devices, gather(): return lax.all_to_all(spread, axis, 0, 0, tiled=True)  11.7 us
    all_to_all x2, waiting for transfers between devices, gather(): return lax.all_to_all(spread, axis, 0, 0, tiled=True)  8.94 us
    pallas_call x1, Pallas kernels, orthonormal(): pl.pallas_call(orthonormal_kernel, out_shape=jax.ShapeDtypeStruct((RANK,...  8.29 us
  transfers between devices with their start and end apart: 6, of which 4 were waited for; matrix products, arithmetic and copies ran while one was open for 0% of the time, Pallas kernels for 0%

profile of v2, /device:TPU:1, one launch (start us, length us, event | category | flops | bytes accessed | tf_op | source)
XLA Modules:
  0.0 189.2 jit_solution(12877185981066824180)
XLA Ops:
  0.6 1.5 broadcast_in_dim.14
  2.1 0.0 copy-start.1
  2.1 7.8 %all-to-all-start = ((bf16[8,4,3584]{2,1,0:T(4,128)(2,1)}), bf16[8,4,3584]{2,1,0:T(4,128)(2,1)S(1)}, u32[]{:S(2)}, u32[]{:S(2)}) async-start(bf16[8,4,3584]{2,1,0:T(4,128)(2,1)} %broadcast_in_dim.14), calls=%async_computation | async-start | bytes 458752 | tf_op jit(solution)/shard_map/all_to_all | solution.py:27
  9.9 0.0 copy-start
  10.0 8.9 %all-to-all-done = bf16[8,4,3584]{2,1,0:T(4,128)(2,1)S(1)} async-done(((bf16[8,4,3584]{2,1,0:T(4,128)(2,1)}), bf16[8,4,3584]{2,1,0:T(4,128)(2,1)S(1)}, u32[]{:S(2)}, u32[]{:S(2)}) %all-to-all-start) | async-done | bytes 229408 | tf_op jit(solution)/shard_map/all_to_all | solution.py:27
  18.9 0.1 reshape.41
  19.0 12.5 %all_gather.6 = bf16[128,3584]{1,0:T(8,128)(2,1)S(1)} all-gather(bf16[32,3584]{1,0:T(8,128)(2,1)S(1)} %reshape.41), channel_id=1, replica_groups=mesh['y'=8,'x'=4,'c'=2,'z'=8] {'x'}, dimensions={0}, use_global_device_ids=true | all-gather | bytes 1146880 | tf_op jit(solution)/shard_map/all_gather | solution.py:233
  31.5 7.8 %collective-permute-start = (bf16[128,3584]{1,0:T(8,128)(2,1)S(1)}, bf16[128,3584]{1,0:T(8,128)(2,1)S(1)}, u32[]{:S(2)}, u32[]{:S(2)}) collective-permute-start(bf16[128,3584]{1,0:T(8,128)(2,1)S(1)} %all_gather.6), channel_id=1, source_target_pairs={{0,8},{8,0},{1,9},{9,1},{2,10},{10,2},{3,11},{11,3},{4,12},{12,4},... | collective-permute-start | bytes 2752520 | tf_op jit(solution)/shard_map/ppermute | solution.py:22
  39.4 0.0 copy-done.1
  39.4 0.0 copy-done
  39.4 0.2 add_convert_fusion.1.blended_ref
  39.6 0.4 fusion
  40.0 1.4 collective-permute-done
  41.4 0.4 fusion.1
  41.8 0.7 convolution_convert_fusion.2
  42.5 0.1 broadcast_in_dim.15
  42.6 26.2 %all_to_all.40 = bf16[8,256,128]{2,1,0:T(8,128)(2,1)S(1)} all-to-all(bf16[8,256,128]{2,1,0:T(8,128)(2,1)S(1)} %broadcast_in_dim.15), channel_id=1, replica_groups=mesh['y'=8,'x'=4,'c'=2,'z'=8] {'z'}, dimensions={0} | all-to-all | bytes 1048576 | tf_op jit(solution)/shard_map/all_to_all | solution.py:27
  68.8 0.1 convert_reduce_fusion.power_ref
  68.9 0.3 fusion.15
  69.1 0.3 fusion.17
  69.4 0.3 fusion.20
  69.7 10.2 %all_to_all.41 = f32[8,48,128]{2,1,0:T(8,128)S(1)} all-to-all(f32[8,48,128]{2,1,0:T(8,128)S(1)} %bitcast.18), channel_id=1, replica_groups=mesh['y'=8,'x'=4,'c'=2,'z'=8] {'x','c'}, dimensions={0} | all-to-all | bytes 393216 | tf_op jit(solution)/shard_map/all_to_all | solution.py:31
  80.0 11.0 %all_to_all.42 = f32[8,48,128]{2,1,0:T(8,128)S(1)} all-to-all(f32[8,48,128]{2,1,0:T(8,128)S(1)} %broadcast_in_dim.16), channel_id=1, replica_groups=mesh['y'=8,'x'=4,'c'=2,'z'=8] {'y'}, dimensions={0} | all-to-all | bytes 393216 | tf_op jit(solution)/shard_map/all_to_all | solution.py:27
  91.1 11.1 %all_to_all.43 = f32[8,48,128]{2,1,0:T(8,128)S(1)} all-to-all(f32[8,48,128]{2,1,0:T(8,128)S(1)} %broadcast_in_dim.17), channel_id=1, replica_groups=mesh['y'=8,'x'=4,'c'=2,'z'=8] {'x','c'}, dimensions={0} | all-to-all | bytes 393216 | tf_op jit(solution)/shard_map/all_to_all | solution.py:27
  102.1 8.3 %orthonormal.1 = bf16[256,128]{1,0:T(8,128)(2,1)S(1)} custom-call(f32[384,128]{1,0:T(8,128)S(1)} %bitcast.17, f32[256,128]{1,0:T(8,128)S(1)} %convert_reduce_fusion.power_ref), custom_call_target="tpu_custom_call" | custom-call | flops 1000000000 | bytes 1000000 | tf_op jit(solution)/shard_map/orthonormal/pallas_call | solution.py:132
  110.4 1.0 convolution_convert_fusion.1.basis_ref
  111.4 0.4 convolution_convert_fusion
  111.8 2.9 %collective-permute-start.1 = (bf16[128,3584]{1,0:T(8,128)(2,1)S(1)}, bf16[128,3584]{1,0:T(8,128)(2,1)S(1)}, u32[]{:S(2)}, u32[]{:S(2)}) collective-permute-start(bf16[128,3584]{1,0:T(8,128)(2,1)S(1)} %convolution_convert_fusion), channel_id=1, source_target_pairs={{0,8},{8,0},{1,9},{9,1},{2,10},{10,2},{3,11},{11,3},{4,12},{12,4},... | collective-permute-start | bytes 2752520 | tf_op jit(solution)/shard_map/ppermute | solution.py:22
  114.7 2.1 %collective-permute-done.1 = bf16[128,3584]{1,0:T(8,128)(2,1)S(1)} collective-permute-done((bf16[128,3584]{1,0:T(8,128)(2,1)S(1)}, bf16[128,3584]{1,0:T(8,128)(2,1)S(1)}, u32[]{:S(2)}, u32[]{:S(2)}) %collective-permute-start.1) | collective-permute-done | bytes 917536 | tf_op jit(solution)/shard_map/ppermute | solution.py:22
  116.8 0.4 add_convert_fusion
  117.2 0.2 reshape.44
  117.4 26.1 %all_to_all.44 = bf16[32,4,3584]{2,1,0:T(4,128)(2,1)S(1)} all-to-all(bf16[32,4,3584]{2,1,0:T(4,128)(2,1)S(1)} %reshape.44), channel_id=1, replica_groups=mesh['y'=8,'x'=4,'c'=2,'z'=8] {'x','y'}, dimensions={0} | all-to-all | bytes 1835008 | tf_op jit(solution)/shard_map/all_to_all | solution.py:31
  143.4 0.4 reduce_sum.60.project_ref
  143.8 0.1 broadcast_in_dim.18
  143.9 14.1 %all_to_all.45 = bf16[8,4,3584]{2,1,0:T(4,128)(2,1)S(1)} all-to-all(bf16[8,4,3584]{2,1,0:T(4,128)(2,1)S(1)} %broadcast_in_dim.18), channel_id=1, replica_groups=mesh['y'=8,'x'=4,'c'=2,'z'=8] {'y'}, dimensions={0} | all-to-all | bytes 458752 | tf_op jit(solution)/shard_map/all_to_all | solution.py:27
  158.0 0.2 multiply_reduce_fusion
  158.2 0.1 broadcast_in_dim.19
  158.3 0.6 broadcast_in_dim.20
  158.9 3.9 %all-to-all-start.7 = ((f32[32,1,32]{2,1,0:T(1,128)}), f32[32,1,32]{2,1,0:T(1,128)S(1)}, u32[]{:S(2)}, u32[]{:S(2)}) async-start(f32[32,1,32]{2,1,0:T(1,128)} %broadcast_in_dim.20), calls=%async_computation.7 | async-start | bytes 32768 | tf_op jit(solution)/shard_map/all_to_all | solution.py:27
  162.8 0.1 reshape.45
  162.9 12.1 %all_gather.7.own_ref = bf16[128,3584]{1,0:T(8,128)(2,1)S(1)} all-gather(bf16[32,3584]{1,0:T(8,128)(2,1)S(1)} %reshape.45), channel_id=1, replica_groups=mesh['y'=8,'x'=4,'c'=2,'z'=8] {'x'}, dimensions={0}, use_global_device_ids=true | all-gather | bytes 1146880 | tf_op jit(solution)/shard_map/all_gather | solution.py:267
  174.9 0.0 all-to-all-done.7
  175.0 0.1 reshape.47
  175.1 8.4 %collective-permute-start.3 = (bf16[128,3584]{1,0:T(8,128)(2,1)S(1)}, bf16[128,3584]{1,0:T(8,128)(2,1)S(1)}, u32[]{:S(2)}, u32[]{:S(2)}) collective-permute-start(bf16[128,3584]{1,0:T(8,128)(2,1)S(1)} %all_gather.7.own_ref), channel_id=1, source_target_pairs={{0,8},{8,0},{1,9},{9,1},{2,10},{10,2},{3,11},{11,3},{4,12},{12,4},... | collective-permute-start | bytes 2752520 | tf_op jit(solution)/shard_map/ppermute | solution.py:22
  183.4 1.9 %collective-permute-start.2 = (f32[1,128]{1,0:T(1,128)S(1)}, f32[1,128]{1,0:T(1,128)S(1)}, u32[]{:S(2)}, u32[]{:S(2)}) collective-permute-start(f32[1,128]{1,0:T(1,128)S(1)} %reshape.47), channel_id=1, source_target_pairs={{0,8},{8,0},{1,9},{9,1},{2,10},{10,2},{3,11},{11,3},{4,12},{12,4},... | collective-permute-start | bytes 1544 | tf_op jit(solution)/shard_map/ppermute | solution.py:22
  185.4 1.1 collective-permute-done.2
  186.4 0.0 collective-permute-done.3.other_ref
  186.4 2.8 %finish.1 = (bf16[128,3584]{1,0:T(8,128)(2,1)}, bf16[128,3584]{1,0:T(8,128)(2,1)}, bf16[4,3584]{1,0:T(4,128)(2,1)}) custom-call(s32[1]{0:T(128)} %bitcast.first_ref, f32[1,256]{1,0:T(1,128)S(1)} %pad_maximum_fusion.1.squares_ref, bf16[256,128]{1,0:T(8,128)(2,1)S(1)} %convolution_convert_fusion.1.basis_ref, bf16[128,3584]{1,0:T(8,128)(2,1)S(1)} %all_gather.7.own_ref, ...), custom_call_target="tpu_custom_call" | custom-call | flops 469762048 | bytes 5242880 | tf_op jit(solution)/shard_map/finish/pallas_call | solution.py:189
  (13 shorter events, 0.1 us)
Async XLA Ops:
  2.1 37.2 %copy-start.1 = (bf16[128,3584]{1,0:T(8,128)(2,1)S(1)}, bf16[128,3584]{1,0:T(8,128)(2,1)}, u32[]{:S(2)}) copy-start(bf16[128,3584]{1,0:T(8,128)(2,1)} %param.4) | copy-start | bytes 2752516
  2.1 16.8 %all-to-all-start = ((bf16[8,4,3584]{2,1,0:T(4,128)(2,1)}), bf16[8,4,3584]{2,1,0:T(4,128)(2,1)S(1)}, u32[]{:S(2)}, u32[]{:S(2)}) async-start(bf16[8,4,3584]{2,1,0:T(4,128)(2,1)} %broadcast_in_dim.14), calls=%async_computation | async-start | bytes 458752 | tf_op jit(solution)/shard_map/all_to_all | solution.py:27
  9.9 29.5 %copy-start = (bf16[128,3584]{1,0:T(8,128)(2,1)S(1)}, bf16[128,3584]{1,0:T(8,128)(2,1)}, u32[]{:S(2)}) copy-start(bf16[128,3584]{1,0:T(8,128)(2,1)} %param.3) | copy-start | bytes 2752516
  31.5 9.9 %collective-permute-start = (bf16[128,3584]{1,0:T(8,128)(2,1)S(1)}, bf16[128,3584]{1,0:T(8,128)(2,1)S(1)}, u32[]{:S(2)}, u32[]{:S(2)}) collective-permute-start(bf16[128,3584]{1,0:T(8,128)(2,1)S(1)} %all_gather.6), channel_id=1, source_target_pairs={{0,8},{8,0},{1,9},{9,1},{2,10},{10,2},{3,11},{11,3},{4,12},{12,4},... | collective-permute-start | bytes 2752520 | tf_op jit(solution)/shard_map/ppermute | solution.py:22
  111.8 4.9 %collective-permute-start.1 = (bf16[128,3584]{1,0:T(8,128)(2,1)S(1)}, bf16[128,3584]{1,0:T(8,128)(2,1)S(1)}, u32[]{:S(2)}, u32[]{:S(2)}) collective-permute-start(bf16[128,3584]{1,0:T(8,128)(2,1)S(1)} %convolution_convert_fusion), channel_id=1, source_target_pairs={{0,8},{8,0},{1,9},{9,1},{2,10},{10,2},{3,11},{11,3},{4,12},{12,4},... | collective-permute-start | bytes 2752520 | tf_op jit(solution)/shard_map/ppermute | solution.py:22
  158.9 16.0 %all-to-all-start.7 = ((f32[32,1,32]{2,1,0:T(1,128)}), f32[32,1,32]{2,1,0:T(1,128)S(1)}, u32[]{:S(2)}, u32[]{:S(2)}) async-start(f32[32,1,32]{2,1,0:T(1,128)} %broadcast_in_dim.20), calls=%async_computation.7 | async-start | bytes 32768 | tf_op jit(solution)/shard_map/all_to_all | solution.py:27
  175.1 11.4 %collective-permute-start.3 = (bf16[128,3584]{1,0:T(8,128)(2,1)S(1)}, bf16[128,3584]{1,0:T(8,128)(2,1)S(1)}, u32[]{:S(2)}, u32[]{:S(2)}) collective-permute-start(bf16[128,3584]{1,0:T(8,128)(2,1)S(1)} %all_gather.7.own_ref), channel_id=1, source_target_pairs={{0,8},{8,0},{1,9},{9,1},{2,10},{10,2},{3,11},{11,3},{4,12},{12,4},... | collective-permute-start | bytes 2752520 | tf_op jit(solution)/shard_map/ppermute | solution.py:22
  183.4 3.0 %collective-permute-start.2 = (f32[1,128]{1,0:T(1,128)S(1)}, f32[1,128]{1,0:T(1,128)S(1)}, u32[]{:S(2)}, u32[]{:S(2)}) collective-permute-start(f32[1,128]{1,0:T(1,128)S(1)} %reshape.47), channel_id=1, source_target_pairs={{0,8},{8,0},{1,9},{9,1},{2,10},{10,2},{3,11},{11,3},{4,12},{12,4},... | collective-permute-start | bytes 1544 | tf_op jit(solution)/shard_map/ppermute | solution.py:22

commit v3 on v2

--- a/solution.py
+++ b/solution.py
@@ -31,25 +31,10 @@
     return jnp.sum(lax.all_to_all(value, axis, 0, 0, tiled=True).astype(jnp.float32), axis=0)
 
 
-def gram_sum(power_t):
-    half = RANK // 2
-    upper, lower = power_t[:half], power_t[half:]
-
-    def product(left, right):
-        return lax.dot_general(
-            left,
-            right,
-            (((1,), (1,)), ((), ())),
-            precision=lax.Precision.HIGHEST,
-            preferred_element_type=jnp.float32,
-        )
-
-    gram = jnp.concatenate(
-        [product(upper, upper), product(upper, lower), product(lower, lower)], axis=0
-    )
-    part = scatter_sum(gram.reshape(NX * NC, -1, half), ("x", "c"))
+def gram_sum(pieces):
+    part = scatter_sum(pieces, "x")
     part = jnp.sum(gather(part, "y", NY), axis=0)
-    return gather(part, ("x", "c"), NX * NC).reshape(3 * half, half)
+    return gather(part, ("x", "c"), NX * NC).reshape(-1, part.shape[-1])
 
 
 SUB, LANES = 8, 128
@@ -97,6 +82,51 @@
             tiles[top, t] = tiles[top, t] * scale
 
 
+def gram_kernel(core_ref, order_ref, own_ref, other_ref, power_ref, gram_ref):
+    half = own_ref.shape[1] // 2
+    other = jnp.concatenate([other_ref[:, half:], other_ref[:, :half]], axis=1)
+    exact = {"precision": lax.Precision.HIGHEST, "preferred_element_type": jnp.float32}
+    power = lax.dot_general(
+        order_ref[...].astype(jnp.float32),
+        jnp.concatenate([own_ref[...], other], axis=0),
+        (((0,), (0,)), ((), ())),
+        **exact,
+    )
+    power_ref[...] = power
+    contract_last = (((1,), (1,)), ((), ()))
+    upper, lower = power[:LANES], power[LANES:]
+    gram = jnp.concatenate(
+        [
+            lax.dot_general(upper, upper, contract_last, **exact),
+            lax.dot_general(upper, lower, contract_last, **exact),
+            lax.dot_general(lower, lower, contract_last, **exact),
+        ],
+        axis=0,
+    )
+    height = gram_ref.shape[1]
+    for x in range(NX):
+        even = gram[2 * x * height : (2 * x + 1) * height]
+        odd = gram[(2 * x + 1) * height : (2 * x + 2) * height]
+        gram_ref[x] = jnp.where(core_ref[0] == 0, even, odd)
+
+
+def gram_pieces(core, order, own, other):
+    rows = own.shape[1]
+    vmem = pl.BlockSpec(memory_space=pltpu.VMEM)
+    return pl.pallas_call(
+        gram_kernel,
+        in_specs=[pl.BlockSpec(memory_space=pltpu.SMEM), vmem, vmem, vmem],
+        out_specs=[vmem, vmem],
+        out_shape=[
+            jax.ShapeDtypeStruct((RANK, rows), jnp.float32),
+            jax.ShapeDtypeStruct((NX, 3 * LANES // (NX * NC), LANES), jnp.float32),
+        ],
+        compiler_params=pltpu.CompilerParams(vmem_limit_bytes=16 * 2**20),
+        cost_estimate=pl.CostEstimate(flops=10**9, bytes_accessed=10**6, transcendentals=0),
+        name="gram_pieces",
+    )(core.reshape(1), order, own, other)
+
+
 def orthonormal_kernel(gram_ref, power_ref, basis_ref, work_ref):
     last = work_ref.shape[1] // LANES
     work_ref[:LANES, :LANES] = gram_ref[:LANES]
@@ -139,63 +169,97 @@
     )(gram, power_t)
 
 
+def terms_kernel(core_ref, basis_ref, blended_ref, other_ref, terms_ref):
+    half = RANK // NC
+    basis = jnp.where(core_ref[0] == 0, basis_ref[:half], basis_ref[half:])
+    both = jnp.concatenate([blended_ref[...], other_ref[...]], axis=0)
+    terms = jnp.dot(basis, both, preferred_element_type=jnp.float32)
+    terms_ref[0] = terms.astype(jnp.bfloat16)
+
+
+def project_terms(core, basis_t, blended, other):
+    rows, cols = blended.shape
+    width = cols // 4
+    columns = pl.BlockSpec((rows, width), lambda j: (0, j))
+    return pl.pallas_call(
+        terms_kernel,
+        grid=(4,),
+        in_specs=[
+            pl.BlockSpec(memory_space=pltpu.SMEM),
+            pl.BlockSpec(basis_t.shape, lambda j: (0, 0)),
+            columns,
+            columns,
+        ],
+        out_specs=pl.BlockSpec((1, RANK // NC, width), lambda j: (j // 2, 0, j % 2)),
+        out_shape=jax.ShapeDtypeStruct((2, RANK // NC, cols // 2), jnp.bfloat16),
+        compiler_params=pltpu.CompilerParams(vmem_limit_bytes=24 * 2**20),
+        cost_estimate=pl.CostEstimate(
+            flops=2 * rows * RANK * cols, bytes_accessed=3 * 2**20, transcendentals=0
+        ),
+        name="project_terms",
+    )(core.reshape(1), basis_t, blended, other)
+
+
 def finish_kernel(
+    core_ref,
     first_ref,
     squares_ref,
     basis_ref,
     own_ref,
     other_ref,
-    project_ref,
     blended_ref,
     momentum_ref,
     update_ref,
     q_ref,
     left_ref,
+    pick_ref,
 ):
-    inverse = 1.0 / jnp.sqrt(squares_ref[...] + 1e-06)
     rows = momentum_ref.shape[0]
+    half = RANK // NC
+    swap = core_ref[0] != 0
 
     @pl.when(pl.program_id(0) == 0)
     def _():
+        inverse = 1.0 / jnp.sqrt(squares_ref[...] + 1e-06)
         basis = basis_ref[...].astype(jnp.float32).T
+        scaled = basis * inverse
         left_ref[:rows] = basis.astype(jnp.bfloat16)
-        left_ref[rows:] = (basis * inverse).astype(jnp.bfloat16)
-
-    project = jnp.concatenate([own_ref[...], other_ref[...]], axis=0)
+        left_ref[rows:] = scaled.astype(jnp.bfloat16)
+        rank = lax.broadcasted_iota(jnp.int32, pick_ref.shape, 1)
+        wanted = first_ref[0] + lax.broadcasted_iota(jnp.int32, pick_ref.shape, 0)
+        pick_ref[...] = jnp.where(rank == wanted, inverse, 0.0)
+
+    own, other = own_ref[0], other_ref[0]
+    project = jnp.concatenate([jnp.where(swap, other, own), jnp.where(swap, own, other)], axis=0)
     both = jnp.dot(left_ref[...], project, preferred_element_type=jnp.float32)
     blended = blended_ref[...].astype(jnp.float32)
     momentum_ref[...] = (blended - (1.0 - MU_KEEP) * both[:rows]).astype(jnp.bfloat16)
     update_ref[...] = (math.sqrt(D * FF / RANK) * both[rows:]).astype(jnp.bfloat16)
-
-    shape = (q_ref.shape[0], RANK)
-    here = lax.broadcasted_iota(jnp.int32, shape, 1) == first_ref[
-        0
-    ] + lax.broadcasted_iota(jnp.int32, shape, 0)
-    mine = jnp.sum(jnp.where(here, inverse, 0.0), axis=1, keepdims=True)
-    q_ref[...] = (project_ref[...].astype(jnp.float32) * mine).astype(jnp.bfloat16)
-
-
-def finish(first, squares, basis_t, own, other, project, blended):
+    chosen = jnp.where(pick_ref[...] != 0.0, 1.0, 0.0).astype(jnp.bfloat16)
+    scale = jnp.sum(pick_ref[...], axis=1, keepdims=True)
+    picked = jnp.dot(chosen, project, preferred_element_type=jnp.float32) * scale
+    q_ref[...] = picked[: q_ref.shape[0]].astype(jnp.bfloat16)
+
+
+def finish(core, first, squares, basis_t, own, other, blended, rank_dev):
     rows, cols = blended.shape
-    rank_dev = project.shape[0]
-    width = 896
+    width = cols // 4
 
     def columns(height):
         return pl.BlockSpec((height, width), lambda j: (0, j))
 
-    def whole(array):
-        return pl.BlockSpec(array.shape, lambda j: (0, 0))
-
+    halves = pl.BlockSpec((1, RANK // NC, width), lambda j: (j // 2, 0, j % 2))
+    smem = pl.BlockSpec(memory_space=pltpu.SMEM)
     return pl.pallas_call(
         finish_kernel,
-        grid=(cols // width,),
+        grid=(4,),
         in_specs=[
-            pl.BlockSpec(memory_space=pltpu.SMEM),
-            whole(squares),
-            whole(basis_t),
-            columns(RANK // NC),
-            columns(RANK // NC),
-            columns(rank_dev),
+            smem,
+            smem,
+            pl.BlockSpec(squares.shape, lambda j: (0, 0)),
+            pl.BlockSpec((RANK, rows), lambda j: (0, 0)),
+            halves,
+            halves,
             columns(rows),
         ],
         out_specs=[columns(rows), columns(rows), columns(rank_dev)],
@@ -204,13 +268,16 @@
             jax.ShapeDtypeStruct((rows, cols), jnp.bfloat16),
             jax.ShapeDtypeStruct((rank_dev, cols), jnp.bfloat16),
         ],
-        scratch_shapes=[pltpu.VMEM((2 * rows, RANK), jnp.bfloat16)],
+        scratch_shapes=[
+            pltpu.VMEM((2 * rows, RANK), jnp.bfloat16),
+            pltpu.VMEM((SUB, RANK), jnp.float32),
+        ],
         compiler_params=pltpu.CompilerParams(vmem_limit_bytes=24 * 2**20),
         cost_estimate=pl.CostEstimate(
             flops=4 * rows * RANK * cols, bytes_accessed=5 * 2**20, transcendentals=0
         ),
         name="finish",
-    )(first, squares, basis_t, own, other, project, blended)
+    )(core.reshape(1), first.reshape(1), squares, basis_t, own, other, blended)
 
 
 def own_first(core, rank_dev):
@@ -224,57 +291,41 @@
 
 
 def body(gradient, momentum, q_basis):
-    core = lax.axis_index("c")
+    core, x, y = lax.axis_index("c"), lax.axis_index("x"), lax.axis_index("y")
     rank_dev, cols = q_basis.shape
+    half = RANK // NC
     blended = (momentum.astype(jnp.float32) + gradient.astype(jnp.float32)).astype(jnp.bfloat16)
-    order = own_first(core, rank_dev)
+    order = lax.optimization_barrier(own_first(core, rank_dev))
 
     q_own = gather(q_basis, "y", NY).reshape(-1, cols)
+    q_own, blended = lax.optimization_barrier((q_own, blended))
+    other = swap_cores(blended)
     q_own = lax.all_gather(q_own, "x", axis=0, tiled=True)
-    q_other = swap_cores(q_own)
     contract_last = (((1,), (1,)), ((), ()))
-    power_own = lax.dot_general(q_own, blended, contract_last, preferred_element_type=jnp.float32)
-    power_other = lax.dot_general(
-        q_other, blended, contract_last, preferred_element_type=jnp.float32
-    )
-    power_t = jnp.concatenate(
-        [power_own.astype(jnp.bfloat16), power_other.astype(jnp.bfloat16)], axis=0
-    )
-    contract_first = (((0,), (0,)), ((), ()))
-    power_t = lax.dot_general(
-        order, power_t, contract_first, preferred_element_type=jnp.float32
-    ).astype(jnp.bfloat16)
-    power_t = jnp.sum(gather(power_t, "z", NZ).astype(jnp.float32), axis=0)
-
-    basis_t = orthonormal(gram_sum(power_t), power_t)
-    matmul = (((1,), (0,)), ((), ()))
-    basis_t = lax.dot_general(order, basis_t, matmul, preferred_element_type=jnp.float32).astype(
-        jnp.bfloat16
-    )
-    own_t, other_t = basis_t[: RANK // NC], basis_t[RANK // NC :]
-
-    other_terms = lax.dot_general(other_t, blended, matmul, preferred_element_type=jnp.float32)
-    arrived = swap_cores(other_terms.astype(jnp.bfloat16))
-    own_terms = lax.dot_general(own_t, blended, matmul, preferred_element_type=jnp.float32)
-    chip_terms = (own_terms + arrived.astype(jnp.float32)).astype(jnp.bfloat16)
-    project = scatter_sum(chip_terms.reshape(NX * NY, rank_dev, cols), ("x", "y"))
-    project = project.astype(jnp.bfloat16)
-
-    own_project = gather(project, "y", NY).reshape(NY * rank_dev, cols)
-    wide = own_project.astype(jnp.float32)
-    squares = gather(jnp.sum(wide * wide, axis=1)[None], ("x", "z"), NX * NZ)
-    squares = jnp.sum(squares.reshape(NX, NZ, NY * rank_dev), axis=1).reshape(1, -1)
-    own_project = lax.all_gather(own_project, "x", axis=0, tiled=True)
-    own_project, squares = lax.optimization_barrier((own_project, squares))
-    place = lax.axis_index("x") * NY + lax.axis_index("y")
+    power_own = [
+        lax.dot_general(q_own, b, contract_last, preferred_element_type=jnp.float32).astype(
+            jnp.bfloat16
+        )
+        for b in (blended, other)
+    ]
+    power_own = gather(jnp.concatenate(power_own, axis=1), "z", NZ)
+    power_own = jnp.sum(power_own.astype(jnp.float32), axis=0)
+    power_t, pieces = gram_pieces(core, order, power_own, swap_cores(power_own))
+    basis_t = orthonormal(gram_sum(pieces), power_t)
+
+    terms = project_terms(core, basis_t, blended, other)
+    terms = terms.reshape(NX * NY, SUB, cols // 2)
+    project = scatter_sum(terms, ("x", "y")).astype(jnp.bfloat16)
+    project = gather(project, "y", NY).reshape(NY * SUB, cols // 2)
+    wide = project.astype(jnp.float32)
+    squares = gather(jnp.sum(wide * wide, axis=1)[None], ("c", "x", "z"), NC * NX * NZ)
+    squares = jnp.sum(squares.reshape(NC, 2, NX // 2, NZ, NY * SUB), axis=(1, 3)).reshape(1, RANK)
+    project = lax.all_gather(project, "x", axis=0, tiled=True)
+    project, squares = lax.optimization_barrier((project, squares))
+    project = project.reshape(2, half, cols // 2)
+    first = ((y * NX + x) * NC + core) * rank_dev
     return finish(
-        (place * rank_dev).reshape(1),
-        jnp.concatenate([squares, swap_cores(squares)], axis=1),
-        basis_t,
-        own_project,
-        swap_cores(own_project),
-        project,
-        blended,
+        core, first, squares, basis_t, project, swap_cores(project), blended, rank_dev
     )
 
 

time: 190 us -> 183 us (0.963)
  blocking collectives: 123 us -> 95.9 us
  waiting for transfers between devices: 13.5 us -> 25.6 us
  starting transfers between devices: 32.6 us -> 39.2 us
  matrix products: 4.06 us -> 0.8 us
  Pallas kernels: 11.1 us -> 13.8 us
    all_to_all x4 -> x3, blocking collectives: 62.4 us -> 37.4 us  [gather(): return lax.all_to_all(spread, axis, 0, 0, tiled=True)]
    all_to_all x2 -> x3, waiting for transfers between devices: 8.94 us -> 23.2 us  [gather(): return lax.all_to_all(spread, axis, 0, 0, tiled=True)]
    all_to_all x2 -> x3, starting transfers between devices: 11.7 us -> 25 us  [gather(): return lax.all_to_all(spread, axis, 0, 0, tiled=True)]
    ppermute x4 -> x3, starting transfers between devices: 20.9 us -> 14.2 us  [swap_cores(): return lax.ppermute(value, 'c', [(0, 1), (1, 0)])]
    all_to_all x2, blocking collectives: 36.3 us -> 32.8 us  [scatter_sum(): lax.all_to_all(value, axis, 0, 0, tiled=True).astype(jnp.float32)]
    dot_general x9 -> x2, matrix products: 4.06 us -> 0.8 us  [body(): lax.dot_general(q_own, b, contract_last, preferred_element_type=jnp.float32)]
    pallas_call x1 -> x3, Pallas kernels: 2.76 us -> 5.19 us  [the longest x1 2.81 us: finish(): pl.pallas_call(finish_kernel, grid=(4,), in_specs=[smem, smem, pl.BlockSp...]
    ppermute x4 -> x3, waiting for transfers between devices: 4.59 us -> 2.38 us  [swap_cores(): return lax.ppermute(value, 'c', [(0, 1), (1, 0)])]
  transfers between devices with their start and end apart: 6 -> 6, of which waited for: 4 -> 4; matrix products, arithmetic and copies ran while one was open for 0% -> 2% of each run, Pallas kernels for 0% -> 0%
where the time goes in v3:
time: 183 us; the launch traced here: 182 us
  blocking collectives  95.9 us (52%)
  starting transfers between devices  39.2 us (21%)
  waiting for transfers between devices  25.6 us (14%)
  Pallas kernels  13.8 us (8%)
  local copies, waits for them, and re-layouts  3.34 us (2%)
  other arithmetic  2.73 us (1%)
    all_to_all x3, blocking collectives, gather(): return lax.all_to_all(spread, axis, 0, 0, tiled=True)  37.4 us
    all_to_all x2, blocking collectives, scatter_sum(): lax.all_to_all(value, axis, 0, 0, tiled=True).astype(jnp.float32)  32.8 us
    all_to_all x3, starting transfers between devices, gather(): return lax.all_to_all(spread, axis, 0, 0, tiled=True)  25 us
    all_to_all x3, waiting for transfers between devices, gather(): return lax.all_to_all(spread, axis, 0, 0, tiled=True)  23.2 us
    ppermute x3, starting transfers between devices, swap_cores(): return lax.ppermute(value, 'c', [(0, 1), (1, 0)])  14.2 us
    all_gather x1, blocking collectives, body(): project = lax.all_gather(project, 'x', axis=0, tiled=True)  12.9 us
    all_gather x1, blocking collectives, body(): q_own = lax.all_gather(q_own, 'x', axis=0, tiled=True)  12.8 us
    pallas_call x1, Pallas kernels, orthonormal(): pl.pallas_call(orthonormal_kernel, out_shape=jax.ShapeDtypeStruct((RANK,...  8.6 us
  transfers between devices with their start and end apart: 6, of which 4 were waited for; matrix products, arithmetic and copies ran while one was open for 2% of the time, Pallas kernels for 0%

profile of v3, /device:TPU:1, one launch (start us, length us, event | category | flops | bytes accessed | tf_op | source)
XLA Modules:
  0.0 182.1 jit_solution(8509705796969447913)
XLA Ops:
  0.6 1.5 broadcast_in_dim.14
  2.1 7.7 %all-to-all-start = ((bf16[8,4,3584]{2,1,0:T(4,128)(2,1)}), bf16[8,4,3584]{2,1,0:T(4,128)(2,1)S(1)}, u32[]{:S(2)}, u32[]{:S(2)}) async-start(bf16[8,4,3584]{2,1,0:T(4,128)(2,1)} %broadcast_in_dim.14), calls=%async_computation | async-start | bytes 458752 | tf_op jit(solution)/shard_map/all_to_all | solution.py:27
  9.8 1.7 add_convert_fusion.blended_ref
  11.4 7.4 %all-to-all-done = bf16[8,4,3584]{2,1,0:T(4,128)(2,1)S(1)} async-done(((bf16[8,4,3584]{2,1,0:T(4,128)(2,1)}), bf16[8,4,3584]{2,1,0:T(4,128)(2,1)S(1)}, u32[]{:S(2)}, u32[]{:S(2)}) %all-to-all-start) | async-done | bytes 229408 | tf_op jit(solution)/shard_map/all_to_all | solution.py:27
  18.8 0.1 reshape.47
  18.9 5.6 %collective-permute-start = (bf16[128,3584]{1,0:T(8,128)(2,1)S(1)}, bf16[128,3584]{1,0:T(8,128)(2,1)S(1)}, u32[]{:S(2)}, u32[]{:S(2)}) collective-permute-start(bf16[128,3584]{1,0:T(8,128)(2,1)S(1)} %add_convert_fusion.blended_ref), channel_id=1, source_target_pairs={{0,8},{8,0},{1,9},{9,1},{2,10},{10,2},{3,11},{11,3},{4,12},{12,4},... | collective-permute-start | bytes 2752520 | tf_op jit(solution)/shard_map/ppermute | solution.py:22
  24.4 12.8 %all_gather.6 = bf16[128,3584]{1,0:T(8,128)(2,1)S(1)} all-gather(bf16[32,3584]{1,0:T(8,128)(2,1)S(1)} %reshape.47), channel_id=1, replica_groups=mesh['y'=8,'x'=4,'c'=2,'z'=8] {'x'}, dimensions={0}, use_global_device_ids=true | all-gather | bytes 1146880 | tf_op jit(solution)/shard_map/all_gather | solution.py:303
  37.2 0.4 convolution_convert_fusion.1
  37.6 0.0 collective-permute-done.other_ref
  37.6 0.4 convolution_convert_fusion
  38.1 0.1 copy.8
  38.2 0.8 broadcast_in_dim.15
  39.0 9.8 %all-to-all-start.1 = ((bf16[8,128,256]{2,1,0:T(8,128)(2,1)}), bf16[8,128,256]{2,1,0:T(8,128)(2,1)S(1)}, u32[]{:S(2)}, u32[]{:S(2)}) async-start(bf16[8,128,256]{2,1,0:T(8,128)(2,1)} %broadcast_in_dim.15), calls=%async_computation.1 | async-start | bytes 1048576 | tf_op jit(solution)/shard_map/all_to_all | solution.py:27
  48.9 15.8 %all-to-all-done.1 = bf16[8,128,256]{2,1,0:T(8,128)(2,1)S(1)} async-done(((bf16[8,128,256]{2,1,0:T(8,128)(2,1)}), bf16[8,128,256]{2,1,0:T(8,128)(2,1)S(1)}, u32[]{:S(2)}, u32[]{:S(2)}) %all-to-all-start.1) | async-done | bytes 524320 | tf_op jit(solution)/shard_map/all_to_all | solution.py:27
  64.7 0.1 convert_reduce_fusion.own_ref
  64.8 4.5 %collective-permute-start.1 = (f32[128,256]{1,0:T(8,128)S(1)}, f32[128,256]{1,0:T(8,128)S(1)}, u32[]{:S(2)}, u32[]{:S(2)}) collective-permute-start(f32[128,256]{1,0:T(8,128)S(1)} %convert_reduce_fusion.own_ref), channel_id=1, source_target_pairs={{0,8},{8,0},{1,9},{9,1},{2,10},{10,2},{3,11},{11,3},{4,12},{12,4},... | collective-permute-start | bytes 393224 | tf_op jit(solution)/shard_map/ppermute | solution.py:22
  69.3 0.6 fusion.10.order_ref
  69.9 0.3 collective-permute-done.1.other_ref
  70.2 1.0 gram_pieces.1
  71.3 7.8 %all_to_all.40 = f32[4,48,128]{2,1,0:T(8,128)S(1)} all-to-all(f32[4,48,128]{2,1,0:T(8,128)S(1)} %get-tuple-element.11), channel_id=1, replica_groups=mesh['y'=8,'x'=4,'c'=2,'z'=8] {'x'}, dimensions={0} | all-to-all | bytes 196608 | tf_op jit(solution)/shard_map/all_to_all | solution.py:31
  79.1 11.1 %all_to_all.41 = f32[8,48,128]{2,1,0:T(8,128)S(1)} all-to-all(f32[8,48,128]{2,1,0:T(8,128)S(1)} %broadcast_in_dim.16), channel_id=1, replica_groups=mesh['y'=8,'x'=4,'c'=2,'z'=8] {'y'}, dimensions={0} | all-to-all | bytes 393216 | tf_op jit(solution)/shard_map/all_to_all | solution.py:27
  90.3 11.1 %all_to_all.42 = f32[8,48,128]{2,1,0:T(8,128)S(1)} all-to-all(f32[8,48,128]{2,1,0:T(8,128)S(1)} %broadcast_in_dim.17), channel_id=1, replica_groups=mesh['y'=8,'x'=4,'c'=2,'z'=8] {'x','c'}, dimensions={0} | all-to-all | bytes 393216 | tf_op jit(solution)/shard_map/all_to_all | solution.py:27
  101.4 8.6 %orthonormal.1.basis_ref = bf16[256,256]{1,0:T(8,128)(2,1)S(1)} custom-call(f32[384,128]{1,0:T(8,128)S(1)} %bitcast.14, f32[256,256]{1,0:T(8,128)S(1)} %get-tuple-element.12.power_ref), custom_call_target="tpu_custom_call" | custom-call | flops 1000000000 | bytes 1000000 | tf_op jit(solution)/shard_map/orthonormal/pallas_call | solution.py:162
  110.0 1.4 project_terms.1
  111.4 25.0 %all_to_all.43 = bf16[32,8,1792]{2,1,0:T(8,128)(2,1)S(1)} all-to-all(bf16[32,8,1792]{2,1,0:T(8,128)(2,1)S(1)} %bitcast.11), channel_id=1, replica_groups=mesh['y'=8,'x'=4,'c'=2,'z'=8] {'x','y'}, dimensions={0} | all-to-all | bytes 1835008 | tf_op jit(solution)/shard_map/all_to_all | solution.py:31
  136.4 0.1 reduce_sum.60
  136.5 15.2 %all_to_all.44 = bf16[8,8,1792]{2,1,0:T(8,128)(2,1)S(1)} all-to-all(bf16[8,8,1792]{2,1,0:T(8,128)(2,1)S(1)} %broadcast_in_dim.18), channel_id=1, replica_groups=mesh['y'=8,'x'=4,'c'=2,'z'=8] {'y'}, dimensions={0} | all-to-all | bytes 458752 | tf_op jit(solution)/shard_map/all_to_all | solution.py:27
  151.7 0.1 multiply_reduce_fusion
  151.8 0.1 broadcast_in_dim.19
  151.9 0.6 broadcast_in_dim.20
  152.6 7.5 %all-to-all-start.7 = ((f32[64,1,64]{2,1,0:T(1,128)}), f32[64,1,64]{2,1,0:T(1,128)S(1)}, u32[]{:S(2)}, u32[]{:S(2)}) async-start(f32[64,1,64]{2,1,0:T(1,128)} %broadcast_in_dim.20), calls=%async_computation.7 | async-start | bytes 65536 | tf_op jit(solution)/shard_map/all_to_all | solution.py:27
  160.1 12.9 %all_gather.7 = bf16[256,1792]{1,0:T(8,128)(2,1)S(1)} all-gather(bf16[64,1792]{1,0:T(8,128)(2,1)S(1)} %bitcast.15), channel_id=1, replica_groups=mesh['y'=8,'x'=4,'c'=2,'z'=8] {'x'}, dimensions={0}, use_global_device_ids=true | all-gather | bytes 1146880 | tf_op jit(solution)/shard_map/all_gather | solution.py:323
  173.0 0.0 all-to-all-done.7
  173.0 0.1 reshape.52.squares_ref
  173.1 4.2 %collective-permute-start.2 = (bf16[2,128,1792]{2,1,0:T(8,128)(2,1)S(1)}, bf16[2,128,1792]{2,1,0:T(8,128)(2,1)S(1)}, u32[]{:S(2)}, u32[]{:S(2)}) collective-permute-start(bf16[2,128,1792]{2,1,0:T(8,128)(2,1)S(1)} %bitcast.12), channel_id=1, source_target_pairs={{0,8},{8,0},{1,9},{9,1},{2,10},{10,2},{3,11},{11,3},{4,12},{12,4},... | collective-permute-start | bytes 2752520 | tf_op jit(solution)/shard_map/ppermute | solution.py:22
  177.2 2.1 %collective-permute-done.2.other_ref = bf16[2,128,1792]{2,1,0:T(8,128)(2,1)S(1)} collective-permute-done((bf16[2,128,1792]{2,1,0:T(8,128)(2,1)S(1)}, bf16[2,128,1792]{2,1,0:T(8,128)(2,1)S(1)}, u32[]{:S(2)}, u32[]{:S(2)}) %collective-permute-start.2) | collective-permute-done | bytes 917536 | tf_op jit(solution)/shard_map/ppermute | solution.py:22
  179.3 2.8 %finish.1 = (bf16[128,3584]{1,0:T(8,128)(2,1)}, bf16[128,3584]{1,0:T(8,128)(2,1)}, bf16[4,3584]{1,0:T(4,128)(2,1)}) custom-call(s32[1]{0:T(128)} %bitcast.core_ref, s32[1]{0:T(128)} %bitcast.1.first_ref, f32[1,256]{1,0:T(1,128)S(1)} %reshape.52.squares_ref, bf16[256,256]{1,0:T(8,128)(2,1)S(1)} %orthonormal.1.basis_ref, bf16[2,128,1792]{2,1,0:T(8,128)(2,1)S(1)} %bitcast.13, ...), custom_call_target="tpu_custom_call" | custom-call | flops 469762048 | bytes 5242880 | tf_op jit(solution)/shard_map/finish/pallas_call | solution.py:253
  (13 shorter events, 0.1 us)
Async XLA Ops:
  2.1 16.7 %all-to-all-start = ((bf16[8,4,3584]{2,1,0:T(4,128)(2,1)}), bf16[8,4,3584]{2,1,0:T(4,128)(2,1)S(1)}, u32[]{:S(2)}, u32[]{:S(2)}) async-start(bf16[8,4,3584]{2,1,0:T(4,128)(2,1)} %broadcast_in_dim.14), calls=%async_computation | async-start | bytes 458752 | tf_op jit(solution)/shard_map/all_to_all | solution.py:27
  18.9 18.8 %collective-permute-start = (bf16[128,3584]{1,0:T(8,128)(2,1)S(1)}, bf16[128,3584]{1,0:T(8,128)(2,1)S(1)}, u32[]{:S(2)}, u32[]{:S(2)}) collective-permute-start(bf16[128,3584]{1,0:T(8,128)(2,1)S(1)} %add_convert_fusion.blended_ref), channel_id=1, source_target_pairs={{0,8},{8,0},{1,9},{9,1},{2,10},{10,2},{3,11},{11,3},{4,12},{12,4},... | collective-permute-start | bytes 2752520 | tf_op jit(solution)/shard_map/ppermute | solution.py:22
  39.0 25.7 %all-to-all-start.1 = ((bf16[8,128,256]{2,1,0:T(8,128)(2,1)}), bf16[8,128,256]{2,1,0:T(8,128)(2,1)S(1)}, u32[]{:S(2)}, u32[]{:S(2)}) async-start(bf16[8,128,256]{2,1,0:T(8,128)(2,1)} %broadcast_in_dim.15), calls=%async_computation.1 | async-start | bytes 1048576 | tf_op jit(solution)/shard_map/all_to_all | solution.py:27
  64.8 5.4 %collective-permute-start.1 = (f32[128,256]{1,0:T(8,128)S(1)}, f32[128,256]{1,0:T(8,128)S(1)}, u32[]{:S(2)}, u32[]{:S(2)}) collective-permute-start(f32[128,256]{1,0:T(8,128)S(1)} %convert_reduce_fusion.own_ref), channel_id=1, source_target_pairs={{0,8},{8,0},{1,9},{9,1},{2,10},{10,2},{3,11},{11,3},{4,12},{12,4},... | collective-permute-start | bytes 393224 | tf_op jit(solution)/shard_map/ppermute | solution.py:22
  152.6 20.4 %all-to-all-start.7 = ((f32[64,1,64]{2,1,0:T(1,128)}), f32[64,1,64]{2,1,0:T(1,128)S(1)}, u32[]{:S(2)}, u32[]{:S(2)}) async-start(f32[64,1,64]{2,1,0:T(1,128)} %broadcast_in_dim.20), calls=%async_computation.7 | async-start | bytes 65536 | tf_op jit(solution)/shard_map/all_to_all | solution.py:27
  173.1 6.2 %collective-permute-start.2 = (bf16[2,128,1792]{2,1,0:T(8,128)(2,1)S(1)}, bf16[2,128,1792]{2,1,0:T(8,128)(2,1)S(1)}, u32[]{:S(2)}, u32[]{:S(2)}) collective-permute-start(bf16[2,128,1792]{2,1,0:T(8,128)(2,1)S(1)} %bitcast.12), channel_id=1, source_target_pairs={{0,8},{8,0},{1,9},{9,1},{2,10},{10,2},{3,11},{11,3},{4,12},{12,4},... | collective-permute-start | bytes 2752520 | tf_op jit(solution)/shard_map/ppermute | solution.py:22

commit v4 on v0

v4 whole, which is shorter than its diff:
```python
import math

import jax
import jax.numpy as jnp
from jax import lax
from jax.experimental import pallas as pl
from jax.experimental.pallas import tpu as pltpu
from jax.sharding import Mesh
from jax.sharding import PartitionSpec as P

D = 8192
FF = 28672
RANK = 256


MU_KEEP = 0.9

NY, NX, NC, NZ = 8, 4, 2, 8


def swap_cores(value):
    return lax.ppermute(value, "c", [(0, 1), (1, 0)])


def gather(value, axis, size):
    spread = jnp.broadcast_to(value[None], (size, *value.shape))
    return lax.all_to_all(spread, axis, 0, 0, tiled=True)


def scatter_sum(value, axis):
    return jnp.sum(lax.all_to_all(value, axis, 0, 0, tiled=True).astype(jnp.float32), axis=0)


def in_vmem(kernel, name, flops, outs, *args, scalars=0, scratch=(), hbm_outs=0):
    vmem, smem, hbm = (pl.BlockSpec(memory_space=m) for m in (pltpu.VMEM, pltpu.SMEM, pl.ANY))
    return pl.pallas_call(
        kernel,
        in_specs=[smem] * scalars + [vmem] * (len(args) - scalars),
        out_specs=[hbm] * hbm_outs + [vmem] * (len(outs) - hbm_outs),
        out_shape=[jax.ShapeDtypeStruct(shape, dtype) for shape, dtype in outs],
        scratch_shapes=list(scratch),
        compiler_params=pltpu.CompilerParams(vmem_limit_bytes=24 * 2**20),
        cost_estimate=pl.CostEstimate(flops=flops, bytes_accessed=10**6, transcendentals=0),
        name=name,
    )(*args)


def power_kernel(q_ref, blended_ref, other_ref, spread_ref):
    contract_last = (((1,), (1,)), ((), ()))
    power = [
        lax.dot_general(
            q_ref[...], rows[...], contract_last, preferred_element_type=jnp.float32
        ).astype(jnp.bfloat16)
        for rows in (blended_ref, other_ref)
    ]
    power = jnp.concatenate(power, axis=1)
    for z in range(NZ):
        spread_ref[z] = power


def squares_kernel(project_ref, spread_ref):
    wide = project_ref[...].astype(jnp.float32)
    sums = jnp.sum(wide * wide, axis=1, keepdims=True)
    line = jnp.broadcast_to(sums, (sums.shape[0], LANES)).T[:1]
    spread_ref[...] = jnp.broadcast_to(line[None], spread_ref.shape)


def gram_sum(pieces):
    part = scatter_sum(pieces, "x")
    part = jnp.sum(gather(part, "y", NY), axis=0)
    return gather(part, ("x", "c"), NX * NC).reshape(-1, part.shape[-1])


SUB, LANES = 8, 128
PANEL = 64
STEP = 16
BLOCKS = 14


def across(value, lane):
    return jnp.broadcast_to(value[:, lane : lane + 1], (SUB, LANES))


def down(value, row):
    return jnp.broadcast_to(value[row : row + 1, :], (SUB, LANES))


def total(values):
    while len(values) > 1:
        pairs = [values[i] + values[i + 1] for i in range(0, len(values) - 1, 2)]
        values = pairs + values[len(pairs) * 2 :]
    return values[0]


def eliminate(tiles, base, last):
    first = base // LANES
    groups = PANEL // SUB
    depth = STEP // SUB
    row_id = lax.broadcasted_iota(jnp.int32, (SUB, LANES), 0)
    for top in range(0, groups, depth):
        lane = (base + top * SUB) % LANES
        cols = [
            {g: across(tiles[g, first], lane + k) for g in range(top + k // SUB, groups)}
            for k in range(STEP)
        ]
        rows, steps, pivots = [], [], [None] * depth
        for k in range(STEP):
            level, row = divmod(k, SUB)
            here = top + level
            pivot = down(cols[k][here], row)
            inverse = 1.0 / pivot
            known = pivots[level]
            pivots[level] = pivot if known is None else jnp.where(row_id == row, pivot, known)
            step = {g: cols[k][g] * inverse for g in range(here, groups)}
            step[here] = jnp.where(row_id > row, step[here], 0.0)
            for m in range(k + 1, STEP):
                entry = down(cols[k][top + m // SUB], m % SUB)
                for g in cols[m]:
                    cols[m][g] = cols[m][g] - step[g] * entry
            line = {t: down(tiles[here, t], row) for t in range(first, last)}
            for g in range(here, top + depth):
                for t in range(first, last):
                    tiles[g, t] = tiles[g, t] - step[g] * line[t]
            rows.append(line)
            steps.append(step)
        for g in range(top + depth, groups):
            for t in range(first, last):
                tiles[g, t] = tiles[g, t] - total([s[g] * r[t] for s, r in zip(steps, rows)])
        for level in range(depth):
            scale = lax.rsqrt(pivots[level])
            for t in range(first, last):
                tiles[top + level, t] = tiles[top + level, t] * scale


def orthonormal_kernel(
    core_ref, gram_ref, power_ref, blended_ref, other_ref, basis_ref, terms_ref, work_ref
):
    last = work_ref.shape[1] // LANES
    work_ref[:LANES, :LANES] = gram_ref[:LANES]
    work_ref[:LANES, LANES:RANK] = gram_ref[LANES:RANK]
    work_ref[LANES:, LANES:RANK] = gram_ref[RANK:]
    work_ref[:, RANK:] = power_ref[...]
    for base in range(0, RANK, PANEL):
        first = base // LANES
        tiles = {
            (g, t): work_ref[base + g * SUB : base + (g + 1) * SUB, t * LANES : (t + 1) * LANES]
            for g in range(PANEL // SUB)
            for t in range(first, last)
        }
        eliminate(tiles, base, last)
        for (g, t), tile in tiles.items():
            work_ref[base + g * SUB : base + (g + 1) * SUB, t * LANES : (t + 1) * LANES] = tile
        below = base + PANEL
        if below < RANK:
            start = below // LANES * LANES
            product = lax.dot_general(
                work_ref[base:below, start:RANK],
                work_ref[base:below, start:],
                (((0,), (0,)), ((), ())),
                precision=lax.Precision.HIGHEST,
                preferred_element_type=jnp.float32,
            )
            work_ref[below:, start:] = work_ref[below:, start:] - product[below - start :]
    basis_ref[...] = work_ref[:, RANK:].astype(basis_ref.dtype)
    half = RANK // NC
    mine = jnp.where(core_ref[0] == 0, work_ref[:half, RANK:], work_ref[half:, RANK:])
    mine = mine.astype(jnp.bfloat16)
    width = terms_ref.shape[2] // 2
    for j in range(4):
        columns = slice(j * width, (j + 1) * width)
        both = jnp.concatenate([blended_ref[:, columns], other_ref[:, columns]], axis=0)
        terms = jnp.dot(mine, both, preferred_element_type=jnp.float32)
        terms_ref[j // 2, :, j % 2 * width : (j % 2 + 1) * width] = terms.astype(jnp.bfloat16)


def orthonormal(core, gram, power_t, blended, other):
    rows, cols = blended.shape
    vmem = pl.BlockSpec(memory_space=pltpu.VMEM)
    return pl.pallas_call(
        orthonormal_kernel,
        in_specs=[pl.BlockSpec(memory_space=pltpu.SMEM), vmem, vmem, vmem, vmem],
        out_specs=[vmem, vmem],
        out_shape=[
            jax.ShapeDtypeStruct((RANK, NC * rows), jnp.bfloat16),
            jax.ShapeDtypeStruct((2, RANK // NC, cols // 2), jnp.bfloat16),
        ],
        scratch_shapes=[pltpu.VMEM((RANK, RANK + NC * rows), jnp.float32)],
        compiler_params=pltpu.CompilerParams(vmem_limit_bytes=24 * 2**20),
        cost_estimate=pl.CostEstimate(flops=10**9, bytes_accessed=10**6, transcendentals=0),
        name="orthonormal",
    )(core.reshape(1), gram, power_t, blended, other)


def own_first(core, rank_dev):
    def low(value, size):
        return value & (size - 1), value >> (size.bit_length() - 1)

    to = lax.broadcasted_iota(jnp.int32, (RANK, RANK), 0)
    source = lax.broadcasted_iota(jnp.int32, (RANK, RANK), 1)
    i, to = low(to, rank_dev)
    y, to = low(to, NY)
    x, c = low(to, NX)
    c = (c + core) & (NC - 1)
    return (((y * NX + x) * NC + c) * rank_dev + i == source).astype(jnp.float32)


def gram_kernel(core_ref, own_ref, other_ref, power_ref, gram_ref):
    half = own_ref.shape[1] // 2
    other = jnp.concatenate([other_ref[:, half:], other_ref[:, :half]], axis=1)
    exact = {"precision": lax.Precision.HIGHEST, "preferred_element_type": jnp.float32}
    power = lax.dot_general(
        own_first(core_ref[0], RANK // (NY * NX * NC)),
        jnp.concatenate([own_ref[...], other], axis=0),
        (((0,), (0,)), ((), ())),
        **exact,
    )
    power_ref[...] = power
    contract_last = (((1,), (1,)), ((), ()))
    upper, lower = power[:LANES], power[LANES:]
    gram = jnp.concatenate(
        [
            lax.dot_general(upper, upper, contract_last, **exact),
            lax.dot_general(upper, lower, contract_last, **exact),
            lax.dot_general(lower, lower, contract_last, **exact),
        ],
        axis=0,
    )
    height = gram_ref.shape[1]
    for x in range(NX):
        even = gram[2 * x * height : (2 * x + 1) * height]
        odd = gram[(2 * x + 1) * height : (2 * x + 2) * height]
        gram_ref[x] = jnp.where(core_ref[0] == 0, even, odd)


def gram_pieces(core, own, other):
    rows = own.shape[1]
    vmem = pl.BlockSpec(memory_space=pltpu.VMEM)
    return pl.pallas_call(
        gram_kernel,
        in_specs=[pl.BlockSpec(memory_space=pltpu.SMEM), vmem, vmem],
        out_specs=[vmem, vmem],
        out_shape=[
            jax.ShapeDtypeStruct((RANK, rows), jnp.float32),
            jax.ShapeDtypeStruct((NX, 3 * LANES // (NX * NC), LANES), jnp.float32),
        ],
        compiler_params=pltpu.CompilerParams(vmem_limit_bytes=16 * 2**20),
        cost_estimate=pl.CostEstimate(flops=10**9, bytes_accessed=10**6, transcendentals=0),
        name="gram_pieces",
    )(core.reshape(1), own, other)


def prepare_kernel(core_ref, place_ref, squares_ref, basis_ref, left_ref, pick_ref):
    swap = core_ref[0] != 0
    rows = left_ref.shape[0] // 2

    def own_half_first(value):
        first, second = jnp.split(value, 2, 1)
        turned = jnp.concatenate([second, first], axis=1)
        return jnp.where(swap, turned, value)

    inverse = own_half_first(1.0 / jnp.sqrt(squares_ref[...] + 1e-06))
    basis = own_half_first(basis_ref[:, :rows].astype(jnp.float32).T)
    left_ref[:rows] = basis.astype(jnp.bfloat16)
    left_ref[rows:] = (basis * inverse).astype(jnp.bfloat16)
    rank = lax.broadcasted_iota(jnp.int32, pick_ref.shape, 1)
    wanted = place_ref[0] + lax.broadcasted_iota(jnp.int32, pick_ref.shape, 0)
    pick_ref[...] = jnp.where(rank == wanted, inverse, 0.0)


def finish_kernel(
    left_ref,
    pick_ref,
    own_ref,
    other_ref,
    blended_ref,
    momentum_hbm,
    update_hbm,
    q_hbm,
    momentum_ref,
    update_ref,
    q_ref,
    sems,
    q_sem,
):
    rows, cols = blended_ref.shape
    pick = pick_ref[...]
    scale = jnp.sum(pick, axis=1, keepdims=True)
    chosen = jnp.where(pick != 0.0, 1.0, 0.0).astype(jnp.bfloat16)
    blocks = sems.shape[1]
    width = cols // blocks
    copies = []
    for j in range(blocks):
        columns = slice(j * width, (j + 1) * width)
        side, j = divmod(j, blocks // 2)
        there = slice(j * width, (j + 1) * width)
        project = [ref[side, :, there] for ref in (own_ref, other_ref)]
        project = jnp.concatenate(project, axis=0)
        both = jnp.dot(left_ref[...], project, preferred_element_type=jnp.float32)
        blended = blended_ref[:, columns].astype(jnp.float32)
        momentum = blended - (1.0 - MU_KEEP) * both[:rows]
        momentum_ref[:, columns] = momentum.astype(jnp.bfloat16)
        update_ref[:, columns] = (math.sqrt(D * FF / RANK) * both[rows:]).astype(jnp.bfloat16)
        for n, (source, target) in enumerate(
            ((momentum_ref, momentum_hbm), (update_ref, update_hbm))
        ):
            copy = pltpu.make_async_copy(
                source.at[:, columns],
                target.at[:, columns],
                sems.at[n, side * (blocks // 2) + j],
            )
            copy.start()
            copies.append(copy)
        picked = jnp.dot(chosen, project, preferred_element_type=jnp.float32) * scale
        q_ref[:, columns] = picked[: q_ref.shape[0]].astype(jnp.bfloat16)
    copy = pltpu.make_async_copy(q_ref, q_hbm, q_sem)
    copy.start()
    copies.append(copy)
    for copy in copies:
        copy.wait()


def finish(core, place, squares, basis_t, own, other, blended, rank_dev):
    rows, cols = blended.shape
    whole = ((rows, cols), jnp.bfloat16)
    left, pick = in_vmem(
        prepare_kernel,
        "prepare",
        10**5,
        [((2 * rows, RANK), jnp.bfloat16), ((SUB, RANK), jnp.float32)],
        core.reshape(1),
        place.reshape(1),
        squares,
        basis_t,
        scalars=2,
    )
    return in_vmem(
        finish_kernel,
        "finish",
        4 * rows * RANK * cols,
        [whole, whole, ((rank_dev, cols), jnp.bfloat16)],
        left,
        pick,
        own,
        other,
        blended,
        scratch=[
            pltpu.VMEM(*whole),
            pltpu.VMEM(*whole),
            pltpu.VMEM((rank_dev, cols), jnp.bfloat16),
            pltpu.SemaphoreType.DMA((2, BLOCKS)),
            pltpu.SemaphoreType.DMA,
        ],
        hbm_outs=3,
    )


def body(gradient, momentum, q_basis):
    core, x, y = lax.axis_index("c"), lax.axis_index("x"), lax.axis_index("y")
    rank_dev, cols = q_basis.shape
    half = RANK // NC
    blended = (momentum.astype(jnp.float32) + gradient.astype(jnp.float32)).astype(jnp.bfloat16)

    q_own = gather(q_basis, "y", NY).reshape(-1, cols)
    q_own, other = lax.optimization_barrier((q_own, swap_cores(blended)))
    q_own = lax.all_gather(q_own, "x", axis=0, tiled=True)
    rows = NC * blended.shape[0]
    (spread,) = in_vmem(
        power_kernel,
        "power",
        2 * half * rows * cols,
        [((NZ, half, rows), jnp.bfloat16)],
        q_own,
        blended,
        other,
    )
    power_own = jnp.sum(
        lax.all_to_all(spread, "z", 0, 0, tiled=True).astype(jnp.float32), axis=0
    )
    power_t, pieces = gram_pieces(core, power_own, swap_cores(power_own))
    basis_t, terms = orthonormal(core, gram_sum(pieces), power_t, blended, other)

    terms = terms.reshape(NX * NY, SUB, cols // 2)
    project = scatter_sum(terms, ("x", "y")).astype(jnp.bfloat16)
    project = gather(project, "y", NY).reshape(NY * SUB, cols // 2)
    peers = NC * NX * NZ
    (spread,) = in_vmem(
        squares_kernel,
        "squares",
        10**6,
        [((peers, 1, NY * SUB), jnp.float32)],
        project,
    )
    squares = lax.all_to_all(spread, ("c", "x", "z"), 0, 0, tiled=True)
    squares = jnp.sum(squares.reshape(NC, 2, NX // 2, NZ, NY * SUB), axis=(1, 3)).reshape(1, RANK)
    project = lax.all_gather(project, "x", axis=0, tiled=True)
    project, squares = lax.optimization_barrier((project, squares))
    project = project.reshape(2, half, cols // 2)
    place = (((y * NX + x) * NC + core) * rank_dev + RANK - half * core) % RANK
    return finish(
        core, place, squares, basis_t, project, swap_cores(project), blended, rank_dev
    )


def solution(mesh):
    split = Mesh(mesh.devices.reshape(NY, NX, NC, NZ), ("y", "x", "c", "z"))
    spec = P(("y", "x", "c"), "z")
    return jax.shard_map(
        body,
        mesh=split,
        in_specs=(spec, spec, spec),
        out_specs=(spec, spec, spec),
        check_vma=False,
    )
```

time: 749 us -> 177 us (0.24)
  waiting for transfers between devices: 355 us -> 2.91 us
  blocking collectives: 294 us -> 132 us
  other arithmetic: 55.6 us -> 1.92 us
  starting transfers between devices: 0.12 us -> 26.4 us
  between operations: 15.2 us -> 0.79 us
  Pallas kernels: 0 us -> 12.2 us
  matrix products: 11.3 us -> 0 us
  local copies, waits for them, and re-layouts: 10.4 us -> 0.26 us
    psum x2 -> x0, blocking collectives: 294 us -> none  [the longest x1 280 us: body(): project = lax.psum(local_terms, 'fsdp').astype(jnp.bfloat16)]
    psum x2 -> x0, waiting for transfers between devices: 263 us -> none  [the longest x1 192 us: body(): gram_total = lax.psum(gram_of(power_full), 'fsdp')]
    all_to_all x0 -> x7, blocking collectives: none -> 108 us  [the longest x4 51.5 us: gather(): return lax.all_to_all(spread, axis, 0, 0, tiled=True)]
    all_gather x1 -> x0, waiting for transfers between devices: 91.6 us -> none  [body(): lax.all_gather(q_basis, 'fsdp', axis=0, tiled=True)]
    another operation x9 -> x0, other arithmetic: 53.7 us -> none  [the longest x6 34 us: orthonormal(): factor = jnp.linalg.cholesky(gram_total)]
    all_gather x0 -> x2, blocking collectives: none -> 24.2 us  [the longest x1 12.9 us: body(): project = lax.all_gather(project, 'x', axis=0, tiled=True)]
    ppermute x0 -> x3, starting transfers between devices: none -> 18.9 us  [swap_cores(): return lax.ppermute(value, 'c', [(0, 1), (1, 0)])]
    pallas_call x0 -> x6, Pallas kernels: none -> 12.2 us  [the longest x1 7.72 us: orthonormal(): pl.pallas_call(orthonormal_kernel, in_specs=[pl.BlockSpec(memory_space=pl...]
  transfers between devices with their start and end apart: 3 -> 4, of which waited for: 3 -> 2; matrix products, arithmetic and copies ran while one was open for 0% -> 0% of each run, Pallas kernels for 0% -> 0%
where the time goes in v4:
time: 177 us
  blocking collectives  132 us (75%)
  starting transfers between devices  26.4 us (15%)
  Pallas kernels  12.2 us (7%)
  waiting for transfers between devices  2.91 us (2%)
  other arithmetic  1.92 us (1%)
    all_to_all x4, blocking collectives, gather(): return lax.all_to_all(spread, axis, 0, 0, tiled=True)  51.5 us
    all_to_all x2, blocking collectives, scatter_sum(): lax.all_to_all(value, axis, 0, 0, tiled=True).astype(jnp.float32)  32.1 us
    all_to_all x1, blocking collectives, body(): lax.all_to_all(spread, 'z', 0, 0, tiled=True).astype(jnp.float32)  24.3 us
    ppermute x3, starting transfers between devices, swap_cores(): return lax.ppermute(value, 'c', [(0, 1), (1, 0)])  18.9 us
    all_gather x1, blocking collectives, body(): project = lax.all_gather(project, 'x', axis=0, tiled=True)  12.9 us
    all_gather x1, blocking collectives, body(): q_own = lax.all_gather(q_own, 'x', axis=0, tiled=True)  11.3 us
    pallas_call x1, Pallas kernels, orthonormal(): pl.pallas_call(orthonormal_kernel, in_specs=[pl.BlockSpec(memory_space=pl...  7.72 us
    all_to_all x1, starting transfers between devices, body(): squares = lax.all_to_all(spread, ('c', 'x', 'z'), 0, 0, tiled=True)  7.51 us
  transfers between devices with their start and end apart: 4, of which 2 were waited for; matrix products, arithmetic and copies ran while one was open for 0% of the time, Pallas kernels for 0%

profile of v4, /device:TPU:1, one launch (start us, length us, event | category | flops | bytes accessed | tf_op | source)
XLA Modules:
  0.0 176.6 jit_solution(4669342025301064711)
XLA Ops:
  0.6 0.0 copy-start
  0.6 1.7 add_convert_fusion.blended_ref
  2.3 8.8 %collective-permute-start = (bf16[128,3584]{1,0:T(8,128)(2,1)S(1)}, bf16[128,3584]{1,0:T(8,128)(2,1)S(1)}, u32[]{:S(2)}, u32[]{:S(2)}) collective-permute-start(bf16[128,3584]{1,0:T(8,128)(2,1)S(1)} %add_convert_fusion.blended_ref), channel_id=1, source_target_pairs={{0,8},{8,0},{1,9},{9,1},{2,10},{10,2},{3,11},{11,3},{4,12},{12,4},... | collective-permute-start | bytes 2752520 | tf_op jit(solution)/shard_map/ppermute | solution.py:22
  11.1 0.0 copy-done
  11.1 0.1 broadcast_in_dim.8
  11.2 14.1 %all_to_all.40 = bf16[8,4,3584]{2,1,0:T(4,128)(2,1)S(1)} all-to-all(bf16[8,4,3584]{2,1,0:T(4,128)(2,1)S(1)} %broadcast_in_dim.8), channel_id=1, replica_groups=mesh['y'=8,'x'=4,'c'=2,'z'=8] {'y'}, dimensions={0} | all-to-all | bytes 458752 | tf_op jit(solution)/shard_map/all_to_all | solution.py:27
  25.3 0.1 reshape.41
  25.3 0.0 collective-permute-done.other_ref
  25.4 11.3 %all_gather.6.q_ref = bf16[128,3584]{1,0:T(8,128)(2,1)S(1)} all-gather(bf16[32,3584]{1,0:T(8,128)(2,1)S(1)} %reshape.41), channel_id=1, replica_groups=mesh['y'=8,'x'=4,'c'=2,'z'=8] {'x'}, dimensions={0}, use_global_device_ids=true | all-gather | bytes 1146880 | tf_op jit(solution)/shard_map/all_gather | solution.py:365
  36.7 0.6 power.1
  37.3 24.3 %all_to_all.41 = bf16[8,128,256]{2,1,0:T(8,128)(2,1)S(1)} all-to-all(bf16[8,128,256]{2,1,0:T(8,128)(2,1)S(1)} %power.1), channel_id=1, replica_groups=mesh['y'=8,'x'=4,'c'=2,'z'=8] {'z'}, dimensions={0} | all-to-all | bytes 1048576 | tf_op jit(solution)/shard_map/all_to_all | solution.py:377
  61.6 0.1 convert_reduce_fusion.own_ref
  61.7 5.9 %collective-permute-start.1 = (f32[128,256]{1,0:T(8,128)S(1)}, f32[128,256]{1,0:T(8,128)S(1)}, u32[]{:S(2)}, u32[]{:S(2)}) collective-permute-start(f32[128,256]{1,0:T(8,128)S(1)} %convert_reduce_fusion.own_ref), channel_id=1, source_target_pairs={{0,8},{8,0},{1,9},{9,1},{2,10},{10,2},{3,11},{11,3},{4,12},{12,4},... | collective-permute-start | bytes 393224 | tf_op jit(solution)/shard_map/ppermute | solution.py:22
  67.6 1.0 collective-permute-done.1.other_ref
  68.6 1.1 gram_pieces.1
  69.7 7.2 %all_to_all.42 = f32[4,48,128]{2,1,0:T(8,128)S(1)} all-to-all(f32[4,48,128]{2,1,0:T(8,128)S(1)} %get-tuple-element.15), channel_id=1, replica_groups=mesh['y'=8,'x'=4,'c'=2,'z'=8] {'x'}, dimensions={0} | all-to-all | bytes 196608 | tf_op jit(solution)/shard_map/all_to_all | solution.py:31
  76.9 11.1 %all_to_all.43 = f32[8,48,128]{2,1,0:T(8,128)S(1)} all-to-all(f32[8,48,128]{2,1,0:T(8,128)S(1)} %broadcast_in_dim.9), channel_id=1, replica_groups=mesh['y'=8,'x'=4,'c'=2,'z'=8] {'y'}, dimensions={0} | all-to-all | bytes 393216 | tf_op jit(solution)/shard_map/all_to_all | solution.py:27
  88.1 11.1 %all_to_all.44 = f32[8,48,128]{2,1,0:T(8,128)S(1)} all-to-all(f32[8,48,128]{2,1,0:T(8,128)S(1)} %broadcast_in_dim.10), channel_id=1, replica_groups=mesh['y'=8,'x'=4,'c'=2,'z'=8] {'x','c'}, dimensions={0} | all-to-all | bytes 393216 | tf_op jit(solution)/shard_map/all_to_all | solution.py:27
  99.2 7.7 %orthonormal.1 = (bf16[256,256]{1,0:T(8,128)(2,1)S(1)}, bf16[2,128,1792]{2,1,0:T(8,128)(2,1)S(1)}) custom-call(s32[1]{0:T(128)} %bitcast.core_ref, f32[384,128]{1,0:T(8,128)S(1)} %bitcast.12, f32[256,256]{1,0:T(8,128)S(1)} %get-tuple-element.16.power_ref, bf16[128,3584]{1,0:T(8,128)(2,1)S(1)} %add_convert_fusion.blended_ref, ...), custom_call_target="tpu_custom_call" | custom-call | flops 1000000000 | bytes 1000000 | tf_op jit(solution)/shard_map/orthonormal/pallas_call | solution.py:179
  106.9 25.0 %all_to_all.45 = bf16[32,8,1792]{2,1,0:T(8,128)(2,1)S(1)} all-to-all(bf16[32,8,1792]{2,1,0:T(8,128)(2,1)S(1)} %bitcast.11), channel_id=1, replica_groups=mesh['y'=8,'x'=4,'c'=2,'z'=8] {'x','y'}, dimensions={0} | all-to-all | bytes 1835008 | tf_op jit(solution)/shard_map/all_to_all | solution.py:31
  131.9 0.1 reduce_sum.51
  132.0 15.2 %all_to_all.46 = bf16[8,8,1792]{2,1,0:T(8,128)(2,1)S(1)} all-to-all(bf16[8,8,1792]{2,1,0:T(8,128)(2,1)S(1)} %broadcast_in_dim.11), channel_id=1, replica_groups=mesh['y'=8,'x'=4,'c'=2,'z'=8] {'y'}, dimensions={0} | all-to-all | bytes 458752 | tf_op jit(solution)/shard_map/all_to_all | solution.py:27
  147.3 0.8 squares.1
  148.1 7.5 %all-to-all-start.7 = ((f32[64,1,64]{2,1,0:T(1,128)}), f32[64,1,64]{2,1,0:T(1,128)S(1)}, u32[]{:S(2)}, u32[]{:S(2)}) async-start(f32[64,1,64]{2,1,0:T(1,128)} %squares.1), calls=%async_computation.7 | async-start | bytes 65536 | tf_op jit(solution)/shard_map/all_to_all | solution.py:393
  155.6 12.9 %all_gather.7 = bf16[256,1792]{1,0:T(8,128)(2,1)S(1)} all-gather(bf16[64,1792]{1,0:T(8,128)(2,1)S(1)} %bitcast.10), channel_id=1, replica_groups=mesh['y'=8,'x'=4,'c'=2,'z'=8] {'x'}, dimensions={0}, use_global_device_ids=true | all-gather | bytes 1146880 | tf_op jit(solution)/shard_map/all_gather | solution.py:395
  168.4 0.0 all-to-all-done.7
  168.5 0.1 reshape.46.squares_ref
  168.6 4.2 %collective-permute-start.2 = (bf16[2,128,1792]{2,1,0:T(8,128)(2,1)S(1)}, bf16[2,128,1792]{2,1,0:T(8,128)(2,1)S(1)}, u32[]{:S(2)}, u32[]{:S(2)}) collective-permute-start(bf16[2,128,1792]{2,1,0:T(8,128)(2,1)S(1)} %bitcast.7), channel_id=1, source_target_pairs={{0,8},{8,0},{1,9},{9,1},{2,10},{10,2},{3,11},{11,3},{4,12},{12,4},... | collective-permute-start | bytes 2752520 | tf_op jit(solution)/shard_map/ppermute | solution.py:22
  172.7 0.1 prepare.1
  172.8 1.9 %collective-permute-done.2.other_ref = bf16[2,128,1792]{2,1,0:T(8,128)(2,1)S(1)} collective-permute-done((bf16[2,128,1792]{2,1,0:T(8,128)(2,1)S(1)}, bf16[2,128,1792]{2,1,0:T(8,128)(2,1)S(1)}, u32[]{:S(2)}, u32[]{:S(2)}) %collective-permute-start.2) | collective-permute-done | bytes 917536 | tf_op jit(solution)/shard_map/ppermute | solution.py:22
  174.8 1.8 %finish.1 = (bf16[128,3584]{1,0:T(8,128)(2,1)}, bf16[128,3584]{1,0:T(8,128)(2,1)}, bf16[4,3584]{1,0:T(4,128)(2,1)}) custom-call(bf16[256,256]{1,0:T(8,128)(2,1)S(1)} %get-tuple-element.20.left_ref, f32[8,256]{1,0:T(8,128)S(1)} %get-tuple-element.21.pick_ref, bf16[2,128,1792]{2,1,0:T(8,128)(2,1)S(1)} %bitcast.8, ...), custom_call_target="tpu_custom_call" | custom-call | flops 469762048 | bytes 1000000 | tf_op jit(solution)/shard_map/finish/pallas_call | solution.py:36
  (6 shorter events, 0.1 us)
Async XLA Ops:
  0.6 10.5 %copy-start = (bf16[4,3584]{1,0:T(4,128)(2,1)S(1)}, bf16[4,3584]{1,0:T(4,128)(2,1)}, u32[]{:S(2)}) copy-start(bf16[4,3584]{1,0:T(4,128)(2,1)} %param.5) | copy-start | bytes 86020
  2.3 23.0 %collective-permute-start = (bf16[128,3584]{1,0:T(8,128)(2,1)S(1)}, bf16[128,3584]{1,0:T(8,128)(2,1)S(1)}, u32[]{:S(2)}, u32[]{:S(2)}) collective-permute-start(bf16[128,3584]{1,0:T(8,128)(2,1)S(1)} %add_convert_fusion.blended_ref), channel_id=1, source_target_pairs={{0,8},{8,0},{1,9},{9,1},{2,10},{10,2},{3,11},{11,3},{4,12},{12,4},... | collective-permute-start | bytes 2752520 | tf_op jit(solution)/shard_map/ppermute | solution.py:22
  61.7 6.9 %collective-permute-start.1 = (f32[128,256]{1,0:T(8,128)S(1)}, f32[128,256]{1,0:T(8,128)S(1)}, u32[]{:S(2)}, u32[]{:S(2)}) collective-permute-start(f32[128,256]{1,0:T(8,128)S(1)} %convert_reduce_fusion.own_ref), channel_id=1, source_target_pairs={{0,8},{8,0},{1,9},{9,1},{2,10},{10,2},{3,11},{11,3},{4,12},{12,4},... | collective-permute-start | bytes 393224 | tf_op jit(solution)/shard_map/ppermute | solution.py:22
  148.1 20.4 %all-to-all-start.7 = ((f32[64,1,64]{2,1,0:T(1,128)}), f32[64,1,64]{2,1,0:T(1,128)S(1)}, u32[]{:S(2)}, u32[]{:S(2)}) async-start(f32[64,1,64]{2,1,0:T(1,128)} %squares.1), calls=%async_computation.7 | async-start | bytes 65536 | tf_op jit(solution)/shard_map/all_to_all | solution.py:393
  168.6 6.2 %collective-permute-start.2 = (bf16[2,128,1792]{2,1,0:T(8,128)(2,1)S(1)}, bf16[2,128,1792]{2,1,0:T(8,128)(2,1)S(1)}, u32[]{:S(2)}, u32[]{:S(2)}) collective-permute-start(bf16[2,128,1792]{2,1,0:T(8,128)(2,1)S(1)} %bitcast.7), channel_id=1, source_target_pairs={{0,8},{8,0},{1,9},{9,1},{2,10},{10,2},{3,11},{11,3},{4,12},{12,4},... | collective-permute-start | bytes 2752520 | tf_op jit(solution)/shard_map/ppermute | solution.py:22

commit v5 on v4

--- a/solution.py
+++ b/solution.py
@@ -132,6 +132,16 @@
                 tiles[top + level, t] = tiles[top + level, t] * scale
 
 
+def own_ranks(core, height):
+    j = lax.broadcasted_iota(jnp.int32, (height, RANK), 0)
+    source = lax.broadcasted_iota(jnp.int32, (height, RANK), 1)
+    size = RANK // (NY * NX * NC)
+    c = jnp.where(j < RANK // NC, core, 1 - core)
+    j = j & (RANK // NC - 1)
+    low = j & (size - 1)
+    return ((j - low) * NC + c * size + low == source).astype(jnp.bfloat16)
+
+
 def orthonormal_kernel(
     core_ref, gram_ref, power_ref, blended_ref, other_ref, basis_ref, terms_ref, work_ref
 ):
@@ -162,8 +172,9 @@
             )
             work_ref[below:, start:] = work_ref[below:, start:] - product[below - start :]
     basis_ref[...] = work_ref[:, RANK:].astype(basis_ref.dtype)
-    half = RANK // NC
-    mine = jnp.where(core_ref[0] == 0, work_ref[:half, RANK:], work_ref[half:, RANK:])
+    mine = jnp.dot(
+        own_ranks(core_ref[0], RANK // NC), basis_ref[...], preferred_element_type=jnp.float32
+    )
     mine = mine.astype(jnp.bfloat16)
     width = terms_ref.shape[2] // 2
     for j in range(4):
@@ -249,50 +260,47 @@
     )(core.reshape(1), own, other)
 
 
-def prepare_kernel(core_ref, place_ref, squares_ref, basis_ref, left_ref, pick_ref):
-    swap = core_ref[0] != 0
+def prepare_kernel(core_ref, place_ref, squares_ref, basis_ref, own_ref, left_ref, q_ref):
     rows = left_ref.shape[0] // 2
-
-    def own_half_first(value):
-        first, second = jnp.split(value, 2, 1)
-        turned = jnp.concatenate([second, first], axis=1)
-        return jnp.where(swap, turned, value)
-
-    inverse = own_half_first(1.0 / jnp.sqrt(squares_ref[...] + 1e-06))
-    basis = own_half_first(basis_ref[:, :rows].astype(jnp.float32).T)
+    half = RANK // NC
+    inverse = 1.0 / jnp.sqrt(squares_ref[...] + 1e-06)
+    turned = jnp.concatenate([inverse[:, half:], inverse[:, :half]], axis=1)
+    inverse = jnp.where(core_ref[0] == 0, inverse, turned)
+    basis = jnp.dot(
+        own_ranks(core_ref[0], RANK), basis_ref[:, :rows], preferred_element_type=jnp.float32
+    ).T
     left_ref[:rows] = basis.astype(jnp.bfloat16)
     left_ref[rows:] = (basis * inverse).astype(jnp.bfloat16)
-    rank = lax.broadcasted_iota(jnp.int32, pick_ref.shape, 1)
-    wanted = place_ref[0] + lax.broadcasted_iota(jnp.int32, pick_ref.shape, 0)
-    pick_ref[...] = jnp.where(rank == wanted, inverse, 0.0)
+    rank = lax.broadcasted_iota(jnp.int32, (SUB, half), 1)
+    chosen = rank == place_ref[0] + lax.broadcasted_iota(jnp.int32, (SUB, half), 0)
+    scale = jnp.sum(jnp.where(chosen, inverse[:, :half], 0.0), axis=1, keepdims=True)
+    chosen = jnp.where(chosen, 1.0, 0.0).astype(jnp.bfloat16)
+    width = own_ref.shape[2]
+    for side in range(2):
+        picked = jnp.dot(chosen, own_ref[side], preferred_element_type=jnp.float32) * scale
+        columns = slice(side * width, (side + 1) * width)
+        q_ref[:, columns] = picked[: q_ref.shape[0]].astype(jnp.bfloat16)
 
 
 def finish_kernel(
     left_ref,
-    pick_ref,
     own_ref,
     other_ref,
     blended_ref,
     momentum_hbm,
     update_hbm,
-    q_hbm,
     momentum_ref,
     update_ref,
-    q_ref,
     sems,
-    q_sem,
 ):
     rows, cols = blended_ref.shape
-    pick = pick_ref[...]
-    scale = jnp.sum(pick, axis=1, keepdims=True)
-    chosen = jnp.where(pick != 0.0, 1.0, 0.0).astype(jnp.bfloat16)
     blocks = sems.shape[1]
     width = cols // blocks
     copies = []
     for j in range(blocks):
         columns = slice(j * width, (j + 1) * width)
-        side, j = divmod(j, blocks // 2)
-        there = slice(j * width, (j + 1) * width)
+        side, k = divmod(j, blocks // 2)
+        there = slice(k * width, (k + 1) * width)
         project = [ref[side, :, there] for ref in (own_ref, other_ref)]
         project = jnp.concatenate(project, axis=0)
         both = jnp.dot(left_ref[...], project, preferred_element_type=jnp.float32)
@@ -304,17 +312,10 @@
             ((momentum_ref, momentum_hbm), (update_ref, update_hbm))
         ):
             copy = pltpu.make_async_copy(
-                source.at[:, columns],
-                target.at[:, columns],
-                sems.at[n, side * (blocks // 2) + j],
+                source.at[:, columns], target.at[:, columns], sems.at[n, j]
             )
             copy.start()
             copies.append(copy)
-        picked = jnp.dot(chosen, project, preferred_element_type=jnp.float32) * scale
-        q_ref[:, columns] = picked[: q_ref.shape[0]].astype(jnp.bfloat16)
-    copy = pltpu.make_async_copy(q_ref, q_hbm, q_sem)
-    copy.start()
-    copies.append(copy)
     for copy in copies:
         copy.wait()
 
@@ -322,36 +323,31 @@
 def finish(core, place, squares, basis_t, own, other, blended, rank_dev):
     rows, cols = blended.shape
     whole = ((rows, cols), jnp.bfloat16)
-    left, pick = in_vmem(
+    left, q_next = in_vmem(
         prepare_kernel,
         "prepare",
         10**5,
-        [((2 * rows, RANK), jnp.bfloat16), ((SUB, RANK), jnp.float32)],
+        [((2 * rows, RANK), jnp.bfloat16), ((rank_dev, cols), jnp.bfloat16)],
         core.reshape(1),
         place.reshape(1),
         squares,
         basis_t,
+        own,
         scalars=2,
     )
-    return in_vmem(
+    momentum_next, update = in_vmem(
         finish_kernel,
         "finish",
         4 * rows * RANK * cols,
-        [whole, whole, ((rank_dev, cols), jnp.bfloat16)],
+        [whole, whole],
         left,
-        pick,
         own,
         other,
         blended,
-        scratch=[
-            pltpu.VMEM(*whole),
-            pltpu.VMEM(*whole),
-            pltpu.VMEM((rank_dev, cols), jnp.bfloat16),
-            pltpu.SemaphoreType.DMA((2, BLOCKS)),
-            pltpu.SemaphoreType.DMA,
-        ],
-        hbm_outs=3,
-    )
+        scratch=[pltpu.VMEM(*whole), pltpu.VMEM(*whole), pltpu.SemaphoreType.DMA((2, BLOCKS))],
+        hbm_outs=2,
+    )
+    return momentum_next, update, q_next
 
 
 def body(gradient, momentum, q_basis):
@@ -379,8 +375,9 @@
     power_t, pieces = gram_pieces(core, power_own, swap_cores(power_own))
     basis_t, terms = orthonormal(core, gram_sum(pieces), power_t, blended, other)
 
-    terms = terms.reshape(NX * NY, SUB, cols // 2)
-    project = scatter_sum(terms, ("x", "y")).astype(jnp.bfloat16)
+    terms = terms.reshape(NX, NY * SUB, cols // 2)
+    project = scatter_sum(terms, "x").astype(jnp.bfloat16).reshape(NY, SUB, cols // 2)
+    project = scatter_sum(project, "y").astype(jnp.bfloat16)
     project = gather(project, "y", NY).reshape(NY * SUB, cols // 2)
     peers = NC * NX * NZ
     (spread,) = in_vmem(
@@ -395,7 +392,7 @@
     project = lax.all_gather(project, "x", axis=0, tiled=True)
     project, squares = lax.optimization_barrier((project, squares))
     project = project.reshape(2, half, cols // 2)
-    place = (((y * NX + x) * NC + core) * rank_dev + RANK - half * core) % RANK
+    place = (y * NX + x) * rank_dev
     return finish(
         core, place, squares, basis_t, project, swap_cores(project), blended, rank_dev
     )

time: 177 us -> 176 us (level)
  blocking collectives: 132 us -> 130 us
    all_to_all x4, blocking collectives: 51.5 us -> 47.9 us  [gather(): return lax.all_to_all(spread, axis, 0, 0, tiled=True)]
    all_to_all x2 -> x3, blocking collectives: 32.1 us -> 33.7 us  [scatter_sum(): lax.all_to_all(value, axis, 0, 0, tiled=True).astype(jnp.float32)]
  transfers between devices with their start and end apart: 4 -> 4, of which waited for: 2 -> 2; matrix products, arithmetic and copies ran while one was open for 0% -> 0% of each run, Pallas kernels for 0% -> 1%
where the time goes in v5:
time: 176 us
  blocking collectives  130 us (74%)
  starting transfers between devices  27.4 us (16%)
  Pallas kernels  13 us (7%)
  waiting for transfers between devices  2.14 us (1%)
  other arithmetic  1.98 us (1%)
    all_to_all x4, blocking collectives, gather(): return lax.all_to_all(spread, axis, 0, 0, tiled=True)  47.9 us
    all_to_all x3, blocking collectives, scatter_sum(): lax.all_to_all(value, axis, 0, 0, tiled=True).astype(jnp.float32)  33.7 us
    all_to_all x1, blocking collectives, body(): lax.all_to_all(spread, 'z', 0, 0, tiled=True).astype(jnp.float32)  24.3 us
    ppermute x3, starting transfers between devices, swap_cores(): return lax.ppermute(value, 'c', [(0, 1), (1, 0)])  18.9 us
    all_gather x1, blocking collectives, body(): project = lax.all_gather(project, 'x', axis=0, tiled=True)  12.9 us
    all_gather x1, blocking collectives, body(): q_own = lax.all_gather(q_own, 'x', axis=0, tiled=True)  11.3 us
    all_to_all x1, starting transfers between devices, body(): squares = lax.all_to_all(spread, ('c', 'x', 'z'), 0, 0, tiled=True)  8.53 us
    pallas_call x1, Pallas kernels, orthonormal(): pl.pallas_call(orthonormal_kernel, in_specs=[pl.BlockSpec(memory_space=pl...  7.88 us
  transfers between devices with their start and end apart: 4, of which 2 were waited for; matrix products, arithmetic and copies ran while one was open for 0% of the time, Pallas kernels for 1%

profile of v5, /device:TPU:1, one launch (start us, length us, event | category | flops | bytes accessed | tf_op | source)
XLA Modules:
  0.0 175.5 jit_solution(15387880206356522903)
XLA Ops:
  0.6 0.0 copy-start
  0.6 1.7 add_convert_fusion.blended_ref
  2.3 8.8 %collective-permute-start = (bf16[128,3584]{1,0:T(8,128)(2,1)S(1)}, bf16[128,3584]{1,0:T(8,128)(2,1)S(1)}, u32[]{:S(2)}, u32[]{:S(2)}) collective-permute-start(bf16[128,3584]{1,0:T(8,128)(2,1)S(1)} %add_convert_fusion.blended_ref), channel_id=1, source_target_pairs={{0,8},{8,0},{1,9},{9,1},{2,10},{10,2},{3,11},{11,3},{4,12},{12,4},... | collective-permute-start | bytes 2752520 | tf_op jit(solution)/shard_map/ppermute | solution.py:22
  11.1 0.0 copy-done
  11.1 0.1 broadcast_in_dim.8
  11.2 14.1 %all_to_all.45 = bf16[8,4,3584]{2,1,0:T(4,128)(2,1)S(1)} all-to-all(bf16[8,4,3584]{2,1,0:T(4,128)(2,1)S(1)} %broadcast_in_dim.8), channel_id=1, replica_groups=mesh['y'=8,'x'=4,'c'=2,'z'=8] {'y'}, dimensions={0} | all-to-all | bytes 458752 | tf_op jit(solution)/shard_map/all_to_all | solution.py:27
  25.3 0.1 reshape.44
  25.3 0.0 collective-permute-done.other_ref
  25.4 11.3 %all_gather.6.q_ref = bf16[128,3584]{1,0:T(8,128)(2,1)S(1)} all-gather(bf16[32,3584]{1,0:T(8,128)(2,1)S(1)} %reshape.44), channel_id=1, replica_groups=mesh['y'=8,'x'=4,'c'=2,'z'=8] {'x'}, dimensions={0}, use_global_device_ids=true | all-gather | bytes 1146880 | tf_op jit(solution)/shard_map/all_gather | solution.py:361
  36.7 0.6 power.1
  37.3 24.3 %all_to_all.46 = bf16[8,128,256]{2,1,0:T(8,128)(2,1)S(1)} all-to-all(bf16[8,128,256]{2,1,0:T(8,128)(2,1)S(1)} %power.1), channel_id=1, replica_groups=mesh['y'=8,'x'=4,'c'=2,'z'=8] {'z'}, dimensions={0} | all-to-all | bytes 1048576 | tf_op jit(solution)/shard_map/all_to_all | solution.py:373
  61.6 0.1 convert_reduce_fusion.own_ref
  61.7 5.9 %collective-permute-start.1 = (f32[128,256]{1,0:T(8,128)S(1)}, f32[128,256]{1,0:T(8,128)S(1)}, u32[]{:S(2)}, u32[]{:S(2)}) collective-permute-start(f32[128,256]{1,0:T(8,128)S(1)} %convert_reduce_fusion.own_ref), channel_id=1, source_target_pairs={{0,8},{8,0},{1,9},{9,1},{2,10},{10,2},{3,11},{11,3},{4,12},{12,4},... | collective-permute-start | bytes 393224 | tf_op jit(solution)/shard_map/ppermute | solution.py:22
  67.6 1.0 collective-permute-done.1.other_ref
  68.6 1.1 gram_pieces.1
  69.7 7.2 %all_to_all.47 = f32[4,48,128]{2,1,0:T(8,128)S(1)} all-to-all(f32[4,48,128]{2,1,0:T(8,128)S(1)} %get-tuple-element.17), channel_id=1, replica_groups=mesh['y'=8,'x'=4,'c'=2,'z'=8] {'x'}, dimensions={0} | all-to-all | bytes 196608 | tf_op jit(solution)/shard_map/all_to_all | solution.py:31
  76.9 11.1 %all_to_all.48 = f32[8,48,128]{2,1,0:T(8,128)S(1)} all-to-all(f32[8,48,128]{2,1,0:T(8,128)S(1)} %broadcast_in_dim.9), channel_id=1, replica_groups=mesh['y'=8,'x'=4,'c'=2,'z'=8] {'y'}, dimensions={0} | all-to-all | bytes 393216 | tf_op jit(solution)/shard_map/all_to_all | solution.py:27
  88.1 11.1 %all_to_all.49 = f32[8,48,128]{2,1,0:T(8,128)S(1)} all-to-all(f32[8,48,128]{2,1,0:T(8,128)S(1)} %broadcast_in_dim.10), channel_id=1, replica_groups=mesh['y'=8,'x'=4,'c'=2,'z'=8] {'x','c'}, dimensions={0} | all-to-all | bytes 393216 | tf_op jit(solution)/shard_map/all_to_all | solution.py:27
  99.2 7.9 %orthonormal.1 = (bf16[256,256]{1,0:T(8,128)(2,1)S(1)}, bf16[2,128,1792]{2,1,0:T(8,128)(2,1)S(1)}) custom-call(s32[1]{0:T(128)} %bitcast.core_ref, f32[384,128]{1,0:T(8,128)S(1)} %bitcast.14, f32[256,256]{1,0:T(8,128)S(1)} %get-tuple-element.18.power_ref, bf16[128,3584]{1,0:T(8,128)(2,1)S(1)} %add_convert_fusion.blended_ref, ...), custom_call_target="tpu_custom_call" | custom-call | flops 1000000000 | bytes 1000000 | tf_op jit(solution)/shard_map/orthonormal/pallas_call | solution.py:190
  107.1 15.2 %all_to_all.50 = bf16[4,64,1792]{2,1,0:T(8,128)(2,1)S(1)} all-to-all(bf16[4,64,1792]{2,1,0:T(8,128)(2,1)S(1)} %bitcast.13), channel_id=1, replica_groups=mesh['y'=8,'x'=4,'c'=2,'z'=8] {'x'}, dimensions={0} | all-to-all | bytes 1835008 | tf_op jit(solution)/shard_map/all_to_all | solution.py:31
  122.3 0.2 reduce_sum.63
  122.4 11.3 %all_to_all.51 = bf16[8,8,1792]{2,1,0:T(8,128)(2,1)S(1)} all-to-all(bf16[8,8,1792]{2,1,0:T(8,128)(2,1)S(1)} %bitcast.15), channel_id=1, replica_groups=mesh['y'=8,'x'=4,'c'=2,'z'=8] {'y'}, dimensions={0} | all-to-all | bytes 458752 | tf_op jit(solution)/shard_map/all_to_all | solution.py:31
  133.8 11.5 %all_to_all.52 = bf16[8,8,1792]{2,1,0:T(8,128)(2,1)S(1)} all-to-all(bf16[8,8,1792]{2,1,0:T(8,128)(2,1)S(1)} %broadcast_in_dim.11), channel_id=1, replica_groups=mesh['y'=8,'x'=4,'c'=2,'z'=8] {'y'}, dimensions={0} | all-to-all | bytes 458752 | tf_op jit(solution)/shard_map/all_to_all | solution.py:27
  145.3 0.8 squares.1
  146.1 8.5 %all-to-all-start.8 = ((f32[64,1,64]{2,1,0:T(1,128)}), f32[64,1,64]{2,1,0:T(1,128)S(1)}, u32[]{:S(2)}, u32[]{:S(2)}) async-start(f32[64,1,64]{2,1,0:T(1,128)} %squares.1), calls=%async_computation.8 | async-start | bytes 65536 | tf_op jit(solution)/shard_map/all_to_all | solution.py:390
  154.7 12.9 %all_gather.7 = bf16[256,1792]{1,0:T(8,128)(2,1)S(1)} all-gather(bf16[64,1792]{1,0:T(8,128)(2,1)S(1)} %bitcast.12), channel_id=1, replica_groups=mesh['y'=8,'x'=4,'c'=2,'z'=8] {'x'}, dimensions={0}, use_global_device_ids=true | all-gather | bytes 1146880 | tf_op jit(solution)/shard_map/all_gather | solution.py:392
  167.5 0.0 all-to-all-done.8
  167.6 0.1 reshape.50.squares_ref
  167.6 4.2 %collective-permute-start.2 = (bf16[2,128,1792]{2,1,0:T(8,128)(2,1)S(1)}, bf16[2,128,1792]{2,1,0:T(8,128)(2,1)S(1)}, u32[]{:S(2)}, u32[]{:S(2)}) collective-permute-start(bf16[2,128,1792]{2,1,0:T(8,128)(2,1)S(1)} %bitcast.8), channel_id=1, source_target_pairs={{0,8},{8,0},{1,9},{9,1},{2,10},{10,2},{3,11},{11,3},{4,12},{12,4},... | collective-permute-start | bytes 2752520 | tf_op jit(solution)/shard_map/ppermute | solution.py:22
  171.8 0.9 prepare.1
  172.7 1.2 collective-permute-done.2.other_ref
  173.9 1.7 finish.1
  (7 shorter events, 0.1 us)
Async XLA Ops:
  0.6 10.5 %copy-start = (bf16[4,3584]{1,0:T(4,128)(2,1)S(1)}, bf16[4,3584]{1,0:T(4,128)(2,1)}, u32[]{:S(2)}) copy-start(bf16[4,3584]{1,0:T(4,128)(2,1)} %param.5) | copy-start | bytes 86020
  2.3 23.0 %collective-permute-start = (bf16[128,3584]{1,0:T(8,128)(2,1)S(1)}, bf16[128,3584]{1,0:T(8,128)(2,1)S(1)}, u32[]{:S(2)}, u32[]{:S(2)}) collective-permute-start(bf16[128,3584]{1,0:T(8,128)(2,1)S(1)} %add_convert_fusion.blended_ref), channel_id=1, source_target_pairs={{0,8},{8,0},{1,9},{9,1},{2,10},{10,2},{3,11},{11,3},{4,12},{12,4},... | collective-permute-start | bytes 2752520 | tf_op jit(solution)/shard_map/ppermute | solution.py:22
  61.7 6.9 %collective-permute-start.1 = (f32[128,256]{1,0:T(8,128)S(1)}, f32[128,256]{1,0:T(8,128)S(1)}, u32[]{:S(2)}, u32[]{:S(2)}) collective-permute-start(f32[128,256]{1,0:T(8,128)S(1)} %convert_reduce_fusion.own_ref), channel_id=1, source_target_pairs={{0,8},{8,0},{1,9},{9,1},{2,10},{10,2},{3,11},{11,3},{4,12},{12,4},... | collective-permute-start | bytes 393224 | tf_op jit(solution)/shard_map/ppermute | solution.py:22
  146.1 21.4 %all-to-all-start.8 = ((f32[64,1,64]{2,1,0:T(1,128)}), f32[64,1,64]{2,1,0:T(1,128)S(1)}, u32[]{:S(2)}, u32[]{:S(2)}) async-start(f32[64,1,64]{2,1,0:T(1,128)} %squares.1), calls=%async_computation.8 | async-start | bytes 65536 | tf_op jit(solution)/shard_map/all_to_all | solution.py:390
  167.6 6.2 %collective-permute-start.2 = (bf16[2,128,1792]{2,1,0:T(8,128)(2,1)S(1)}, bf16[2,128,1792]{2,1,0:T(8,128)(2,1)S(1)}, u32[]{:S(2)}, u32[]{:S(2)}) collective-permute-start(bf16[2,128,1792]{2,1,0:T(8,128)(2,1)S(1)} %bitcast.8), channel_id=1, source_target_pairs={{0,8},{8,0},{1,9},{9,1},{2,10},{10,2},{3,11},{11,3},{4,12},{12,4},... | collective-permute-start | bytes 2752520 | tf_op jit(solution)/shard_map/ppermute | solution.py:22

commit v6 on v5

--- a/solution.py
+++ b/solution.py
@@ -68,7 +68,7 @@
 def gram_sum(pieces):
     part = scatter_sum(pieces, "x")
     part = jnp.sum(gather(part, "y", NY), axis=0)
-    return gather(part, ("x", "c"), NX * NC).reshape(-1, part.shape[-1])
+    return gather(part, ("c", "x"), NX * NC).reshape(-1, part.shape[-1])
 
 
 SUB, LANES = 8, 128
@@ -146,9 +146,11 @@
     core_ref, gram_ref, power_ref, blended_ref, other_ref, basis_ref, terms_ref, work_ref
 ):
     last = work_ref.shape[1] // LANES
+    half, core = LANES // 2, LANES * 3 // 2
     work_ref[:LANES, :LANES] = gram_ref[:LANES]
-    work_ref[:LANES, LANES:RANK] = gram_ref[LANES:RANK]
-    work_ref[LANES:, LANES:RANK] = gram_ref[RANK:]
+    work_ref[:half, LANES:RANK] = gram_ref[LANES:core]
+    work_ref[half:LANES, LANES:RANK] = gram_ref[core + LANES :]
+    work_ref[LANES:, LANES:RANK] = gram_ref[core : core + LANES]
     work_ref[:, RANK:] = power_ref[...]
     for base in range(0, RANK, PANEL):
         first = base // LANES
@@ -226,21 +228,21 @@
         **exact,
     )
     power_ref[...] = power
+    first = core_ref[0] == 0
+    upper, lower = power[:LANES], power[LANES:]
+    own = jnp.where(first, upper, lower)
+    cross = jnp.where(first, upper[: LANES // 2], upper[LANES // 2 :])
     contract_last = (((1,), (1,)), ((), ()))
-    upper, lower = power[:LANES], power[LANES:]
     gram = jnp.concatenate(
         [
-            lax.dot_general(upper, upper, contract_last, **exact),
-            lax.dot_general(upper, lower, contract_last, **exact),
-            lax.dot_general(lower, lower, contract_last, **exact),
+            lax.dot_general(own, own, contract_last, **exact),
+            lax.dot_general(cross, lower, contract_last, **exact),
         ],
         axis=0,
     )
     height = gram_ref.shape[1]
     for x in range(NX):
-        even = gram[2 * x * height : (2 * x + 1) * height]
-        odd = gram[(2 * x + 1) * height : (2 * x + 2) * height]
-        gram_ref[x] = jnp.where(core_ref[0] == 0, even, odd)
+        gram_ref[x] = gram[x * height : (x + 1) * height]
 
 
 def gram_pieces(core, own, other):

time: 176 us -> 176 us (level)
  no operation moved by 1% of the time
where the time goes in v6:
time: 176 us
  blocking collectives  130 us (74%)
  starting transfers between devices  27.4 us (16%)
  Pallas kernels  13 us (7%)
  waiting for transfers between devices  2.14 us (1%)
  other arithmetic  1.98 us (1%)
    all_to_all x4, blocking collectives, gather(): return lax.all_to_all(spread, axis, 0, 0, tiled=True)  47.9 us
    all_to_all x3, blocking collectives, scatter_sum(): lax.all_to_all(value, axis, 0, 0, tiled=True).astype(jnp.float32)  33.6 us
    all_to_all x1, blocking collectives, body(): lax.all_to_all(spread, 'z', 0, 0, tiled=True).astype(jnp.float32)  24.3 us
    ppermute x3, starting transfers between devices, swap_cores(): return lax.ppermute(value, 'c', [(0, 1), (1, 0)])  18.9 us
    all_gather x1, blocking collectives, body(): project = lax.all_gather(project, 'x', axis=0, tiled=True)  12.9 us
    all_gather x1, blocking collectives, body(): q_own = lax.all_gather(q_own, 'x', axis=0, tiled=True)  11.3 us
    all_to_all x1, starting transfers between devices, body(): squares = lax.all_to_all(spread, ('c', 'x', 'z'), 0, 0, tiled=True)  8.51 us
    pallas_call x1, Pallas kernels, orthonormal(): pl.pallas_call(orthonormal_kernel, in_specs=[pl.BlockSpec(memory_space=pl...  7.88 us
  transfers between devices with their start and end apart: 4, of which 2 were waited for; matrix products, arithmetic and copies ran while one was open for 0% of the time, Pallas kernels for 1%

profile of v6, /device:TPU:1, one launch (start us, length us, event | category | flops | bytes accessed | tf_op | source)
XLA Modules:
  0.0 175.5 jit_solution(6187606027231843488)
XLA Ops:
  0.6 0.0 copy-start
  0.6 1.7 add_convert_fusion.blended_ref
  2.3 8.8 %collective-permute-start = (bf16[128,3584]{1,0:T(8,128)(2,1)S(1)}, bf16[128,3584]{1,0:T(8,128)(2,1)S(1)}, u32[]{:S(2)}, u32[]{:S(2)}) collective-permute-start(bf16[128,3584]{1,0:T(8,128)(2,1)S(1)} %add_convert_fusion.blended_ref), channel_id=1, source_target_pairs={{0,8},{8,0},{1,9},{9,1},{2,10},{10,2},{3,11},{11,3},{4,12},{12,4},... | collective-permute-start | bytes 2752520 | tf_op jit(solution)/shard_map/ppermute | solution.py:22
  11.1 0.0 copy-done
  11.1 0.1 broadcast_in_dim.8
  11.2 14.1 %all_to_all.45 = bf16[8,4,3584]{2,1,0:T(4,128)(2,1)S(1)} all-to-all(bf16[8,4,3584]{2,1,0:T(4,128)(2,1)S(1)} %broadcast_in_dim.8), channel_id=1, replica_groups=mesh['y'=8,'x'=4,'c'=2,'z'=8] {'y'}, dimensions={0} | all-to-all | bytes 458752 | tf_op jit(solution)/shard_map/all_to_all | solution.py:27
  25.3 0.1 reshape.44
  25.3 0.0 collective-permute-done.other_ref
  25.4 11.3 %all_gather.6.q_ref = bf16[128,3584]{1,0:T(8,128)(2,1)S(1)} all-gather(bf16[32,3584]{1,0:T(8,128)(2,1)S(1)} %reshape.44), channel_id=1, replica_groups=mesh['y'=8,'x'=4,'c'=2,'z'=8] {'x'}, dimensions={0}, use_global_device_ids=true | all-gather | bytes 1146880 | tf_op jit(solution)/shard_map/all_gather | solution.py:363
  36.7 0.6 power.1
  37.3 24.3 %all_to_all.46 = bf16[8,128,256]{2,1,0:T(8,128)(2,1)S(1)} all-to-all(bf16[8,128,256]{2,1,0:T(8,128)(2,1)S(1)} %power.1), channel_id=1, replica_groups=mesh['y'=8,'x'=4,'c'=2,'z'=8] {'z'}, dimensions={0} | all-to-all | bytes 1048576 | tf_op jit(solution)/shard_map/all_to_all | solution.py:375
  61.6 0.1 convert_reduce_fusion.own_ref
  61.7 5.9 %collective-permute-start.1 = (f32[128,256]{1,0:T(8,128)S(1)}, f32[128,256]{1,0:T(8,128)S(1)}, u32[]{:S(2)}, u32[]{:S(2)}) collective-permute-start(f32[128,256]{1,0:T(8,128)S(1)} %convert_reduce_fusion.own_ref), channel_id=1, source_target_pairs={{0,8},{8,0},{1,9},{9,1},{2,10},{10,2},{3,11},{11,3},{4,12},{12,4},... | collective-permute-start | bytes 393224 | tf_op jit(solution)/shard_map/ppermute | solution.py:22
  67.6 1.0 collective-permute-done.1.other_ref
  68.6 1.2 gram_pieces.1
  69.7 7.2 %all_to_all.47 = f32[4,48,128]{2,1,0:T(8,128)S(1)} all-to-all(f32[4,48,128]{2,1,0:T(8,128)S(1)} %get-tuple-element.17), channel_id=1, replica_groups=mesh['y'=8,'x'=4,'c'=2,'z'=8] {'x'}, dimensions={0} | all-to-all | bytes 196608 | tf_op jit(solution)/shard_map/all_to_all | solution.py:31
  77.0 11.1 %all_to_all.48 = f32[8,48,128]{2,1,0:T(8,128)S(1)} all-to-all(f32[8,48,128]{2,1,0:T(8,128)S(1)} %broadcast_in_dim.9), channel_id=1, replica_groups=mesh['y'=8,'x'=4,'c'=2,'z'=8] {'y'}, dimensions={0} | all-to-all | bytes 393216 | tf_op jit(solution)/shard_map/all_to_all | solution.py:27
  88.1 11.1 %all_to_all.49 = f32[8,48,128]{2,1,0:T(8,128)S(1)} all-to-all(f32[8,48,128]{2,1,0:T(8,128)S(1)} %broadcast_in_dim.10), channel_id=1, replica_groups=mesh['y'=8,'x'=4,'c'=2,'z'=8] {'c','x'}, dimensions={0} | all-to-all | bytes 393216 | tf_op jit(solution)/shard_map/all_to_all | solution.py:27
  99.3 7.9 %orthonormal.1 = (bf16[256,256]{1,0:T(8,128)(2,1)S(1)}, bf16[2,128,1792]{2,1,0:T(8,128)(2,1)S(1)}) custom-call(s32[1]{0:T(128)} %bitcast.core_ref, f32[384,128]{1,0:T(8,128)S(1)} %bitcast.14, f32[256,256]{1,0:T(8,128)S(1)} %get-tuple-element.18.power_ref, bf16[128,3584]{1,0:T(8,128)(2,1)S(1)} %add_convert_fusion.blended_ref, ...), custom_call_target="tpu_custom_call" | custom-call | flops 1000000000 | bytes 1000000 | tf_op jit(solution)/shard_map/orthonormal/pallas_call | solution.py:192
  107.1 15.1 %all_to_all.50 = bf16[4,64,1792]{2,1,0:T(8,128)(2,1)S(1)} all-to-all(bf16[4,64,1792]{2,1,0:T(8,128)(2,1)S(1)} %bitcast.13), channel_id=1, replica_groups=mesh['y'=8,'x'=4,'c'=2,'z'=8] {'x'}, dimensions={0} | all-to-all | bytes 1835008 | tf_op jit(solution)/shard_map/all_to_all | solution.py:31
  122.3 0.2 reduce_sum.63
  122.4 11.3 %all_to_all.51 = bf16[8,8,1792]{2,1,0:T(8,128)(2,1)S(1)} all-to-all(bf16[8,8,1792]{2,1,0:T(8,128)(2,1)S(1)} %bitcast.15), channel_id=1, replica_groups=mesh['y'=8,'x'=4,'c'=2,'z'=8] {'y'}, dimensions={0} | all-to-all | bytes 458752 | tf_op jit(solution)/shard_map/all_to_all | solution.py:31
  133.8 11.5 %all_to_all.52 = bf16[8,8,1792]{2,1,0:T(8,128)(2,1)S(1)} all-to-all(bf16[8,8,1792]{2,1,0:T(8,128)(2,1)S(1)} %broadcast_in_dim.11), channel_id=1, replica_groups=mesh['y'=8,'x'=4,'c'=2,'z'=8] {'y'}, dimensions={0} | all-to-all | bytes 458752 | tf_op jit(solution)/shard_map/all_to_all | solution.py:27
  145.3 0.8 squares.1
  146.1 8.5 %all-to-all-start.8 = ((f32[64,1,64]{2,1,0:T(1,128)}), f32[64,1,64]{2,1,0:T(1,128)S(1)}, u32[]{:S(2)}, u32[]{:S(2)}) async-start(f32[64,1,64]{2,1,0:T(1,128)} %squares.1), calls=%async_computation.8 | async-start | bytes 65536 | tf_op jit(solution)/shard_map/all_to_all | solution.py:392
  154.7 12.9 %all_gather.7 = bf16[256,1792]{1,0:T(8,128)(2,1)S(1)} all-gather(bf16[64,1792]{1,0:T(8,128)(2,1)S(1)} %bitcast.12), channel_id=1, replica_groups=mesh['y'=8,'x'=4,'c'=2,'z'=8] {'x'}, dimensions={0}, use_global_device_ids=true | all-gather | bytes 1146880 | tf_op jit(solution)/shard_map/all_gather | solution.py:394
  167.5 0.0 all-to-all-done.8
  167.5 0.1 reshape.50.squares_ref
  167.6 4.2 %collective-permute-start.2 = (bf16[2,128,1792]{2,1,0:T(8,128)(2,1)S(1)}, bf16[2,128,1792]{2,1,0:T(8,128)(2,1)S(1)}, u32[]{:S(2)}, u32[]{:S(2)}) collective-permute-start(bf16[2,128,1792]{2,1,0:T(8,128)(2,1)S(1)} %bitcast.8), channel_id=1, source_target_pairs={{0,8},{8,0},{1,9},{9,1},{2,10},{10,2},{3,11},{11,3},{4,12},{12,4},... | collective-permute-start | bytes 2752520 | tf_op jit(solution)/shard_map/ppermute | solution.py:22
  171.8 0.9 prepare.1
  172.7 1.2 collective-permute-done.2.other_ref
  173.9 1.7 finish.1
  (7 shorter events, 0.1 us)
Async XLA Ops:
  0.6 10.5 %copy-start = (bf16[4,3584]{1,0:T(4,128)(2,1)S(1)}, bf16[4,3584]{1,0:T(4,128)(2,1)}, u32[]{:S(2)}) copy-start(bf16[4,3584]{1,0:T(4,128)(2,1)} %param.5) | copy-start | bytes 86020
  2.3 23.0 %collective-permute-start = (bf16[128,3584]{1,0:T(8,128)(2,1)S(1)}, bf16[128,3584]{1,0:T(8,128)(2,1)S(1)}, u32[]{:S(2)}, u32[]{:S(2)}) collective-permute-start(bf16[128,3584]{1,0:T(8,128)(2,1)S(1)} %add_convert_fusion.blended_ref), channel_id=1, source_target_pairs={{0,8},{8,0},{1,9},{9,1},{2,10},{10,2},{3,11},{11,3},{4,12},{12,4},... | collective-permute-start | bytes 2752520 | tf_op jit(solution)/shard_map/ppermute | solution.py:22
  61.7 6.9 %collective-permute-start.1 = (f32[128,256]{1,0:T(8,128)S(1)}, f32[128,256]{1,0:T(8,128)S(1)}, u32[]{:S(2)}, u32[]{:S(2)}) collective-permute-start(f32[128,256]{1,0:T(8,128)S(1)} %convert_reduce_fusion.own_ref), channel_id=1, source_target_pairs={{0,8},{8,0},{1,9},{9,1},{2,10},{10,2},{3,11},{11,3},{4,12},{12,4},... | collective-permute-start | bytes 393224 | tf_op jit(solution)/shard_map/ppermute | solution.py:22
  146.1 21.4 %all-to-all-start.8 = ((f32[64,1,64]{2,1,0:T(1,128)}), f32[64,1,64]{2,1,0:T(1,128)S(1)}, u32[]{:S(2)}, u32[]{:S(2)}) async-start(f32[64,1,64]{2,1,0:T(1,128)} %squares.1), calls=%async_computation.8 | async-start | bytes 65536 | tf_op jit(solution)/shard_map/all_to_all | solution.py:392
  167.6 6.2 %collective-permute-start.2 = (bf16[2,128,1792]{2,1,0:T(8,128)(2,1)S(1)}, bf16[2,128,1792]{2,1,0:T(8,128)(2,1)S(1)}, u32[]{:S(2)}, u32[]{:S(2)}) collective-permute-start(bf16[2,128,1792]{2,1,0:T(8,128)(2,1)S(1)} %bitcast.8), channel_id=1, source_target_pairs={{0,8},{8,0},{1,9},{9,1},{2,10},{10,2},{3,11},{11,3},{4,12},{12,4},... | collective-permute-start | bytes 2752520 | tf_op jit(solution)/shard_map/ppermute | solution.py:22

commit v7 on v6

--- a/solution.py
+++ b/solution.py
@@ -45,17 +45,20 @@
     )(*args)
 
 
-def power_kernel(q_ref, blended_ref, other_ref, spread_ref):
+def power_kernel(core_ref, q_ref, blended_ref, other_ref, spread_ref):
     contract_last = (((1,), (1,)), ((), ()))
-    power = [
+    own, other = (
         lax.dot_general(
             q_ref[...], rows[...], contract_last, preferred_element_type=jnp.float32
-        ).astype(jnp.bfloat16)
+        )
         for rows in (blended_ref, other_ref)
-    ]
-    power = jnp.concatenate(power, axis=1)
+    )
+    first = core_ref[0] == 0
+    power = [jnp.where(first, own, other), jnp.where(first, other, own)]
+    power = [p.astype(jnp.bfloat16) for p in power]
     for z in range(NZ):
-        spread_ref[z] = power
+        for c in range(NC):
+            spread_ref[z * NC + c] = power[c]
 
 
 def squares_kernel(project_ref, spread_ref):
@@ -66,7 +69,7 @@
 
 
 def gram_sum(pieces):
-    part = scatter_sum(pieces, "x")
+    part = scatter_sum(pieces, ("x", "c"))
     part = jnp.sum(gather(part, "y", NY), axis=0)
     return gather(part, ("c", "x"), NX * NC).reshape(-1, part.shape[-1])
 
@@ -143,7 +146,15 @@
 
 
 def orthonormal_kernel(
-    core_ref, gram_ref, power_ref, blended_ref, other_ref, basis_ref, terms_ref, work_ref
+    core_ref,
+    gram_ref,
+    power_ref,
+    other_power_ref,
+    blended_ref,
+    other_ref,
+    basis_ref,
+    terms_ref,
+    work_ref,
 ):
     last = work_ref.shape[1] // LANES
     half, core = LANES // 2, LANES * 3 // 2
@@ -151,7 +162,8 @@
     work_ref[:half, LANES:RANK] = gram_ref[LANES:core]
     work_ref[half:LANES, LANES:RANK] = gram_ref[core + LANES :]
     work_ref[LANES:, LANES:RANK] = gram_ref[core : core + LANES]
-    work_ref[:, RANK:] = power_ref[...]
+    work_ref[:, RANK : RANK + LANES] = power_ref[...]
+    work_ref[:, RANK + LANES :] = other_power_ref[...]
     for base in range(0, RANK, PANEL):
         first = base // LANES
         tiles = {
@@ -186,12 +198,12 @@
         terms_ref[j // 2, :, j % 2 * width : (j % 2 + 1) * width] = terms.astype(jnp.bfloat16)
 
 
-def orthonormal(core, gram, power_t, blended, other):
+def orthonormal(core, gram, power_t, other_power_t, blended, other):
     rows, cols = blended.shape
     vmem = pl.BlockSpec(memory_space=pltpu.VMEM)
     return pl.pallas_call(
         orthonormal_kernel,
-        in_specs=[pl.BlockSpec(memory_space=pltpu.SMEM), vmem, vmem, vmem, vmem],
+        in_specs=[pl.BlockSpec(memory_space=pltpu.SMEM)] + [vmem] * 5,
         out_specs=[vmem, vmem],
         out_shape=[
             jax.ShapeDtypeStruct((RANK, NC * rows), jnp.bfloat16),
@@ -201,10 +213,10 @@
         compiler_params=pltpu.CompilerParams(vmem_limit_bytes=24 * 2**20),
         cost_estimate=pl.CostEstimate(flops=10**9, bytes_accessed=10**6, transcendentals=0),
         name="orthonormal",
-    )(core.reshape(1), gram, power_t, blended, other)
-
-
-def own_first(core, rank_dev):
+    )(core.reshape(1), gram, power_t, other_power_t, blended, other)
+
+
+def rank_order(rank_dev):
     def low(value, size):
         return value & (size - 1), value >> (size.bit_length() - 1)
 
@@ -213,53 +225,47 @@
     i, to = low(to, rank_dev)
     y, to = low(to, NY)
     x, c = low(to, NX)
-    c = (c + core) & (NC - 1)
     return (((y * NX + x) * NC + c) * rank_dev + i == source).astype(jnp.float32)
 
 
-def gram_kernel(core_ref, own_ref, other_ref, power_ref, gram_ref):
-    half = own_ref.shape[1] // 2
-    other = jnp.concatenate([other_ref[:, half:], other_ref[:, :half]], axis=1)
+def gram_kernel(terms_ref, power_ref, gram_ref):
     exact = {"precision": lax.Precision.HIGHEST, "preferred_element_type": jnp.float32}
+    halves = [
+        total([terms_ref[z * NC + c].astype(jnp.float32) for z in range(NZ)]) for c in range(NC)
+    ]
     power = lax.dot_general(
-        own_first(core_ref[0], RANK // (NY * NX * NC)),
-        jnp.concatenate([own_ref[...], other], axis=0),
+        rank_order(RANK // (NY * NX * NC)),
+        jnp.concatenate(halves, axis=0),
         (((0,), (0,)), ((), ())),
         **exact,
     )
     power_ref[...] = power
-    first = core_ref[0] == 0
+    contract_last = (((1,), (1,)), ((), ()))
     upper, lower = power[:LANES], power[LANES:]
-    own = jnp.where(first, upper, lower)
-    cross = jnp.where(first, upper[: LANES // 2], upper[LANES // 2 :])
-    contract_last = (((1,), (1,)), ((), ()))
-    gram = jnp.concatenate(
-        [
-            lax.dot_general(own, own, contract_last, **exact),
-            lax.dot_general(cross, lower, contract_last, **exact),
-        ],
-        axis=0,
-    )
+    top = lax.dot_general(upper, power, contract_last, **exact)
+    corner = lax.dot_general(lower, lower, contract_last, **exact)
+    cross = top[:, LANES:]
+    half = LANES // 2
+    gram = jnp.concatenate([top[:, :LANES], cross[:half], corner, cross[half:]], axis=0)
     height = gram_ref.shape[1]
     for x in range(NX):
-        gram_ref[x] = gram[x * height : (x + 1) * height]
-
-
-def gram_pieces(core, own, other):
-    rows = own.shape[1]
-    vmem = pl.BlockSpec(memory_space=pltpu.VMEM)
-    return pl.pallas_call(
+        for c in range(NC):
+            piece = c * NX + x
+            gram_ref[x * NC + c] = gram[piece * height : (piece + 1) * height]
+
+
+def gram_pieces(terms):
+    rows = terms.shape[2]
+    return in_vmem(
         gram_kernel,
-        in_specs=[pl.BlockSpec(memory_space=pltpu.SMEM), vmem, vmem],
-        out_specs=[vmem, vmem],
-        out_shape=[
-            jax.ShapeDtypeStruct((RANK, rows), jnp.float32),
-            jax.ShapeDtypeStruct((NX, 3 * LANES // (NX * NC), LANES), jnp.float32),
+        "gram_pieces",
+        10**9,
+        [
+            ((RANK, rows), jnp.float32),
+            ((NX * NC, 3 * LANES // (NX * NC), LANES), jnp.float32),
         ],
-        compiler_params=pltpu.CompilerParams(vmem_limit_bytes=16 * 2**20),
-        cost_estimate=pl.CostEstimate(flops=10**9, bytes_accessed=10**6, transcendentals=0),
-        name="gram_pieces",
-    )(core.reshape(1), own, other)
+        terms,
+    )
 
 
 def prepare_kernel(core_ref, place_ref, squares_ref, basis_ref, own_ref, left_ref, q_ref):
@@ -356,26 +362,27 @@
     core, x, y = lax.axis_index("c"), lax.axis_index("x"), lax.axis_index("y")
     rank_dev, cols = q_basis.shape
     half = RANK // NC
+    core, gradient, momentum = lax.optimization_barrier((core, gradient, momentum))
     blended = (momentum.astype(jnp.float32) + gradient.astype(jnp.float32)).astype(jnp.bfloat16)
 
     q_own = gather(q_basis, "y", NY).reshape(-1, cols)
     q_own, other = lax.optimization_barrier((q_own, swap_cores(blended)))
     q_own = lax.all_gather(q_own, "x", axis=0, tiled=True)
-    rows = NC * blended.shape[0]
+    rows = blended.shape[0]
     (spread,) = in_vmem(
         power_kernel,
         "power",
-        2 * half * rows * cols,
-        [((NZ, half, rows), jnp.bfloat16)],
+        4 * half * rows * cols,
+        [((NZ * NC, half, rows), jnp.bfloat16)],
+        core.reshape(1),
         q_own,
         blended,
         other,
-    )
-    power_own = jnp.sum(
-        lax.all_to_all(spread, "z", 0, 0, tiled=True).astype(jnp.float32), axis=0
-    )
-    power_t, pieces = gram_pieces(core, power_own, swap_cores(power_own))
-    basis_t, terms = orthonormal(core, gram_sum(pieces), power_t, blended, other)
+        scalars=1,
+    )
+    power_t, pieces = gram_pieces(lax.all_to_all(spread, ("z", "c"), 0, 0, tiled=True))
+    gram = gram_sum(pieces)
+    basis_t, terms = orthonormal(core, gram, power_t, swap_cores(power_t), blended, other)
 
     terms = terms.reshape(NX, NY * SUB, cols // 2)
     project = scatter_sum(terms, "x").astype(jnp.bfloat16).reshape(NY, SUB, cols // 2)

time: 176 us -> 179 us (1.017)
  blocking collectives: 130 us -> 127 us
  waiting for transfers between devices: 2.14 us -> 5.07 us
  starting transfers between devices: 27.4 us -> 29.6 us
    all_to_all x4 -> x3, blocking collectives: 47.9 us -> 36.6 us  [gather(): return lax.all_to_all(spread, axis, 0, 0, tiled=True)]
    all_to_all x0 -> x1, starting transfers between devices: none -> 6.12 us  [gather(): return lax.all_to_all(spread, axis, 0, 0, tiled=True)]
    all_to_all x1, blocking collectives: 24.3 us -> 29.6 us  [body(): lax.all_to_all(spread, ('z', 'c'), 0, 0, tiled=True)]
    ppermute x3, starting transfers between devices: 18.9 us -> 14.9 us  [swap_cores(): return lax.ppermute(value, 'c', [(0, 1), (1, 0)])]
    all_to_all x3, blocking collectives: 33.6 us -> 36.8 us  [scatter_sum(): lax.all_to_all(value, axis, 0, 0, tiled=True).astype(jnp.float32)]
    all_to_all x0 -> x1, waiting for transfers between devices: none -> 2.66 us  [gather(): return lax.all_to_all(spread, axis, 0, 0, tiled=True)]
    pallas_call x4 -> x5, Pallas kernels: 4 us -> 5.2 us  [in_vmem(): pl.pallas_call(kernel, in_specs=[smem] * scalars + [vmem] * (len(args) -...]
  transfers between devices with their start and end apart: 4 -> 5, of which waited for: 2 -> 3; matrix products, arithmetic and copies ran while one was open for 0% -> 0% of each run, Pallas kernels for 1% -> 0%
where the time goes in v7:
time: 179 us
  blocking collectives  127 us (71%)
  starting transfers between devices  29.6 us (17%)
  Pallas kernels  13.1 us (7%)
  waiting for transfers between devices  5.07 us (3%)
  other arithmetic  1.92 us (1%)
    all_to_all x3, blocking collectives, scatter_sum(): lax.all_to_all(value, axis, 0, 0, tiled=True).astype(jnp.float32)  36.8 us
    all_to_all x3, blocking collectives, gather(): return lax.all_to_all(spread, axis, 0, 0, tiled=True)  36.6 us
    all_to_all x1, blocking collectives, body(): lax.all_to_all(spread, ('z', 'c'), 0, 0, tiled=True)  29.6 us
    ppermute x3, starting transfers between devices, swap_cores(): return lax.ppermute(value, 'c', [(0, 1), (1, 0)])  14.9 us
    all_gather x1, blocking collectives, body(): project = lax.all_gather(project, 'x', axis=0, tiled=True)  12.9 us
    all_gather x1, blocking collectives, body(): q_own = lax.all_gather(q_own, 'x', axis=0, tiled=True)  11.3 us
    all_to_all x1, starting transfers between devices, body(): squares = lax.all_to_all(spread, ('c', 'x', 'z'), 0, 0, tiled=True)  8.52 us
    pallas_call x1, Pallas kernels, orthonormal(): pl.pallas_call(orthonormal_kernel, in_specs=[pl.BlockSpec(memory_space=pl...  7.87 us
  transfers between devices with their start and end apart: 5, of which 3 were waited for; matrix products, arithmetic and copies ran while one was open for 0% of the time, Pallas kernels for 0%

profile of v7, /device:TPU:1, one launch (start us, length us, event | category | flops | bytes accessed | tf_op | source)
XLA Modules:
  0.0 178.6 jit_solution(16662127743816032772)
XLA Ops:
  0.6 0.0 copy-start
  0.6 1.7 add_convert_fusion.blended_ref
  2.3 8.8 %collective-permute-start = (bf16[128,3584]{1,0:T(8,128)(2,1)S(1)}, bf16[128,3584]{1,0:T(8,128)(2,1)S(1)}, u32[]{:S(2)}, u32[]{:S(2)}) collective-permute-start(bf16[128,3584]{1,0:T(8,128)(2,1)S(1)} %add_convert_fusion.blended_ref), channel_id=1, source_target_pairs={{0,8},{8,0},{1,9},{9,1},{2,10},{10,2},{3,11},{11,3},{4,12},{12,4},... | collective-permute-start | bytes 2752520 | tf_op jit(solution)/shard_map/ppermute | solution.py:22
  11.1 0.0 copy-done
  11.1 0.1 broadcast_in_dim.8
  11.2 14.1 %all_to_all.45 = bf16[8,4,3584]{2,1,0:T(4,128)(2,1)S(1)} all-to-all(bf16[8,4,3584]{2,1,0:T(4,128)(2,1)S(1)} %broadcast_in_dim.8), channel_id=1, replica_groups=mesh['y'=8,'x'=4,'c'=2,'z'=8] {'y'}, dimensions={0} | all-to-all | bytes 458752 | tf_op jit(solution)/shard_map/all_to_all | solution.py:27
  25.3 0.1 reshape.44
  25.3 0.0 collective-permute-done.other_ref
  25.4 11.3 %all_gather.6.q_ref = bf16[128,3584]{1,0:T(8,128)(2,1)S(1)} all-gather(bf16[32,3584]{1,0:T(8,128)(2,1)S(1)} %reshape.44), channel_id=1, replica_groups=mesh['y'=8,'x'=4,'c'=2,'z'=8] {'x'}, dimensions={0}, use_global_device_ids=true | all-gather | bytes 1146880 | tf_op jit(solution)/shard_map/all_gather | solution.py:370
  36.7 0.7 power.1
  37.4 29.6 %all_to_all.46.terms_ref = bf16[16,128,128]{2,1,0:T(8,128)(2,1)S(1)} all-to-all(bf16[16,128,128]{2,1,0:T(8,128)(2,1)S(1)} %power.1), channel_id=1, replica_groups=mesh['y'=8,'x'=4,'c'=2,'z'=8] {'z','c'}, dimensions={0} | all-to-all | bytes 1048576 | tf_op jit(solution)/shard_map/all_to_all | solution.py:383
  66.9 1.2 gram_pieces.1
  68.1 10.4 %all_to_all.47 = f32[8,48,128]{2,1,0:T(8,128)S(1)} all-to-all(f32[8,48,128]{2,1,0:T(8,128)S(1)} %get-tuple-element.23), channel_id=1, replica_groups=mesh['y'=8,'x'=4,'c'=2,'z'=8] {'x','c'}, dimensions={0} | all-to-all | bytes 393216 | tf_op jit(solution)/shard_map/all_to_all | solution.py:31
  78.6 11.0 %all_to_all.48 = f32[8,48,128]{2,1,0:T(8,128)S(1)} all-to-all(f32[8,48,128]{2,1,0:T(8,128)S(1)} %broadcast_in_dim.9), channel_id=1, replica_groups=mesh['y'=8,'x'=4,'c'=2,'z'=8] {'y'}, dimensions={0} | all-to-all | bytes 393216 | tf_op jit(solution)/shard_map/all_to_all | solution.py:27
  89.6 0.7 broadcast_in_dim.10
  90.3 6.1 %all-to-all-start.4 = ((f32[8,48,128]{2,1,0:T(8,128)}), f32[8,48,128]{2,1,0:T(8,128)S(1)}, u32[]{:S(2)}, u32[]{:S(2)}) async-start(f32[8,48,128]{2,1,0:T(8,128)} %broadcast_in_dim.10), calls=%async_computation.4 | async-start | bytes 393216 | tf_op jit(solution)/shard_map/all_to_all | solution.py:27
  96.4 2.0 %collective-permute-start.1 = (f32[256,128]{1,0:T(8,128)S(1)}, f32[256,128]{1,0:T(8,128)S(1)}, u32[]{:S(2)}, u32[]{:S(2)}) collective-permute-start(f32[256,128]{1,0:T(8,128)S(1)} %get-tuple-element.24.power_ref), channel_id=1, source_target_pairs={{0,8},{8,0},{1,9},{9,1},{2,10},{10,2},{3,11},{11,3},{4,12},{12,4},... | collective-permute-start | bytes 393224 | tf_op jit(solution)/shard_map/ppermute | solution.py:22
  98.4 1.2 collective-permute-done.1.other_power_ref
  99.7 2.7 %all-to-all-done.4 = f32[8,48,128]{2,1,0:T(8,128)S(1)} async-done(((f32[8,48,128]{2,1,0:T(8,128)}), f32[8,48,128]{2,1,0:T(8,128)S(1)}, u32[]{:S(2)}, u32[]{:S(2)}) %all-to-all-start.4) | async-done | bytes 196640 | tf_op jit(solution)/shard_map/all_to_all | solution.py:27
  102.3 7.9 %orthonormal.1 = (bf16[256,256]{1,0:T(8,128)(2,1)S(1)}, bf16[2,128,1792]{2,1,0:T(8,128)(2,1)S(1)}) custom-call(s32[1]{0:T(128)} %bitcast.core_ref, f32[384,128]{1,0:T(8,128)S(1)} %bitcast.14, f32[256,128]{1,0:T(8,128)S(1)} %get-tuple-element.24.power_ref, f32[256,128]{1,0:T(8,128)S(1)} %collective-permute-done.1.other_power_ref, ...), custom_call_target="tpu_custom_call" | custom-call | flops 1000000000 | bytes 1000000 | tf_op jit(solution)/shard_map/orthonormal/pallas_call | solution.py:204
  110.2 15.1 %all_to_all.49 = bf16[4,64,1792]{2,1,0:T(8,128)(2,1)S(1)} all-to-all(bf16[4,64,1792]{2,1,0:T(8,128)(2,1)S(1)} %bitcast.13), channel_id=1, replica_groups=mesh['y'=8,'x'=4,'c'=2,'z'=8] {'x'}, dimensions={0} | all-to-all | bytes 1835008 | tf_op jit(solution)/shard_map/all_to_all | solution.py:31
  125.3 0.2 reduce_sum.53
  125.5 11.3 %all_to_all.50 = bf16[8,8,1792]{2,1,0:T(8,128)(2,1)S(1)} all-to-all(bf16[8,8,1792]{2,1,0:T(8,128)(2,1)S(1)} %bitcast.15), channel_id=1, replica_groups=mesh['y'=8,'x'=4,'c'=2,'z'=8] {'y'}, dimensions={0} | all-to-all | bytes 458752 | tf_op jit(solution)/shard_map/all_to_all | solution.py:31
  136.9 11.5 %all_to_all.51 = bf16[8,8,1792]{2,1,0:T(8,128)(2,1)S(1)} all-to-all(bf16[8,8,1792]{2,1,0:T(8,128)(2,1)S(1)} %broadcast_in_dim.11), channel_id=1, replica_groups=mesh['y'=8,'x'=4,'c'=2,'z'=8] {'y'}, dimensions={0} | all-to-all | bytes 458752 | tf_op jit(solution)/shard_map/all_to_all | solution.py:27
  148.4 0.8 squares.1
  149.2 8.5 %all-to-all-start.8 = ((f32[64,1,64]{2,1,0:T(1,128)}), f32[64,1,64]{2,1,0:T(1,128)S(1)}, u32[]{:S(2)}, u32[]{:S(2)}) async-start(f32[64,1,64]{2,1,0:T(1,128)} %squares.1), calls=%async_computation.8 | async-start | bytes 65536 | tf_op jit(solution)/shard_map/all_to_all | solution.py:399
  157.7 12.9 %all_gather.7 = bf16[256,1792]{1,0:T(8,128)(2,1)S(1)} all-gather(bf16[64,1792]{1,0:T(8,128)(2,1)S(1)} %bitcast.12), channel_id=1, replica_groups=mesh['y'=8,'x'=4,'c'=2,'z'=8] {'x'}, dimensions={0}, use_global_device_ids=true | all-gather | bytes 1146880 | tf_op jit(solution)/shard_map/all_gather | solution.py:401
  170.6 0.0 all-to-all-done.8
  170.6 0.1 reshape.50.squares_ref
  170.7 4.2 %collective-permute-start.2 = (bf16[2,128,1792]{2,1,0:T(8,128)(2,1)S(1)}, bf16[2,128,1792]{2,1,0:T(8,128)(2,1)S(1)}, u32[]{:S(2)}, u32[]{:S(2)}) collective-permute-start(bf16[2,128,1792]{2,1,0:T(8,128)(2,1)S(1)} %bitcast.8), channel_id=1, source_target_pairs={{0,8},{8,0},{1,9},{9,1},{2,10},{10,2},{3,11},{11,3},{4,12},{12,4},... | collective-permute-start | bytes 2752520 | tf_op jit(solution)/shard_map/ppermute | solution.py:22
  174.9 0.9 prepare.1
  175.8 1.2 collective-permute-done.2.other_ref
  176.9 1.7 finish.1
  (6 shorter events, 0.1 us)
Async XLA Ops:
  0.6 10.5 %copy-start = (bf16[4,3584]{1,0:T(4,128)(2,1)S(1)}, bf16[4,3584]{1,0:T(4,128)(2,1)}, u32[]{:S(2)}) copy-start(bf16[4,3584]{1,0:T(4,128)(2,1)} %param.5) | copy-start | bytes 86020
  2.3 23.0 %collective-permute-start = (bf16[128,3584]{1,0:T(8,128)(2,1)S(1)}, bf16[128,3584]{1,0:T(8,128)(2,1)S(1)}, u32[]{:S(2)}, u32[]{:S(2)}) collective-permute-start(bf16[128,3584]{1,0:T(8,128)(2,1)S(1)} %add_convert_fusion.blended_ref), channel_id=1, source_target_pairs={{0,8},{8,0},{1,9},{9,1},{2,10},{10,2},{3,11},{11,3},{4,12},{12,4},... | collective-permute-start | bytes 2752520 | tf_op jit(solution)/shard_map/ppermute | solution.py:22
  90.3 12.0 %all-to-all-start.4 = ((f32[8,48,128]{2,1,0:T(8,128)}), f32[8,48,128]{2,1,0:T(8,128)S(1)}, u32[]{:S(2)}, u32[]{:S(2)}) async-start(f32[8,48,128]{2,1,0:T(8,128)} %broadcast_in_dim.10), calls=%async_computation.4 | async-start | bytes 393216 | tf_op jit(solution)/shard_map/all_to_all | solution.py:27
  96.4 3.2 %collective-permute-start.1 = (f32[256,128]{1,0:T(8,128)S(1)}, f32[256,128]{1,0:T(8,128)S(1)}, u32[]{:S(2)}, u32[]{:S(2)}) collective-permute-start(f32[256,128]{1,0:T(8,128)S(1)} %get-tuple-element.24.power_ref), channel_id=1, source_target_pairs={{0,8},{8,0},{1,9},{9,1},{2,10},{10,2},{3,11},{11,3},{4,12},{12,4},... | collective-permute-start | bytes 393224 | tf_op jit(solution)/shard_map/ppermute | solution.py:22
  149.2 21.4 %all-to-all-start.8 = ((f32[64,1,64]{2,1,0:T(1,128)}), f32[64,1,64]{2,1,0:T(1,128)S(1)}, u32[]{:S(2)}, u32[]{:S(2)}) async-start(f32[64,1,64]{2,1,0:T(1,128)} %squares.1), calls=%async_computation.8 | async-start | bytes 65536 | tf_op jit(solution)/shard_map/all_to_all | solution.py:399
  170.7 6.2 %collective-permute-start.2 = (bf16[2,128,1792]{2,1,0:T(8,128)(2,1)S(1)}, bf16[2,128,1792]{2,1,0:T(8,128)(2,1)S(1)}, u32[]{:S(2)}, u32[]{:S(2)}) collective-permute-start(bf16[2,128,1792]{2,1,0:T(8,128)(2,1)S(1)} %bitcast.8), channel_id=1, source_target_pairs={{0,8},{8,0},{1,9},{9,1},{2,10},{10,2},{3,11},{11,3},{4,12},{12,4},... | collective-permute-start | bytes 2752520 | tf_op jit(solution)/shard_map/ppermute | solution.py:22

commit v8 on v6

--- a/solution.py
+++ b/solution.py
@@ -262,8 +262,10 @@
     )(core.reshape(1), own, other)
 
 
-def prepare_kernel(core_ref, place_ref, squares_ref, basis_ref, own_ref, left_ref, q_ref):
-    rows = left_ref.shape[0] // 2
+def prepare_kernel(
+    core_ref, place_ref, squares_ref, basis_ref, own_ref, blended_ref, left_ref, part_ref, q_ref
+):
+    rows = blended_ref.shape[0]
     half = RANK // NC
     inverse = 1.0 / jnp.sqrt(squares_ref[...] + 1e-06)
     turned = jnp.concatenate([inverse[:, half:], inverse[:, :half]], axis=1)
@@ -271,8 +273,8 @@
     basis = jnp.dot(
         own_ranks(core_ref[0], RANK), basis_ref[:, :rows], preferred_element_type=jnp.float32
     ).T
-    left_ref[:rows] = basis.astype(jnp.bfloat16)
-    left_ref[rows:] = (basis * inverse).astype(jnp.bfloat16)
+    left = jnp.concatenate([basis, basis * inverse], axis=0).astype(jnp.bfloat16)
+    left_ref[...] = left[:, half:]
     rank = lax.broadcasted_iota(jnp.int32, (SUB, half), 1)
     chosen = rank == place_ref[0] + lax.broadcasted_iota(jnp.int32, (SUB, half), 0)
     scale = jnp.sum(jnp.where(chosen, inverse[:, :half], 0.0), axis=1, keepdims=True)
@@ -282,20 +284,23 @@
         picked = jnp.dot(chosen, own_ref[side], preferred_element_type=jnp.float32) * scale
         columns = slice(side * width, (side + 1) * width)
         q_ref[:, columns] = picked[: q_ref.shape[0]].astype(jnp.bfloat16)
+        both = jnp.dot(left[:, :half], own_ref[side], preferred_element_type=jnp.float32)
+        blended = blended_ref[:, columns].astype(jnp.float32)
+        part_ref[:rows, columns] = blended - (1.0 - MU_KEEP) * both[:rows]
+        part_ref[rows:, columns] = math.sqrt(D * FF / RANK) * both[rows:]
 
 
 def finish_kernel(
     left_ref,
-    own_ref,
+    part_ref,
     other_ref,
-    blended_ref,
     momentum_hbm,
     update_hbm,
     momentum_ref,
     update_ref,
     sems,
 ):
-    rows, cols = blended_ref.shape
+    rows, cols = momentum_ref.shape
     blocks = sems.shape[1]
     width = cols // blocks
     copies = []
@@ -303,13 +308,11 @@
         columns = slice(j * width, (j + 1) * width)
         side, k = divmod(j, blocks // 2)
         there = slice(k * width, (k + 1) * width)
-        project = [ref[side, :, there] for ref in (own_ref, other_ref)]
-        project = jnp.concatenate(project, axis=0)
-        both = jnp.dot(left_ref[...], project, preferred_element_type=jnp.float32)
-        blended = blended_ref[:, columns].astype(jnp.float32)
-        momentum = blended - (1.0 - MU_KEEP) * both[:rows]
+        both = jnp.dot(left_ref[...], other_ref[side, :, there], preferred_element_type=jnp.float32)
+        momentum = part_ref[:rows, columns] - (1.0 - MU_KEEP) * both[:rows]
         momentum_ref[:, columns] = momentum.astype(jnp.bfloat16)
-        update_ref[:, columns] = (math.sqrt(D * FF / RANK) * both[rows:]).astype(jnp.bfloat16)
+        update = part_ref[rows:, columns] + math.sqrt(D * FF / RANK) * both[rows:]
+        update_ref[:, columns] = update.astype(jnp.bfloat16)
         for n, (source, target) in enumerate(
             ((momentum_ref, momentum_hbm), (update_ref, update_hbm))
         ):
@@ -325,16 +328,21 @@
 def finish(core, place, squares, basis_t, own, other, blended, rank_dev):
     rows, cols = blended.shape
     whole = ((rows, cols), jnp.bfloat16)
-    left, q_next = in_vmem(
+    left, part, q_next = in_vmem(
         prepare_kernel,
         "prepare",
         10**5,
-        [((2 * rows, RANK), jnp.bfloat16), ((rank_dev, cols), jnp.bfloat16)],
+        [
+            ((2 * rows, RANK // NC), jnp.bfloat16),
+            ((2 * rows, cols), jnp.float32),
+            ((rank_dev, cols), jnp.bfloat16),
+        ],
         core.reshape(1),
         place.reshape(1),
         squares,
         basis_t,
         own,
+        blended,
         scalars=2,
     )
     momentum_next, update = in_vmem(
@@ -343,9 +351,8 @@
         4 * rows * RANK * cols,
         [whole, whole],
         left,
-        own,
+        part,
         other,
-        blended,
         scratch=[pltpu.VMEM(*whole), pltpu.VMEM(*whole), pltpu.SemaphoreType.DMA((2, BLOCKS))],
         hbm_outs=2,
     )

time: 176 us -> 176 us (level)
  no operation moved by 1% of the time
where the time goes in v8:
time: 176 us
  blocking collectives  130 us (74%)
  starting transfers between devices  27.4 us (16%)
  Pallas kernels  13.4 us (8%)
  other arithmetic  1.98 us (1%)
  waiting for transfers between devices  1.79 us (1%)
    all_to_all x4, blocking collectives, gather(): return lax.all_to_all(spread, axis, 0, 0, tiled=True)  47.9 us
    all_to_all x3, blocking collectives, scatter_sum(): lax.all_to_all(value, axis, 0, 0, tiled=True).astype(jnp.float32)  33.6 us
    all_to_all x1, blocking collectives, body(): lax.all_to_all(spread, 'z', 0, 0, tiled=True).astype(jnp.float32)  24.3 us
    ppermute x3, starting transfers between devices, swap_cores(): return lax.ppermute(value, 'c', [(0, 1), (1, 0)])  18.9 us
    all_gather x1, blocking collectives, body(): project = lax.all_gather(project, 'x', axis=0, tiled=True)  12.9 us
    all_gather x1, blocking collectives, body(): q_own = lax.all_gather(q_own, 'x', axis=0, tiled=True)  11.3 us
    all_to_all x1, starting transfers between devices, body(): squares = lax.all_to_all(spread, ('c', 'x', 'z'), 0, 0, tiled=True)  8.51 us
    pallas_call x1, Pallas kernels, orthonormal(): pl.pallas_call(orthonormal_kernel, in_specs=[pl.BlockSpec(memory_space=pl...  7.88 us
  transfers between devices with their start and end apart: 4, of which 2 were waited for; matrix products, arithmetic and copies ran while one was open for 0% of the time, Pallas kernels for 1%

profile of v8, /device:TPU:1, one launch (start us, length us, event | category | flops | bytes accessed | tf_op | source)
XLA Modules:
  0.0 175.5 jit_solution(4364289241771405481)
XLA Ops:
  0.6 0.0 copy-start
  0.6 1.7 add_convert_fusion.blended_ref
  2.3 8.8 %collective-permute-start = (bf16[128,3584]{1,0:T(8,128)(2,1)S(1)}, bf16[128,3584]{1,0:T(8,128)(2,1)S(1)}, u32[]{:S(2)}, u32[]{:S(2)}) collective-permute-start(bf16[128,3584]{1,0:T(8,128)(2,1)S(1)} %add_convert_fusion.blended_ref), channel_id=1, source_target_pairs={{0,8},{8,0},{1,9},{9,1},{2,10},{10,2},{3,11},{11,3},{4,12},{12,4},... | collective-permute-start | bytes 2752520 | tf_op jit(solution)/shard_map/ppermute | solution.py:22
  11.1 0.0 copy-done
  11.1 0.1 broadcast_in_dim.8
  11.2 14.1 %all_to_all.45 = bf16[8,4,3584]{2,1,0:T(4,128)(2,1)S(1)} all-to-all(bf16[8,4,3584]{2,1,0:T(4,128)(2,1)S(1)} %broadcast_in_dim.8), channel_id=1, replica_groups=mesh['y'=8,'x'=4,'c'=2,'z'=8] {'y'}, dimensions={0} | all-to-all | bytes 458752 | tf_op jit(solution)/shard_map/all_to_all | solution.py:27
  25.3 0.1 reshape.44
  25.3 0.0 collective-permute-done.other_ref
  25.4 11.3 %all_gather.6.q_ref = bf16[128,3584]{1,0:T(8,128)(2,1)S(1)} all-gather(bf16[32,3584]{1,0:T(8,128)(2,1)S(1)} %reshape.44), channel_id=1, replica_groups=mesh['y'=8,'x'=4,'c'=2,'z'=8] {'x'}, dimensions={0}, use_global_device_ids=true | all-gather | bytes 1146880 | tf_op jit(solution)/shard_map/all_gather | solution.py:370
  36.7 0.6 power.1
  37.3 24.3 %all_to_all.46 = bf16[8,128,256]{2,1,0:T(8,128)(2,1)S(1)} all-to-all(bf16[8,128,256]{2,1,0:T(8,128)(2,1)S(1)} %power.1), channel_id=1, replica_groups=mesh['y'=8,'x'=4,'c'=2,'z'=8] {'z'}, dimensions={0} | all-to-all | bytes 1048576 | tf_op jit(solution)/shard_map/all_to_all | solution.py:382
  61.6 0.1 convert_reduce_fusion.own_ref
  61.7 5.9 %collective-permute-start.1 = (f32[128,256]{1,0:T(8,128)S(1)}, f32[128,256]{1,0:T(8,128)S(1)}, u32[]{:S(2)}, u32[]{:S(2)}) collective-permute-start(f32[128,256]{1,0:T(8,128)S(1)} %convert_reduce_fusion.own_ref), channel_id=1, source_target_pairs={{0,8},{8,0},{1,9},{9,1},{2,10},{10,2},{3,11},{11,3},{4,12},{12,4},... | collective-permute-start | bytes 393224 | tf_op jit(solution)/shard_map/ppermute | solution.py:22
  67.6 1.0 collective-permute-done.1.other_ref
  68.6 1.2 gram_pieces.1
  69.7 7.2 %all_to_all.47 = f32[4,48,128]{2,1,0:T(8,128)S(1)} all-to-all(f32[4,48,128]{2,1,0:T(8,128)S(1)} %get-tuple-element.18), channel_id=1, replica_groups=mesh['y'=8,'x'=4,'c'=2,'z'=8] {'x'}, dimensions={0} | all-to-all | bytes 196608 | tf_op jit(solution)/shard_map/all_to_all | solution.py:31
  77.0 11.1 %all_to_all.48 = f32[8,48,128]{2,1,0:T(8,128)S(1)} all-to-all(f32[8,48,128]{2,1,0:T(8,128)S(1)} %broadcast_in_dim.9), channel_id=1, replica_groups=mesh['y'=8,'x'=4,'c'=2,'z'=8] {'y'}, dimensions={0} | all-to-all | bytes 393216 | tf_op jit(solution)/shard_map/all_to_all | solution.py:27
  88.1 11.1 %all_to_all.49 = f32[8,48,128]{2,1,0:T(8,128)S(1)} all-to-all(f32[8,48,128]{2,1,0:T(8,128)S(1)} %broadcast_in_dim.10), channel_id=1, replica_groups=mesh['y'=8,'x'=4,'c'=2,'z'=8] {'c','x'}, dimensions={0} | all-to-all | bytes 393216 | tf_op jit(solution)/shard_map/all_to_all | solution.py:27
  99.3 7.9 %orthonormal.1 = (bf16[256,256]{1,0:T(8,128)(2,1)S(1)}, bf16[2,128,1792]{2,1,0:T(8,128)(2,1)S(1)}) custom-call(s32[1]{0:T(128)} %bitcast.core_ref, f32[384,128]{1,0:T(8,128)S(1)} %bitcast.13, f32[256,256]{1,0:T(8,128)S(1)} %get-tuple-element.19.power_ref, bf16[128,3584]{1,0:T(8,128)(2,1)S(1)} %add_convert_fusion.blended_ref, ...), custom_call_target="tpu_custom_call" | custom-call | flops 1000000000 | bytes 1000000 | tf_op jit(solution)/shard_map/orthonormal/pallas_call | solution.py:192
  107.1 15.1 %all_to_all.50 = bf16[4,64,1792]{2,1,0:T(8,128)(2,1)S(1)} all-to-all(bf16[4,64,1792]{2,1,0:T(8,128)(2,1)S(1)} %bitcast.12), channel_id=1, replica_groups=mesh['y'=8,'x'=4,'c'=2,'z'=8] {'x'}, dimensions={0} | all-to-all | bytes 1835008 | tf_op jit(solution)/shard_map/all_to_all | solution.py:31
  122.3 0.2 reduce_sum.63
  122.4 11.3 %all_to_all.51 = bf16[8,8,1792]{2,1,0:T(8,128)(2,1)S(1)} all-to-all(bf16[8,8,1792]{2,1,0:T(8,128)(2,1)S(1)} %bitcast.14), channel_id=1, replica_groups=mesh['y'=8,'x'=4,'c'=2,'z'=8] {'y'}, dimensions={0} | all-to-all | bytes 458752 | tf_op jit(solution)/shard_map/all_to_all | solution.py:31
  133.8 11.5 %all_to_all.52 = bf16[8,8,1792]{2,1,0:T(8,128)(2,1)S(1)} all-to-all(bf16[8,8,1792]{2,1,0:T(8,128)(2,1)S(1)} %broadcast_in_dim.11), channel_id=1, replica_groups=mesh['y'=8,'x'=4,'c'=2,'z'=8] {'y'}, dimensions={0} | all-to-all | bytes 458752 | tf_op jit(solution)/shard_map/all_to_all | solution.py:27
  145.3 0.8 squares.1
  146.1 8.5 %all-to-all-start.8 = ((f32[64,1,64]{2,1,0:T(1,128)}), f32[64,1,64]{2,1,0:T(1,128)S(1)}, u32[]{:S(2)}, u32[]{:S(2)}) async-start(f32[64,1,64]{2,1,0:T(1,128)} %squares.1), calls=%async_computation.8 | async-start | bytes 65536 | tf_op jit(solution)/shard_map/all_to_all | solution.py:399
  154.7 12.9 %all_gather.7 = bf16[256,1792]{1,0:T(8,128)(2,1)S(1)} all-gather(bf16[64,1792]{1,0:T(8,128)(2,1)S(1)} %bitcast.11), channel_id=1, replica_groups=mesh['y'=8,'x'=4,'c'=2,'z'=8] {'x'}, dimensions={0}, use_global_device_ids=true | all-gather | bytes 1146880 | tf_op jit(solution)/shard_map/all_gather | solution.py:401
  167.5 0.0 all-to-all-done.8
  167.5 0.1 reshape.50.squares_ref
  167.6 4.2 %collective-permute-start.2 = (bf16[2,128,1792]{2,1,0:T(8,128)(2,1)S(1)}, bf16[2,128,1792]{2,1,0:T(8,128)(2,1)S(1)}, u32[]{:S(2)}, u32[]{:S(2)}) collective-permute-start(bf16[2,128,1792]{2,1,0:T(8,128)(2,1)S(1)} %bitcast.8), channel_id=1, source_target_pairs={{0,8},{8,0},{1,9},{9,1},{2,10},{10,2},{3,11},{11,3},{4,12},{12,4},... | collective-permute-start | bytes 2752520 | tf_op jit(solution)/shard_map/ppermute | solution.py:22
  171.8 1.2 prepare.1
  173.0 0.8 collective-permute-done.2.other_ref
  173.9 1.6 finish.1
  (7 shorter events, 0.1 us)
Async XLA Ops:
  0.6 10.5 %copy-start = (bf16[4,3584]{1,0:T(4,128)(2,1)S(1)}, bf16[4,3584]{1,0:T(4,128)(2,1)}, u32[]{:S(2)}) copy-start(bf16[4,3584]{1,0:T(4,128)(2,1)} %param.5) | copy-start | bytes 86020
  2.3 23.0 %collective-permute-start = (bf16[128,3584]{1,0:T(8,128)(2,1)S(1)}, bf16[128,3584]{1,0:T(8,128)(2,1)S(1)}, u32[]{:S(2)}, u32[]{:S(2)}) collective-permute-start(bf16[128,3584]{1,0:T(8,128)(2,1)S(1)} %add_convert_fusion.blended_ref), channel_id=1, source_target_pairs={{0,8},{8,0},{1,9},{9,1},{2,10},{10,2},{3,11},{11,3},{4,12},{12,4},... | collective-permute-start | bytes 2752520 | tf_op jit(solution)/shard_map/ppermute | solution.py:22
  61.7 6.9 %collective-permute-start.1 = (f32[128,256]{1,0:T(8,128)S(1)}, f32[128,256]{1,0:T(8,128)S(1)}, u32[]{:S(2)}, u32[]{:S(2)}) collective-permute-start(f32[128,256]{1,0:T(8,128)S(1)} %convert_reduce_fusion.own_ref), channel_id=1, source_target_pairs={{0,8},{8,0},{1,9},{9,1},{2,10},{10,2},{3,11},{11,3},{4,12},{12,4},... | collective-permute-start | bytes 393224 | tf_op jit(solution)/shard_map/ppermute | solution.py:22
  146.1 21.4 %all-to-all-start.8 = ((f32[64,1,64]{2,1,0:T(1,128)}), f32[64,1,64]{2,1,0:T(1,128)S(1)}, u32[]{:S(2)}, u32[]{:S(2)}) async-start(f32[64,1,64]{2,1,0:T(1,128)} %squares.1), calls=%async_computation.8 | async-start | bytes 65536 | tf_op jit(solution)/shard_map/all_to_all | solution.py:399
  167.6 6.2 %collective-permute-start.2 = (bf16[2,128,1792]{2,1,0:T(8,128)(2,1)S(1)}, bf16[2,128,1792]{2,1,0:T(8,128)(2,1)S(1)}, u32[]{:S(2)}, u32[]{:S(2)}) collective-permute-start(bf16[2,128,1792]{2,1,0:T(8,128)(2,1)S(1)} %bitcast.8), channel_id=1, source_target_pairs={{0,8},{8,0},{1,9},{9,1},{2,10},{10,2},{3,11},{11,3},{4,12},{12,4},... | collective-permute-start | bytes 2752520 | tf_op jit(solution)/shard_map/ppermute | solution.py:22

commit v9 on v8

--- a/solution.py
+++ b/solution.py
@@ -74,7 +74,7 @@
 SUB, LANES = 8, 128
 PANEL = 64
 STEP = 16
-BLOCKS = 14
+BLOCKS = 4
 
 
 def across(value, lane):

time: 176 us -> 176 us (level)
  no operation moved by 1% of the time
where the time goes in v9:
time: 176 us; the launch traced here: 175 us
  blocking collectives  130 us (74%)
  starting transfers between devices  27.4 us (16%)
  Pallas kernels  13.3 us (8%)
  other arithmetic  1.98 us (1%)
  waiting for transfers between devices  1.79 us (1%)
    all_to_all x4, blocking collectives, gather(): return lax.all_to_all(spread, axis, 0, 0, tiled=True)  47.9 us
    all_to_all x3, blocking collectives, scatter_sum(): lax.all_to_all(value, axis, 0, 0, tiled=True).astype(jnp.float32)  33.6 us
    all_to_all x1, blocking collectives, body(): lax.all_to_all(spread, 'z', 0, 0, tiled=True).astype(jnp.float32)  24.3 us
    ppermute x3, starting transfers between devices, swap_cores(): return lax.ppermute(value, 'c', [(0, 1), (1, 0)])  18.9 us
    all_gather x1, blocking collectives, body(): project = lax.all_gather(project, 'x', axis=0, tiled=True)  12.9 us
    all_gather x1, blocking collectives, body(): q_own = lax.all_gather(q_own, 'x', axis=0, tiled=True)  11.3 us
    all_to_all x1, starting transfers between devices, body(): squares = lax.all_to_all(spread, ('c', 'x', 'z'), 0, 0, tiled=True)  8.51 us
    pallas_call x1, Pallas kernels, orthonormal(): pl.pallas_call(orthonormal_kernel, in_specs=[pl.BlockSpec(memory_space=pl...  7.88 us
  transfers between devices with their start and end apart: 4, of which 2 were waited for; matrix products, arithmetic and copies ran while one was open for 0% of the time, Pallas kernels for 1%

profile of v9, /device:TPU:1, one launch (start us, length us, event | category | flops | bytes accessed | tf_op | source)
XLA Modules:
  0.0 175.4 jit_solution(3037391083872168511)
XLA Ops:
  0.6 0.0 copy-start
  0.6 1.7 add_convert_fusion.blended_ref
  2.3 8.8 %collective-permute-start = (bf16[128,3584]{1,0:T(8,128)(2,1)S(1)}, bf16[128,3584]{1,0:T(8,128)(2,1)S(1)}, u32[]{:S(2)}, u32[]{:S(2)}) collective-permute-start(bf16[128,3584]{1,0:T(8,128)(2,1)S(1)} %add_convert_fusion.blended_ref), channel_id=1, source_target_pairs={{0,8},{8,0},{1,9},{9,1},{2,10},{10,2},{3,11},{11,3},{4,12},{12,4},... | collective-permute-start | bytes 2752520 | tf_op jit(solution)/shard_map/ppermute | solution.py:22
  11.1 0.0 copy-done
  11.1 0.1 broadcast_in_dim.8
  11.2 14.1 %all_to_all.45 = bf16[8,4,3584]{2,1,0:T(4,128)(2,1)S(1)} all-to-all(bf16[8,4,3584]{2,1,0:T(4,128)(2,1)S(1)} %broadcast_in_dim.8), channel_id=1, replica_groups=mesh['y'=8,'x'=4,'c'=2,'z'=8] {'y'}, dimensions={0} | all-to-all | bytes 458752 | tf_op jit(solution)/shard_map/all_to_all | solution.py:27
  25.3 0.1 reshape.44
  25.3 0.0 collective-permute-done.other_ref
  25.4 11.3 %all_gather.6.q_ref = bf16[128,3584]{1,0:T(8,128)(2,1)S(1)} all-gather(bf16[32,3584]{1,0:T(8,128)(2,1)S(1)} %reshape.44), channel_id=1, replica_groups=mesh['y'=8,'x'=4,'c'=2,'z'=8] {'x'}, dimensions={0}, use_global_device_ids=true | all-gather | bytes 1146880 | tf_op jit(solution)/shard_map/all_gather | solution.py:370
  36.7 0.6 power.1
  37.3 24.3 %all_to_all.46 = bf16[8,128,256]{2,1,0:T(8,128)(2,1)S(1)} all-to-all(bf16[8,128,256]{2,1,0:T(8,128)(2,1)S(1)} %power.1), channel_id=1, replica_groups=mesh['y'=8,'x'=4,'c'=2,'z'=8] {'z'}, dimensions={0} | all-to-all | bytes 1048576 | tf_op jit(solution)/shard_map/all_to_all | solution.py:382
  61.6 0.1 convert_reduce_fusion.own_ref
  61.7 5.9 %collective-permute-start.1 = (f32[128,256]{1,0:T(8,128)S(1)}, f32[128,256]{1,0:T(8,128)S(1)}, u32[]{:S(2)}, u32[]{:S(2)}) collective-permute-start(f32[128,256]{1,0:T(8,128)S(1)} %convert_reduce_fusion.own_ref), channel_id=1, source_target_pairs={{0,8},{8,0},{1,9},{9,1},{2,10},{10,2},{3,11},{11,3},{4,12},{12,4},... | collective-permute-start | bytes 393224 | tf_op jit(solution)/shard_map/ppermute | solution.py:22
  67.6 1.0 collective-permute-done.1.other_ref
  68.6 1.2 gram_pieces.1
  69.7 7.2 %all_to_all.47 = f32[4,48,128]{2,1,0:T(8,128)S(1)} all-to-all(f32[4,48,128]{2,1,0:T(8,128)S(1)} %get-tuple-element.18), channel_id=1, replica_groups=mesh['y'=8,'x'=4,'c'=2,'z'=8] {'x'}, dimensions={0} | all-to-all | bytes 196608 | tf_op jit(solution)/shard_map/all_to_all | solution.py:31
  77.0 11.1 %all_to_all.48 = f32[8,48,128]{2,1,0:T(8,128)S(1)} all-to-all(f32[8,48,128]{2,1,0:T(8,128)S(1)} %broadcast_in_dim.9), channel_id=1, replica_groups=mesh['y'=8,'x'=4,'c'=2,'z'=8] {'y'}, dimensions={0} | all-to-all | bytes 393216 | tf_op jit(solution)/shard_map/all_to_all | solution.py:27
  88.1 11.1 %all_to_all.49 = f32[8,48,128]{2,1,0:T(8,128)S(1)} all-to-all(f32[8,48,128]{2,1,0:T(8,128)S(1)} %broadcast_in_dim.10), channel_id=1, replica_groups=mesh['y'=8,'x'=4,'c'=2,'z'=8] {'c','x'}, dimensions={0} | all-to-all | bytes 393216 | tf_op jit(solution)/shard_map/all_to_all | solution.py:27
  99.3 7.9 %orthonormal.1 = (bf16[256,256]{1,0:T(8,128)(2,1)S(1)}, bf16[2,128,1792]{2,1,0:T(8,128)(2,1)S(1)}) custom-call(s32[1]{0:T(128)} %bitcast.core_ref, f32[384,128]{1,0:T(8,128)S(1)} %bitcast.13, f32[256,256]{1,0:T(8,128)S(1)} %get-tuple-element.19.power_ref, bf16[128,3584]{1,0:T(8,128)(2,1)S(1)} %add_convert_fusion.blended_ref, ...), custom_call_target="tpu_custom_call" | custom-call | flops 1000000000 | bytes 1000000 | tf_op jit(solution)/shard_map/orthonormal/pallas_call | solution.py:192
  107.1 15.1 %all_to_all.50 = bf16[4,64,1792]{2,1,0:T(8,128)(2,1)S(1)} all-to-all(bf16[4,64,1792]{2,1,0:T(8,128)(2,1)S(1)} %bitcast.12), channel_id=1, replica_groups=mesh['y'=8,'x'=4,'c'=2,'z'=8] {'x'}, dimensions={0} | all-to-all | bytes 1835008 | tf_op jit(solution)/shard_map/all_to_all | solution.py:31
  122.3 0.2 reduce_sum.63
  122.4 11.3 %all_to_all.51 = bf16[8,8,1792]{2,1,0:T(8,128)(2,1)S(1)} all-to-all(bf16[8,8,1792]{2,1,0:T(8,128)(2,1)S(1)} %bitcast.14), channel_id=1, replica_groups=mesh['y'=8,'x'=4,'c'=2,'z'=8] {'y'}, dimensions={0} | all-to-all | bytes 458752 | tf_op jit(solution)/shard_map/all_to_all | solution.py:31
  133.8 11.5 %all_to_all.52 = bf16[8,8,1792]{2,1,0:T(8,128)(2,1)S(1)} all-to-all(bf16[8,8,1792]{2,1,0:T(8,128)(2,1)S(1)} %broadcast_in_dim.11), channel_id=1, replica_groups=mesh['y'=8,'x'=4,'c'=2,'z'=8] {'y'}, dimensions={0} | all-to-all | bytes 458752 | tf_op jit(solution)/shard_map/all_to_all | solution.py:27
  145.3 0.8 squares.1
  146.1 8.5 %all-to-all-start.8 = ((f32[64,1,64]{2,1,0:T(1,128)}), f32[64,1,64]{2,1,0:T(1,128)S(1)}, u32[]{:S(2)}, u32[]{:S(2)}) async-start(f32[64,1,64]{2,1,0:T(1,128)} %squares.1), calls=%async_computation.8 | async-start | bytes 65536 | tf_op jit(solution)/shard_map/all_to_all | solution.py:399
  154.7 12.9 %all_gather.7 = bf16[256,1792]{1,0:T(8,128)(2,1)S(1)} all-gather(bf16[64,1792]{1,0:T(8,128)(2,1)S(1)} %bitcast.11), channel_id=1, replica_groups=mesh['y'=8,'x'=4,'c'=2,'z'=8] {'x'}, dimensions={0}, use_global_device_ids=true | all-gather | bytes 1146880 | tf_op jit(solution)/shard_map/all_gather | solution.py:401
  167.5 0.0 all-to-all-done.8
  167.5 0.1 reshape.50.squares_ref
  167.6 4.2 %collective-permute-start.2 = (bf16[2,128,1792]{2,1,0:T(8,128)(2,1)S(1)}, bf16[2,128,1792]{2,1,0:T(8,128)(2,1)S(1)}, u32[]{:S(2)}, u32[]{:S(2)}) collective-permute-start(bf16[2,128,1792]{2,1,0:T(8,128)(2,1)S(1)} %bitcast.8), channel_id=1, source_target_pairs={{0,8},{8,0},{1,9},{9,1},{2,10},{10,2},{3,11},{11,3},{4,12},{12,4},... | collective-permute-start | bytes 2752520 | tf_op jit(solution)/shard_map/ppermute | solution.py:22
  171.8 1.2 prepare.1
  173.0 0.8 collective-permute-done.2.other_ref
  173.9 1.5 finish.1
  (7 shorter events, 0.1 us)
Async XLA Ops:
  0.6 10.5 %copy-start = (bf16[4,3584]{1,0:T(4,128)(2,1)S(1)}, bf16[4,3584]{1,0:T(4,128)(2,1)}, u32[]{:S(2)}) copy-start(bf16[4,3584]{1,0:T(4,128)(2,1)} %param.5) | copy-start | bytes 86020
  2.3 23.0 %collective-permute-start = (bf16[128,3584]{1,0:T(8,128)(2,1)S(1)}, bf16[128,3584]{1,0:T(8,128)(2,1)S(1)}, u32[]{:S(2)}, u32[]{:S(2)}) collective-permute-start(bf16[128,3584]{1,0:T(8,128)(2,1)S(1)} %add_convert_fusion.blended_ref), channel_id=1, source_target_pairs={{0,8},{8,0},{1,9},{9,1},{2,10},{10,2},{3,11},{11,3},{4,12},{12,4},... | collective-permute-start | bytes 2752520 | tf_op jit(solution)/shard_map/ppermute | solution.py:22
  61.7 6.9 %collective-permute-start.1 = (f32[128,256]{1,0:T(8,128)S(1)}, f32[128,256]{1,0:T(8,128)S(1)}, u32[]{:S(2)}, u32[]{:S(2)}) collective-permute-start(f32[128,256]{1,0:T(8,128)S(1)} %convert_reduce_fusion.own_ref), channel_id=1, source_target_pairs={{0,8},{8,0},{1,9},{9,1},{2,10},{10,2},{3,11},{11,3},{4,12},{12,4},... | collective-permute-start | bytes 393224 | tf_op jit(solution)/shard_map/ppermute | solution.py:22
  146.1 21.4 %all-to-all-start.8 = ((f32[64,1,64]{2,1,0:T(1,128)}), f32[64,1,64]{2,1,0:T(1,128)S(1)}, u32[]{:S(2)}, u32[]{:S(2)}) async-start(f32[64,1,64]{2,1,0:T(1,128)} %squares.1), calls=%async_computation.8 | async-start | bytes 65536 | tf_op jit(solution)/shard_map/all_to_all | solution.py:399
  167.6 6.2 %collective-permute-start.2 = (bf16[2,128,1792]{2,1,0:T(8,128)(2,1)S(1)}, bf16[2,128,1792]{2,1,0:T(8,128)(2,1)S(1)}, u32[]{:S(2)}, u32[]{:S(2)}) collective-permute-start(bf16[2,128,1792]{2,1,0:T(8,128)(2,1)S(1)} %bitcast.8), channel_id=1, source_target_pairs={{0,8},{8,0},{1,9},{9,1},{2,10},{10,2},{3,11},{11,3},{4,12},{12,4},... | collective-permute-start | bytes 2752520 | tf_op jit(solution)/shard_map/ppermute | solution.py:22
